TPU v7x, 32 devices: a whole 2x2x4 slice. The times are simulated.
32 devices in a mesh: fsdp: 4 (over z), ctx: 2 (over core), tp: 4 (over y, x).
Axes of the slice: x: 2, y: 2, z: 4, core: 2. Of those that a mesh axis runs over, the one named last changes fastest.
Arguments:
- latents: bfloat16 [32, 4, 32, 32], P(('fsdp', 'ctx')), may hold values from -5 to 5
- noise_sample: bfloat16 [32, 4, 32, 32], P(('fsdp', 'ctx')), may hold values from -5 to 5
- timesteps: int32 [32], P(('fsdp', 'ctx')), may hold values from 0 to 999
- class_labels: int32 [32], P(('fsdp', 'ctx')), may hold values from 0 to 999
- w_block: float32 [1024, 13, 1024], P(('fsdp', 'ctx'), None, 'tp'), may hold values from -0.1875 to 0.1875
- w_output: float32 [5, 1024, 1024], P(None, 'tp', ('fsdp', 'ctx')), may hold values from -0.375 to 0.375
- w_top: float32 [1024, 3072], P(('fsdp', 'ctx'), 'tp'), may hold values from -0.1875 to 0.1875
- w_head: float32 [1024, 16], P(('fsdp', 'ctx')), may hold values from -0.1875 to 0.1875
- w_embed: float32 [1272, 1024], P('tp', ('fsdp', 'ctx')), may hold values from -1 to 1
- biases: float32 [19, 1024], replicated, may hold values from -0.6 to 0.6
- m_block: float32 [1024, 13, 1024], P(('fsdp', 'ctx'), None, 'tp'), may hold values from -0.000113846974 to 0.000113846974
- m_output: float32 [5, 1024, 1024], P(None, 'tp', ('fsdp', 'ctx')), may hold values from -0.000113846974 to 0.000113846974
- m_top: float32 [1024, 3072], P(('fsdp', 'ctx'), 'tp'), may hold values from -0.000113846974 to 0.000113846974
- m_head: float32 [1024, 16], P(('fsdp', 'ctx')), may hold values from -0.004296875 to 0.004296875
- m_embed: float32 [1272, 1024], P('tp', ('fsdp', 'ctx')), may hold values from -0.000113846974 to 0.000113846974
- m_biases: float32 [19, 1024], replicated, may hold values from -0.0004553879 to 0.0004553879
- v_block: float32 [1024, 13, 1024], P(('fsdp', 'ctx'), None, 'tp'), may hold values from 2.1423361e-11 to 1.7138689e-10
- v_output: float32 [5, 1024, 1024], P(None, 'tp', ('fsdp', 'ctx')), may hold values from 2.1423361e-11 to 1.7138689e-10
- v_top: float32 [1024, 3072], P(('fsdp', 'ctx'), 'tp'), may hold values from 2.1423361e-11 to 1.7138689e-10
- v_head: float32 [1024, 16], P(('fsdp', 'ctx')), may hold values from 3.051758e-08 to 2.4414064e-07
- v_embed: float32 [1272, 1024], P('tp', ('fsdp', 'ctx')), may hold values from 2.1423361e-11 to 1.7138689e-10
- v_biases: float32 [19, 1024], replicated, may hold values from 3.4277378e-10 to 2.7421903e-09
Outputs:
- loss: float32 [], replicated
- grad_norm: float32 [], replicated
- new_block: float32 [1024, 13, 1024], P(('fsdp', 'ctx'), None, 'tp')
- new_output: float32 [5, 1024, 1024], P(None, 'tp', ('fsdp', 'ctx'))
- new_top: float32 [1024, 3072], P(('fsdp', 'ctx'), 'tp')
- new_head: float32 [1024, 16], P(('fsdp', 'ctx'))
- new_embed: float32 [1272, 1024], P('tp', ('fsdp', 'ctx'))
- new_biases: float32 [19, 1024], replicated
- first_block: float32 [1024, 13, 1024], P(('fsdp', 'ctx'), None, 'tp')
- first_output: float32 [5, 1024, 1024], P(None, 'tp', ('fsdp', 'ctx'))
- first_top: float32 [1024, 3072], P(('fsdp', 'ctx'), 'tp')
- first_head: float32 [1024, 16], P(('fsdp', 'ctx'))
- first_embed: float32 [1272, 1024], P('tp', ('fsdp', 'ctx'))
- first_biases: float32 [19, 1024], replicated
- second_block: float32 [1024, 13, 1024], P(('fsdp', 'ctx'), None, 'tp')
- second_output: float32 [5, 1024, 1024], P(None, 'tp', ('fsdp', 'ctx'))
- second_top: float32 [1024, 3072], P(('fsdp', 'ctx'), 'tp')
- second_head: float32 [1024, 16], P(('fsdp', 'ctx'))
- second_embed: float32 [1272, 1024], P('tp', ('fsdp', 'ctx'))
- second_biases: float32 [19, 1024], replicated
- clipped_bias_grad: float32 [19, 1024], replicated
All inputs are finite; a program needn't handle non-finite values.
Results may differ from a plain program's by a relative error of at most 0.012.
Values may be sent and summed in bfloat16 or wider, within the bound.
No kernel may reach another device: no remote copies, remote signals or barrier semaphores. Data moves between devices by JAX's collectives and lax.ppermute only.
A program may use at most 192 MiB of HBM per device.

v0:
```python
import math

import jax
import jax.numpy as jnp
from jax import lax
from jax.sharding import PartitionSpec as P

HEAD_DIM = 64
CLASSES = 1000
FREQ = 256
TIMESTEPS = 1000
ADAM_STEP = 10


PRECISE = lax.Precision.HIGHEST


def exact_dot(left, right):
    return jnp.dot(left, right, precision=PRECISE)


def layer_norm(values):
    center = values - jnp.mean(values, axis=-1, keepdims=True)
    spread = jnp.mean(center * center, axis=-1, keepdims=True)
    return center * lax.rsqrt(spread + 1e-06)


def modulate(values, shift, scale):
    return layer_norm(values) * (1.0 + scale[:, None, :]) + shift[:, None, :]


def gelu_tanh(values):
    return jax.nn.gelu(values, approximate=True)


def time_freq(step_ids, width):
    half_width = width // 2
    rates = jnp.exp(-math.log(10000.0) * jnp.arange(half_width, dtype=jnp.float32) / half_width)
    angles = step_ids.astype(jnp.float32)[:, None] * rates[None, :]
    return jnp.concatenate([jnp.cos(angles), jnp.sin(angles)], axis=-1)


def position_table(token_ids, grid_side, width):
    quarter = width // 4
    rates = jnp.exp(-math.log(10000.0) * jnp.arange(quarter, dtype=jnp.float32) / quarter)
    row_angle = (token_ids // grid_side).astype(jnp.float32)[:, None] * rates[None, :]
    col_angle = (token_ids % grid_side).astype(jnp.float32)[:, None] * rates[None, :]
    return jnp.concatenate(
        [jnp.sin(row_angle), jnp.cos(row_angle), jnp.sin(col_angle), jnp.cos(col_angle)], axis=-1
    )


def plan(step_ids):
    fraction = (step_ids.astype(jnp.float32) / TIMESTEPS + 0.008) / 1.008
    kept_share = jnp.cos(fraction * (math.pi / 2.0)) ** 2
    return (jnp.sqrt(kept_share), jnp.sqrt(1.0 - kept_share))


def patchify(field):
    img_count, chan_count, row_count, col_count = field.shape
    shaped = field.reshape(img_count, chan_count, row_count // 2, 2, col_count // 2, 2)
    shaped = shaped.transpose(0, 2, 4, 1, 3, 5)
    return shaped.reshape(img_count, row_count // 2 * (col_count // 2), chan_count * 4)


def adam_update(weight, gradient, first_mom, second_mom, clip_factor):
    clipped = gradient * clip_factor
    first_new = 0.9 * first_mom + 0.1 * clipped
    second_new = 0.999 * second_mom + 0.001 * clipped * clipped
    corr_first = 1.0 - 0.9**ADAM_STEP
    corr_second = 1.0 - 0.999**ADAM_STEP
    direction = first_new / corr_first / (jnp.sqrt(second_new / corr_second) + 1e-08)
    return (weight - 0.04 * (direction + 0.01 * weight), first_new, second_new)


def head_sum(values):
    return lax.psum(values, "tp")


def layer_views(block_full, output_full):
    width = block_full.shape[0]
    local_width = block_full.shape[2]
    w_qkv = block_full[:, 0:3, :].reshape(width, 3 * local_width)
    w_up = block_full[:, 3:7, :].reshape(width, 4 * local_width)
    w_mod = block_full[:, 7:13, :].reshape(width, 6 * local_width)
    w_proj = output_full[0]
    w_down = output_full[1:5].reshape(4 * local_width, width)
    return (w_qkv, w_up, w_mod, w_proj, w_down)


def layer_forward(resid_in, modulation, views, layer_bias):
    w_qkv, w_up, w_mod, w_proj, w_down = views
    bias_qkv, bias_proj, bias_up, bias_down = layer_bias
    img_count, tok_count, width = resid_in.shape
    local_width = w_proj.shape[0]
    head_local = local_width // HEAD_DIM
    attn_in = modulate(resid_in, modulation[:, 0], modulation[:, 1]).astype(jnp.bfloat16)
    qkv_low = (
        jnp.einsum("btd,de->bte", attn_in, w_qkv, preferred_element_type=jnp.float32) + bias_qkv
    ).astype(jnp.bfloat16)
    qkv_low = qkv_low.reshape(img_count, tok_count, 3, head_local, HEAD_DIM)
    queries = qkv_low[:, :, 0]
    keys_all = qkv_low[:, :, 1]
    values_all = qkv_low[:, :, 2]
    scores = (
        jnp.einsum("bqhd,bkhd->bhqk", queries, keys_all, preferred_element_type=jnp.float32) * 0.125
    )
    log_total = jax.nn.logsumexp(scores, axis=-1, keepdims=True)
    probs_low = jnp.exp(scores - log_total).astype(jnp.bfloat16)
    attended = jnp.einsum(
        "bhqk,bkhd->bqhd", probs_low, values_all, preferred_element_type=jnp.float32
    )
    attended = attended.astype(jnp.bfloat16).reshape(img_count, tok_count, local_width)
    attn_out = (
        head_sum(jnp.einsum("btc,cd->btd", attended, w_proj, preferred_element_type=jnp.float32))
        + bias_proj
    )
    resid_mid = resid_in + modulation[:, 2][:, None, :] * attn_out
    mlp_in = modulate(resid_mid, modulation[:, 3], modulation[:, 4]).astype(jnp.bfloat16)
    up_pre = jnp.einsum("btd,df->btf", mlp_in, w_up, preferred_element_type=jnp.float32) + bias_up
    up_act = gelu_tanh(up_pre).astype(jnp.bfloat16)
    mlp_out = (
        head_sum(jnp.einsum("btf,fd->btd", up_act, w_down, preferred_element_type=jnp.float32))
        + bias_down
    )
    resid_out = resid_mid + modulation[:, 5][:, None, :] * mlp_out
    kept = (
        attn_in,
        queries,
        keys_all,
        values_all,
        log_total,
        probs_low,
        attended,
        attn_out,
        resid_mid,
        mlp_in,
        up_pre,
        up_act,
        mlp_out,
    )
    return (resid_out, kept)


def layer_backward(grad_resid, resid_in, modulation, views, kept, owned_low):
    w_qkv, w_up, w_mod, w_proj, w_down = views
    (
        attn_in,
        queries,
        keys_all,
        values_all,
        log_total,
        probs_low,
        attended,
        attn_out,
        resid_mid,
        mlp_in,
        up_pre,
        up_act,
        mlp_out,
    ) = kept
    img_count, tok_count, width = resid_in.shape
    local_width = w_proj.shape[0]
    head_local = local_width // HEAD_DIM
    grad_gate_b = jnp.sum(grad_resid * mlp_out, axis=1)
    grad_mlp = (grad_resid * modulation[:, 5][:, None, :]).astype(jnp.bfloat16)
    grad_b_down = jnp.sum((grad_mlp * owned_low[:, None, None]).astype(jnp.float32), axis=(0, 1))
    grad_w_down = jnp.einsum("btf,btd->fd", up_act, grad_mlp, preferred_element_type=jnp.float32)
    grad_up_act = jnp.einsum("btd,fd->btf", grad_mlp, w_down, preferred_element_type=jnp.float32)
    grad_up = jax.vjp(gelu_tanh, up_pre)[1](grad_up_act)[0].astype(jnp.bfloat16)
    grad_b_up = jnp.sum(grad_up.astype(jnp.float32), axis=(0, 1))
    grad_w_up = jnp.einsum("btd,btf->df", mlp_in, grad_up, preferred_element_type=jnp.float32)
    grad_mlp_in = head_sum(
        jnp.einsum("btf,df->btd", grad_up, w_up, preferred_element_type=jnp.float32)
    )
    grad_norm_b = jax.vjp(modulate, resid_mid, modulation[:, 3], modulation[:, 4])[1](grad_mlp_in)
    grad_resid = grad_resid + grad_norm_b[0]
    grad_gate_a = jnp.sum(grad_resid * attn_out, axis=1)
    grad_attn = (grad_resid * modulation[:, 2][:, None, :]).astype(jnp.bfloat16)
    grad_b_proj = jnp.sum((grad_attn * owned_low[:, None, None]).astype(jnp.float32), axis=(0, 1))
    grad_w_proj = jnp.einsum("btc,btd->cd", attended, grad_attn, preferred_element_type=jnp.float32)
    grad_attended = jnp.einsum("btd,cd->btc", grad_attn, w_proj, preferred_element_type=jnp.float32)
    grad_attended = grad_attended.astype(jnp.bfloat16).reshape(
        img_count, tok_count, head_local, HEAD_DIM
    )
    scores = (
        jnp.einsum("bqhd,bkhd->bhqk", queries, keys_all, preferred_element_type=jnp.float32) * 0.125
    )
    probs = jnp.exp(scores - log_total)
    grad_probs = jnp.einsum(
        "bqhd,bkhd->bhqk", grad_attended, values_all, preferred_element_type=jnp.float32
    )
    grad_scores = (
        probs * (grad_probs - jnp.sum(grad_probs * probs, axis=-1, keepdims=True))
    ).astype(jnp.bfloat16)
    grad_queries = (
        jnp.einsum("bhqk,bkhd->bqhd", grad_scores, keys_all, preferred_element_type=jnp.float32)
        * 0.125
    )
    grad_keys = (
        jnp.einsum("bhqk,bqhd->bkhd", grad_scores, queries, preferred_element_type=jnp.float32)
        * 0.125
    )
    grad_values = jnp.einsum(
        "bhqk,bqhd->bkhd", probs_low, grad_attended, preferred_element_type=jnp.float32
    )
    grad_qkv = jnp.stack([grad_queries, grad_keys, grad_values], axis=2).astype(jnp.bfloat16)
    grad_qkv = grad_qkv.reshape(img_count, tok_count, 3 * local_width)
    grad_b_qkv = jnp.sum(grad_qkv.astype(jnp.float32), axis=(0, 1))
    grad_w_qkv = jnp.einsum("btd,bte->de", attn_in, grad_qkv, preferred_element_type=jnp.float32)
    grad_attn_in = head_sum(
        jnp.einsum("bte,de->btd", grad_qkv, w_qkv, preferred_element_type=jnp.float32)
    )
    grad_norm_a = jax.vjp(modulate, resid_in, modulation[:, 0], modulation[:, 1])[1](grad_attn_in)
    grad_resid_in = grad_resid + grad_norm_a[0]
    grad_modulation = jnp.stack(
        [grad_norm_a[1], grad_norm_a[2], grad_gate_a, grad_norm_b[1], grad_norm_b[2], grad_gate_b],
        axis=1,
    )
    weight_grads = (grad_w_qkv, grad_w_up, grad_w_proj, grad_w_down)
    bias_grads = (grad_b_qkv, grad_b_proj, grad_b_up, grad_b_down)
    return (grad_resid_in, grad_modulation, weight_grads, bias_grads)


def on_device(
    latents,
    noise_sample,
    timesteps,
    class_labels,
    w_block,
    w_output,
    w_top,
    w_head,
    w_embed,
    biases,
    m_block,
    m_output,
    m_top,
    m_head,
    m_embed,
    m_biases,
    v_block,
    v_output,
    v_top,
    v_head,
    v_embed,
    v_biases,
):
    img_count = latents.shape[0]
    tp_count = lax.axis_size("tp")
    tp_rank = lax.axis_index("tp")
    local_width = w_block.shape[2]
    width = local_width * tp_count
    grid_side = latents.shape[3] // 2
    tok_count = latents.shape[2] // 2 * grid_side
    images_all = img_count * lax.axis_size("fsdp") * lax.axis_size("ctx")

    def tp_cols(rows_values):
        return lax.dynamic_slice_in_dim(
            rows_values, tp_rank * local_width, local_width, rows_values.ndim - 1
        )

    def tp_place(rows_values):
        empty_rows = jnp.zeros((rows_values.shape[0], width), jnp.float32)
        return lax.dynamic_update_slice_in_dim(empty_rows, rows_values, tp_rank * local_width, 1)

    layer_low = (w_block.astype(jnp.bfloat16), w_output.astype(jnp.bfloat16))
    block_full, output_full = (
        lax.all_gather(layer_low[0], ("fsdp", "ctx"), axis=0, tiled=True),
        lax.all_gather(layer_low[1], ("fsdp", "ctx"), axis=2, tiled=True),
    )
    embed_part, top_part, head_full = (
        lax.all_gather(w_embed.astype(jnp.bfloat16), ("fsdp", "ctx"), axis=1, tiled=True),
        lax.all_gather(w_top.astype(jnp.bfloat16), ("fsdp", "ctx"), axis=0, tiled=True),
        lax.all_gather(w_head.astype(jnp.bfloat16), ("fsdp", "ctx"), axis=0, tiled=True),
    )
    embed_full, top_full = (
        lax.all_gather(embed_part, "tp", axis=0, tiled=True),
        lax.all_gather(top_part, "tp", axis=1, tiled=True),
    )
    views = layer_views(block_full, output_full)
    layer_bias = (
        jnp.concatenate(
            [tp_cols(biases[9]), jnp.zeros((local_width,), jnp.float32), tp_cols(biases[10])]
        ),
        biases[11],
        tp_cols(biases[12:16]).reshape(4 * local_width),
        biases[16],
    )
    keep_rate, drop_rate = plan(timesteps)
    latent_vals = latents.astype(jnp.float32)
    noise_vals = noise_sample.astype(jnp.float32)
    noisy = (
        keep_rate[:, None, None, None] * latent_vals + drop_rate[:, None, None, None] * noise_vals
    )
    patches = patchify(noisy).astype(jnp.bfloat16)
    target = patchify(noise_vals)
    freq_low = time_freq(timesteps, FREQ).astype(jnp.bfloat16)
    w_t1 = embed_full[:FREQ]
    table = embed_full[FREQ : FREQ + CLASSES]
    w_patch = embed_full[FREQ + CLASSES :]
    w_t2 = top_full[:, :width]
    w_final = top_full[:, width : 3 * width]
    t_pre = jnp.dot(freq_low, w_t1, preferred_element_type=jnp.float32) + biases[1]
    t_hidden = jax.nn.silu(t_pre).astype(jnp.bfloat16)
    one_hot = (class_labels[:, None] == jnp.arange(CLASSES, dtype=jnp.int32)[None, :]).astype(
        jnp.bfloat16
    )
    cond = (
        jnp.dot(t_hidden, w_t2, preferred_element_type=jnp.float32)
        + biases[2]
        + jnp.dot(one_hot, table, preferred_element_type=jnp.float32)
    )
    cond_low = jax.nn.silu(cond).astype(jnp.bfloat16)
    mod_part = (
        jnp.dot(cond_low, views[2], preferred_element_type=jnp.float32).reshape(
            img_count, 6, local_width
        )
        + tp_cols(biases[3:9])[None]
    )
    modulation = lax.all_gather(mod_part, "tp", axis=2, tiled=True)
    final_mod = jnp.dot(cond_low, w_final, preferred_element_type=jnp.float32) + biases[
        17:19
    ].reshape(2 * width)
    shift_f = final_mod[:, :width]
    scale_f = final_mod[:, width:]
    token_ids = jnp.arange(tok_count, dtype=jnp.int32)
    resid_in = (
        jnp.einsum("btc,cd->btd", patches, w_patch, preferred_element_type=jnp.float32)
        + biases[0]
        + position_table(token_ids, grid_side, width)[None]
    )
    resid_out, kept = layer_forward(resid_in, modulation, views, layer_bias)
    head_in = modulate(resid_out, shift_f, scale_f).astype(jnp.bfloat16)
    predicted = jnp.einsum("btd,dc->btc", head_in, head_full, preferred_element_type=jnp.float32)
    error = predicted - target
    owned_img = (jnp.arange(img_count, dtype=jnp.int32) % tp_count == tp_rank).astype(jnp.float32)
    owned_low = owned_img.astype(jnp.bfloat16)
    loss_part = jnp.sum(owned_img[:, None, None] * error * error) / images_all
    grad_pred = (2.0 / images_all * error).astype(jnp.bfloat16)
    grad_head_in = jnp.einsum(
        "btc,dc->btd", grad_pred, head_full, preferred_element_type=jnp.float32
    )
    grad_head = jnp.einsum("btd,btc->dc", head_in, grad_pred, preferred_element_type=jnp.float32)
    grad_final_parts = jax.vjp(modulate, resid_out, shift_f, scale_f)[1](grad_head_in)
    grad_final_all = jnp.concatenate([grad_final_parts[1], grad_final_parts[2]], axis=-1)
    grad_final = grad_final_all * owned_img[:, None]
    block_again, output_again = (
        lax.all_gather(layer_low[0], ("fsdp", "ctx"), axis=0, tiled=True),
        lax.all_gather(layer_low[1], ("fsdp", "ctx"), axis=2, tiled=True),
    )
    views = layer_views(block_again, output_again)
    grad_resid_in, grad_modulation, weight_grads, bias_grads = layer_backward(
        grad_final_parts[0], resid_in, modulation, views, kept, owned_low
    )
    grad_w_qkv, grad_w_up, grad_w_proj, grad_w_down = weight_grads
    grad_b_qkv, grad_b_proj, grad_b_up, grad_b_down = bias_grads
    grad_resid_bf = grad_resid_in.astype(jnp.bfloat16)
    grad_resid_low = grad_resid_bf * owned_low[:, None, None]
    grad_b_patch = jnp.sum(grad_resid_low.astype(jnp.float32), axis=(0, 1))
    grad_mod_local = tp_cols(grad_modulation).reshape(img_count, 6 * local_width)
    cond_low_full = cond_low.astype(jnp.float32)
    grad_w_mod = exact_dot(cond_low_full.T, grad_mod_local)
    mod_back = exact_dot(grad_mod_local, views[2].astype(jnp.float32).T)
    bias_weight = jnp.ones_like(owned_img)
    grad_w_patch = jnp.einsum(
        "btc,btd->cd", patches, grad_resid_low, preferred_element_type=jnp.float32
    )
    grad_w_final = exact_dot(cond_low_full.T, grad_final)
    grad_cond_act = mod_back + exact_dot(grad_final, w_final.astype(jnp.float32).T)
    grad_cond = jax.vjp(jax.nn.silu, cond)[1](grad_cond_act)[0]
    grad_table = exact_dot(one_hot.astype(jnp.float32).T, grad_cond)
    grad_w_t2 = exact_dot(t_hidden.astype(jnp.float32).T, grad_cond)
    grad_t_pre = jax.vjp(jax.nn.silu, t_pre)[1](exact_dot(grad_cond, w_t2.astype(jnp.float32).T))[0]
    grad_w_t1 = exact_dot(freq_low.astype(jnp.float32).T, grad_t_pre)
    grad_block = jnp.concatenate(
        [
            grad_w_qkv.reshape(width, 3, local_width),
            grad_w_up.reshape(width, 4, local_width),
            grad_w_mod.reshape(width, 6, local_width),
        ],
        axis=1,
    )
    grad_output = jnp.concatenate(
        [grad_w_proj[None], grad_w_down.reshape(4, local_width, width)], axis=0
    )
    grad_embed = jnp.concatenate([grad_w_t1, grad_table, grad_w_patch], axis=0)
    grad_top = jnp.concatenate([grad_w_t2, grad_w_final], axis=1)
    grad_bias = jnp.concatenate(
        [
            grad_b_patch[None],
            jnp.sum(grad_t_pre * bias_weight[:, None], axis=0)[None],
            jnp.sum(grad_cond * bias_weight[:, None], axis=0)[None],
            tp_place(jnp.sum(grad_mod_local, axis=0).reshape(6, local_width)),
            tp_place(jnp.stack([grad_b_qkv[:local_width], grad_b_qkv[2 * local_width :]])),
            grad_b_proj[None],
            tp_place(grad_b_up.reshape(4, local_width)),
            grad_b_down[None],
            jnp.sum(grad_final, axis=0).reshape(2, width),
        ],
        axis=0,
    )
    block_sum, output_sum = (
        lax.psum_scatter(grad_block, ("fsdp", "ctx"), scatter_dimension=0, tiled=True),
        lax.psum_scatter(grad_output, ("fsdp", "ctx"), scatter_dimension=2, tiled=True),
    )
    embed_tp, top_tp = (
        lax.psum_scatter(grad_embed, "tp", scatter_dimension=0, tiled=True),
        lax.psum_scatter(grad_top, "tp", scatter_dimension=1, tiled=True),
    )
    embed_sum, top_sum, head_grad_sum = (
        lax.psum_scatter(embed_tp, ("fsdp", "ctx"), scatter_dimension=1, tiled=True),
        lax.psum_scatter(top_tp, ("fsdp", "ctx"), scatter_dimension=0, tiled=True),
        lax.psum_scatter(grad_head, ("fsdp", "ctx"), scatter_dimension=0, tiled=True),
    )
    bias_sum, loss_total = lax.psum((grad_bias, loss_part), ("fsdp", "ctx", "tp"))
    head_squares = jnp.where(tp_rank == 0, jnp.sum(head_grad_sum * head_grad_sum), 0.0)
    shard_squares = (
        jnp.sum(block_sum * block_sum)
        + jnp.sum(output_sum * output_sum)
        + jnp.sum(embed_sum * embed_sum)
        + jnp.sum(top_sum * top_sum)
        + head_squares
    )
    grad_norm = jnp.sqrt(
        lax.psum(shard_squares, ("fsdp", "ctx", "tp")) + jnp.sum(bias_sum * bias_sum)
    )
    clip_factor = jnp.minimum(1.0, 1.0 / (grad_norm + 1e-06))
    upd_block = adam_update(w_block, block_sum, m_block, v_block, clip_factor)
    upd_output = adam_update(w_output, output_sum, m_output, v_output, clip_factor)
    upd_top = adam_update(w_top, top_sum, m_top, v_top, clip_factor)
    upd_head = adam_update(w_head, head_grad_sum, m_head, v_head, clip_factor)
    upd_embed = adam_update(w_embed, embed_sum, m_embed, v_embed, clip_factor)
    upd_biases = adam_update(biases, bias_sum, m_biases, v_biases, clip_factor)
    return (
        loss_total,
        grad_norm,
        upd_block[0],
        upd_output[0],
        upd_top[0],
        upd_head[0],
        upd_embed[0],
        upd_biases[0],
        upd_block[1],
        upd_output[1],
        upd_top[1],
        upd_head[1],
        upd_embed[1],
        upd_biases[1],
        upd_block[2],
        upd_output[2],
        upd_top[2],
        upd_head[2],
        upd_embed[2],
        upd_biases[2],
        bias_sum * clip_factor,
    )


def solution(mesh):
    placed = (
        P(("fsdp", "ctx"), None, None, None),
        P(("fsdp", "ctx"), None, None, None),
        P(("fsdp", "ctx")),
        P(("fsdp", "ctx")),
        P(("fsdp", "ctx"), None, "tp"),
        P(None, "tp", ("fsdp", "ctx")),
        P(("fsdp", "ctx"), "tp"),
        P(("fsdp", "ctx"), None),
        P("tp", ("fsdp", "ctx")),
        P(),
        P(("fsdp", "ctx"), None, "tp"),
        P(None, "tp", ("fsdp", "ctx")),
        P(("fsdp", "ctx"), "tp"),
        P(("fsdp", "ctx"), None),
        P("tp", ("fsdp", "ctx")),
        P(),
        P(("fsdp", "ctx"), None, "tp"),
        P(None, "tp", ("fsdp", "ctx")),
        P(("fsdp", "ctx"), "tp"),
        P(("fsdp", "ctx"), None),
        P("tp", ("fsdp", "ctx")),
        P(),
    )
    return jax.shard_map(
        on_device,
        mesh=mesh,
        in_specs=placed,
        out_specs=(
            P(),
            P(),
            P(("fsdp", "ctx"), None, "tp"),
            P(None, "tp", ("fsdp", "ctx")),
            P(("fsdp", "ctx"), "tp"),
            P(("fsdp", "ctx"), None),
            P("tp", ("fsdp", "ctx")),
            P(),
            P(("fsdp", "ctx"), None, "tp"),
            P(None, "tp", ("fsdp", "ctx")),
            P(("fsdp", "ctx"), "tp"),
            P(("fsdp", "ctx"), None),
            P("tp", ("fsdp", "ctx")),
            P(),
            P(("fsdp", "ctx"), None, "tp"),
            P(None, "tp", ("fsdp", "ctx")),
            P(("fsdp", "ctx"), "tp"),
            P(("fsdp", "ctx"), None),
            P("tp", ("fsdp", "ctx")),
            P(),
            P(),
        ),
        check_vma=False,
    )
```

profile of v0, /device:TPU:0, one launch (start us, length us, event | category | flops | bytes accessed | tf_op | source)
XLA Modules:
  0.0 1441.0 jit_solution(6745464077062834751)
XLA Ops:
  10.1 17.4 %all_gather.26 = bf16[318,1024]{1,0:T(8,128)(2,1)} all-gather(bf16[318,128]{1,0:T(8,128)(2,1)S(1)} %convert_element_type.175), channel_id=1, replica_groups=mesh['fsdp'=4,'ctx'=2,'tp'=4] {'fsdp','ctx'}, dimensions={1}, use_global_device_ids=true | all-gather | bytes 732672 | tf_op jit(solution)/shard_map/all_gather | solution.py:273
  30.1 9.0 all-gather.7.cloned.1.call-done
  46.1 33.6 %all-gather.15.cloned.1.call-done = bf16[4,318,1024]{2,1,0:T(8,128)(2,1)} async-done(((bf16[1,318,1024]{2,1,0:T(8,128)(2,1)}), bf16[4,318,1024]{2,1,0:T(8,128)(2,1)}) %all-gather.15.cloned.1.call-update) | async-done | bytes 2605072 | tf_op jit(solution)/shard_map/all_gather | solution.py:278
  88.9 62.1 %all-gather.11.cloned.1.call-done = bf16[1024,13,256]{2,0,1:T(8,128)(2,1)} async-done(((bf16[128,13,256]{2,0,1:T(8,128)(2,1)}), bf16[1024,13,256]{2,0,1:T(8,128)(2,1)}) %all-gather.11.cloned.1.call-update) | async-done | bytes 6815760 | tf_op jit(solution)/shard_map/all_gather | solution.py:269
  157.9 4.9 copy.139
  162.8 58.7 %all-gather.9.cloned.1.call-done = bf16[1024,3072]{1,0:T(8,128)(2,1)} async-done(((bf16[1024,768]{1,0:T(8,128)(2,1)}), bf16[1024,3072]{1,0:T(8,128)(2,1)}) %all-gather.9.cloned.1.call-update) | async-done | bytes 6291472 | tf_op jit(solution)/shard_map/all_gather | solution.py:279
  226.5 8.9 all_gather.31
  245.0 13.5 all-gather.13.cloned.1.call-done
  271.8 92.9 %all-reduce.9.cloned.1.call-done = f32[4,256,1024]{2,1,0:T(8,128)} async-done(((f32[4,256,1024]{2,1,0:T(8,128)}), f32[4,256,1024]{2,1,0:T(8,128)}) %all-reduce.9.cloned.1.call-update) | async-done | bytes 4194320 | tf_op jit(solution)/shard_map/psum | solution.py:77
  374.3 4.8 fusion.111
  384.2 13.2 all_gather.33
  400.3 82.8 %all-reduce.11.cloned.1.call-done = f32[4,256,1024]{2,1,0:T(8,128)} async-done(((f32[4,256,1024]{2,1,0:T(8,128)}), f32[4,256,1024]{2,1,0:T(8,128)}) %all-reduce.11.cloned.1.call-update) | async-done | bytes 4194320 | tf_op jit(solution)/shard_map/psum | solution.py:77
  498.2 5.7 convert_reduce_fusion.1
  510.3 103.2 %all-reduce.13.cloned.1.call-done = f32[4,256,1024]{2,1,0:T(8,128)} async-done(((f32[4,256,1024]{2,1,0:T(8,128)}), f32[4,256,1024]{2,1,0:T(8,128)}) %all-reduce.13.cloned.1.call-update) | async-done | bytes 4194320 | tf_op jit(solution)/shard_map/psum | solution.py:77
  621.7 4.7 convert_reduce_fusion
  639.7 5.8 fusion.108
  645.5 97.6 %all-reduce.15.cloned.1.call-done = f32[4,256,1024]{2,1,0:T(8,128)} async-done(((f32[4,256,1024]{2,1,0:T(8,128)}), f32[4,256,1024]{2,1,0:T(8,128)}) %all-reduce.15.cloned.1.call-update) | async-done | bytes 4194320 | tf_op jit(solution)/shard_map/psum | solution.py:77
  758.8 6.2 fusion.127
  768.8 10.8 pad_maximum_fusion.1
  792.7 105.5 %fusion = f32[320,1024]{1,0:T(8,128)S(1)} fusion(f32[1272,1024]{1,0:T(8,128)} %pad_maximum_fusion.3), kind=kCustom, calls=%all-reduce-scatter | all-reduce-scatter fusion | flops 1310721 | bytes 6521344
  912.9 6.1 fusion.110
  924.1 6.9 fusion.60
  931.0 5.5 copy.160
  936.5 4.8 fusion.25
  945.0 5.3 pad_maximum_fusion
  952.0 21.9 %reduce-scatter.19.cloned.1.call-done = f32[128,16]{0,1:T(8,128)} async-done(((f32[1024,16]{0,1:T(8,128)}), f32[128,16]{0,1:T(8,128)}) %reduce-scatter.19.cloned.1.call-update) | async-done | bytes 8208 | tf_op jit(solution)/shard_map/reduce_scatter | solution.py:414
  981.1 27.2 %reduce-scatter.13.cloned.1.call-done = f32[318,128]{1,0:T(8,128)} async-done(((f32[318,1024]{1,0:T(8,128)}), f32[318,128]{1,0:T(8,128)}) %reduce-scatter.13.cloned.1.call-update) | async-done | bytes 162832 | tf_op jit(solution)/shard_map/reduce_scatter | solution.py:412
  1009.8 58.8 %reduce-scatter.11.cloned.1.call-done = f32[5,256,128]{2,1,0:T(8,128)} async-done(((f32[5,256,1024]{2,1,0:T(8,128)}), f32[5,256,128]{2,1,0:T(8,128)}) %reduce-scatter.11.cloned.1.call-update) | async-done | bytes 655376 | tf_op jit(solution)/shard_map/reduce_scatter | solution.py:405
  1070.6 137.8 %reduce-scatter.9.cloned.1.call-done = f32[128,13,256]{2,0,1:T(8,128)} async-done(((f32[1024,13,256]{2,0,1:T(8,128)}), f32[128,13,256]{2,0,1:T(8,128)}) %reduce-scatter.9.cloned.1.call-update) | async-done | bytes 1703952 | tf_op jit(solution)/shard_map/reduce_scatter | solution.py:404
  1212.8 36.6 %reduce-scatter.17.cloned.1.call-done = f32[128,768]{1,0:T(8,128)} async-done(((f32[1024,768]{1,0:T(8,128)}), f32[128,768]{1,0:T(8,128)}) %reduce-scatter.17.cloned.1.call-update) | async-done | bytes 393232 | tf_op jit(solution)/shard_map/reduce_scatter | solution.py:413
  1251.8 124.3 %all-reduce.17.cloned.1.call-done = f32[19,1024]{1,0:T(8,128)} async-done(((f32[19,1024]{1,0:T(8,128)}), f32[19,1024]{1,0:T(8,128)}) %all-reduce.17.cloned.1.call-update) | async-done | bytes 77840 | tf_op jit(solution)/shard_map/psum | solution.py:416
  1377.6 41.2 %all-reduce.2 = (f32[]{:T(128)}, f32[]{:T(128)}) all-reduce(f32[]{:T(128)S(6)} %div.213, f32[]{:T(128)S(6)} %add.459), channel_id=1, replica_groups=mesh['fsdp'=4,'ctx'=2,'tp'=4] {'fsdp','ctx','tp'}, use_global_device_ids=true, to_apply=%region_11.12 | all-reduce | flops 2 | bytes 16 | tf_op jit(solution)/shard_map/psum | solution.py:416
  (387 shorter events, 200.5 us)
Async XLA Ops:
  7.2 32.0 %all-gather.7.cloned.1.call-start = ((), (), s32[]{:S(2)}) async-start(), calls=%async_computation.6 | async-start | bytes 1769472 | tf_op jit(solution)/shard_map/all_gather | solution.py:274
  9.0 70.7 %all-gather.15.cloned.1.call-start = ((), (), s32[]{:S(2)}) async-start(), calls=%async_computation.21 | async-start | bytes 3276800 | tf_op jit(solution)/shard_map/all_gather | solution.py:278
  27.5 123.5 %all-gather.11.cloned.1.call-start = ((), (), s32[]{:S(2)}) async-start(), calls=%async_computation.8 | async-start | bytes 7667712 | tf_op jit(solution)/shard_map/all_gather | solution.py:269
  30.1 191.5 %all-gather.9.cloned.1.call-start = ((), (), s32[]{:S(2)}) async-start(), calls=%async_computation.7 | async-start | bytes 7864320 | tf_op jit(solution)/shard_map/all_gather | solution.py:279
  39.2 219.3 %all-gather.13.cloned.1.call-start = ((), (), s32[]{:S(2)}) async-start(), calls=%async_computation.9 | async-start | bytes 2949120 | tf_op jit(solution)/shard_map/all_gather | solution.py:270
  40.0 324.7 %all-reduce.9.cloned.1.call-start = ((), (), s32[]{:S(2)}) async-start(), calls=%async_computation.10 | async-start | bytes 8388608 | tf_op jit(solution)/shard_map/psum | solution.py:77
  40.2 324.5 %copy-start.55 = (f32[1,1024]{1,0:T(1,128)}, f32[1,1024]{1,0:T(1,128)S(1)}, u32[]{:S(2)}) copy-start(f32[1,1024]{1,0:T(1,128)S(1)} %get-tuple-element.75) | copy-start | bytes 12292
  40.3 442.8 %copy-start.57 = (f32[1,1024]{1,0:T(1,128)}, f32[1,1024]{1,0:T(1,128)S(1)}, u32[]{:S(2)}) copy-start(f32[1,1024]{1,0:T(1,128)S(1)} %get-tuple-element.74) | copy-start | bytes 12292
  88.2 147.8 %copy-start.59 = (f32[4,256]{1,0:T(4,128)}, f32[4,256]{1,0:T(4,128)S(1)}, u32[]{:S(2)}) copy-start(f32[4,256]{1,0:T(4,128)S(1)} %fusion.86) | copy-start | bytes 12292
  88.4 133.1 %copy-start.49 = (f32[4,1024]{1,0:T(4,128)}, f32[4,1024]{1,0:T(4,128)S(1)}, u32[]{:S(2)}) copy-start(f32[4,1024]{1,0:T(4,128)S(1)} %convolution_add_fusion) | copy-start | bytes 49156
  262.2 220.8 %all-reduce.11.cloned.1.call-start = ((), (), s32[]{:S(2)}) async-start(), calls=%async_computation.11 | async-start | bytes 8388608 | tf_op jit(solution)/shard_map/psum | solution.py:77
  262.3 110.0 %copy-start.85 = (f32[1,2,4,128]{3,1,2,0:T(2,128)}, f32[1,2,4,128]{3,1,2,0:T(2,128)S(1)}, u32[]{:S(2)}) copy-start(f32[1,2,4,128]{3,1,2,0:T(2,128)S(1)} %copy.183) | copy-start | bytes 12292
  379.1 234.5 %all-reduce.13.cloned.1.call-start = ((), (), s32[]{:S(2)}) async-start(), calls=%async_computation.12 | async-start | bytes 8388608 | tf_op jit(solution)/shard_map/psum | solution.py:77
  495.1 126.4 %copy-start.21 = (bf16[4,256,1024]{2,1,0:T(8,128)(2,1)}, bf16[4,256,1024]{2,1,0:T(8,128)(2,1)S(1)}, u32[]{:S(2)}) copy-start(bf16[4,256,1024]{2,1,0:T(8,128)(2,1)S(1)} %get-tuple-element.66) | copy-start | bytes 6291460
  509.6 233.5 %all-reduce.15.cloned.1.call-start = ((), (), s32[]{:S(2)}) async-start(), calls=%async_computation.13 | async-start | bytes 8388608 | tf_op jit(solution)/shard_map/psum | solution.py:77
  639.1 311.4 %reduce-scatter.15.cloned.1.call-start = ((), (), s32[]{:S(2)}) async-start(), calls=%async_computation.17 | async-start | bytes 15728640 | tf_op jit(solution)/shard_map/reduce_scatter | solution.py:409
  779.7 194.3 %reduce-scatter.19.cloned.1.call-start = ((), (), s32[]{:S(2)}) async-start(), calls=%async_computation.19 | async-start | bytes 73728 | tf_op jit(solution)/shard_map/reduce_scatter | solution.py:414
  898.3 7.6 collective-permute-start
  905.8 102.5 %reduce-scatter.13.cloned.1.call-start = ((), (), s32[]{:S(2)}) async-start(), calls=%async_computation.16 | async-start | bytes 1474560 | tf_op jit(solution)/shard_map/reduce_scatter | solution.py:412
  912.8 155.8 %reduce-scatter.11.cloned.1.call-start = ((), (), s32[]{:S(2)}) async-start(), calls=%async_computation.15 | async-start | bytes 5898240 | tf_op jit(solution)/shard_map/reduce_scatter | solution.py:405
  922.5 285.9 %reduce-scatter.9.cloned.1.call-start = ((), (), s32[]{:S(2)}) async-start(), calls=%async_computation.14 | async-start | bytes 15335424 | tf_op jit(solution)/shard_map/reduce_scatter | solution.py:404
  950.4 469.8 %copy-start.72 = (f32[128,16]{0,1:T(8,128)S(1)}, f32[128,16]{0,1:T(8,128)}, u32[]{:S(2)}) copy-start(f32[128,16]{0,1:T(8,128)} %param.29) | copy-start | bytes 24580
  950.4 471.2 %copy-start.46 = (f32[19,1024]{1,0:T(8,128)S(1)}, f32[19,1024]{1,0:T(8,128)}, u32[]{:S(2)}) copy-start(f32[19,1024]{1,0:T(8,128)} %param.37) | copy-start | bytes 233476
  950.4 471.2 %copy-start.47 = (f32[19,1024]{1,0:T(8,128)S(1)}, f32[19,1024]{1,0:T(8,128)}, u32[]{:S(2)}) copy-start(f32[19,1024]{1,0:T(8,128)} %param.43) | copy-start | bytes 233476
  950.4 472.8 %copy-start.42 = (f32[318,128]{1,0:T(8,128)S(1)}, f32[318,128]{1,0:T(8,128)}, u32[]{:S(2)}) copy-start(f32[318,128]{1,0:T(8,128)} %param.30) | copy-start | bytes 488452
  950.4 299.0 %reduce-scatter.17.cloned.1.call-start = ((), (), s32[]{:S(2)}) async-start(), calls=%async_computation.18 | async-start | bytes 3538944 | tf_op jit(solution)/shard_map/reduce_scatter | solution.py:413
  950.5 474.9 %copy-start.39 = (f32[128,768]{1,0:T(8,128)S(1)}, f32[128,768]{1,0:T(8,128)}, u32[]{:S(2)}) copy-start(f32[128,768]{1,0:T(8,128)} %param.28) | copy-start | bytes 1179652
  951.0 477.1 %copy-start.30 = (f32[5,256,128]{2,1,0:T(8,128)S(1)}, f32[5,256,128]{2,1,0:T(8,128)}, u32[]{:S(2)}) copy-start(f32[5,256,128]{2,1,0:T(8,128)} %param.27) | copy-start | bytes 1966084
  951.0 477.1 %copy-start.40 = (f32[5,256,128]{2,1,0:T(8,128)S(1)}, f32[5,256,128]{2,1,0:T(8,128)}, u32[]{:S(2)}) copy-start(f32[5,256,128]{2,1,0:T(8,128)} %param.33) | copy-start | bytes 1966084
  951.0 477.1 %copy-start.41 = (f32[5,256,128]{2,1,0:T(8,128)S(1)}, f32[5,256,128]{2,1,0:T(8,128)}, u32[]{:S(2)}) copy-start(f32[5,256,128]{2,1,0:T(8,128)} %param.39) | copy-start | bytes 1966084
  951.0 425.0 %all-reduce.17.cloned.1.call-start = ((), (), s32[]{:S(2)}) async-start(), calls=%async_computation.20 | async-start | bytes 196608 | tf_op jit(solution)/shard_map/psum | solution.py:416
  1068.7 359.4 %copy-start.28 = (f32[5,256,128]{2,1,0:T(8,128)S(1)}, f32[5,256,128]{2,1,0:T(8,128)}, u32[]{:S(2)}) copy-start(f32[5,256,128]{2,1,0:T(8,128)} %reduce-scatter.11.cloned.1.call-done) | copy-start | bytes 1966084
  (91 other events, 1733.0 us)
Sparse Core Ops, SparseCore 0:
  10.3 28.8 all-gather.6
  41.0 38.6 all-gather.14
  81.9 69.0 all-gather.10
  152.7 68.8 all-gather.8
  223.5 34.8 all-gather.12
  262.3 102.3 all-reduce.8
  379.2 103.8 all-reduce.10
  509.7 103.8 all-reduce.12
  639.2 103.8 all-reduce.14
  779.8 161.2 reduce-scatter.14
  943.9 30.0 reduce-scatter.18
  976.7 31.4 reduce-scatter.12
  1010.7 57.9 reduce-scatter.10
  1070.9 137.4 reduce-scatter.8
  1210.7 38.6 reduce-scatter.16
  1256.3 119.6 all-reduce.16
where the time goes:
time: 1450 us; the launch traced here: 1440 us
  waiting for transfers between devices  961 us (66%)
  blocking collectives  186 us (13%)
  matrix products  102 us (7%)
  other arithmetic  93.1 us (6%)
  local copies, waits for them, and re-layouts  70.9 us (5%)
  between operations  22.8 us (2%)
    psum x4, waiting for transfers between devices, head_sum(): return lax.psum(values, 'tp')  377 us
    reduce_scatter x1, waiting for transfers between devices, on_device(): lax.psum_scatter(grad_block, ('fsdp', 'ctx'), scatter_dimension=0, tiled=...  138 us
    psum x1, waiting for transfers between devices, on_device(): lax.psum((grad_bias, loss_part), ('fsdp', 'ctx', 'tp'))  124 us
    unnamed x1, blocking collectives  106 us
    all_gather x1, waiting for transfers between devices, on_device(): lax.all_gather(layer_low[0], ('fsdp', 'ctx'), axis=0, tiled=True)  62.1 us
    reduce_scatter x1, waiting for transfers between devices, on_device(): lax.psum_scatter(grad_output, ('fsdp', 'ctx'), scatter_dimension=2, tiled...  58.8 us
    all_gather x1, waiting for transfers between devices, on_device(): lax.all_gather(top_part, 'tp', axis=1, tiled=True)  58.7 us
    psum x1, blocking collectives, on_device(): lax.psum((grad_bias, loss_part), ('fsdp', 'ctx', 'tp'))  41.2 us
  transfers between devices with their start and end apart: 17, of which 15 were waited for; matrix products, arithmetic and copies ran while one was open for 17% of the time, Pallas kernels for 0%

commit v1 on v0

v1 whole, which is shorter than its diff:
```python
import functools
import math

import jax
import jax.numpy as jnp
from jax import lax
from jax.experimental import pallas as pl
from jax.experimental.pallas import tpu as pltpu
from jax.sharding import PartitionSpec as P

HEAD_DIM = 64
CLASSES = 1000
FREQ = 256
TIMESTEPS = 1000
ADAM_STEP = 10
PATCH_ROWS = 16

PRECISE = lax.Precision.HIGHEST
BF = jnp.bfloat16
F32 = jnp.float32


def exact_dot(left, right):
    return jnp.dot(left, right, precision=PRECISE)


def mm(left, right):
    return jnp.dot(left, right, preferred_element_type=F32)


def mm_nt(left, right):
    return lax.dot_general(left, right, (((1,), (1,)), ((), ())), preferred_element_type=F32)


def mm_tn(left, right):
    return lax.dot_general(left, right, (((0,), (0,)), ((), ())), preferred_element_type=F32)


def layer_norm(values):
    center = values - jnp.mean(values, axis=-1, keepdims=True)
    spread = jnp.mean(center * center, axis=-1, keepdims=True)
    return center * lax.rsqrt(spread + 1e-06)


def modulate(values, shift, scale):
    return layer_norm(values) * (1.0 + scale[:, None, :]) + shift[:, None, :]


def gelu_tanh(values):
    return jax.nn.gelu(values, approximate=True)


def plan(step_ids):
    fraction = (step_ids.astype(F32) / TIMESTEPS + 0.008) / 1.008
    kept_share = jnp.cos(fraction * (math.pi / 2.0)) ** 2
    return (jnp.sqrt(kept_share), jnp.sqrt(1.0 - kept_share))


def patchify(field):
    img_count, chan_count, row_count, col_count = field.shape
    shaped = field.reshape(img_count, chan_count, row_count // 2, 2, col_count // 2, 2)
    shaped = shaped.transpose(0, 2, 4, 1, 3, 5)
    return shaped.reshape(img_count, row_count // 2 * (col_count // 2), chan_count * 4)


def adam_update(weight, gradient, first_mom, second_mom, clip_factor):
    clipped = gradient * clip_factor
    first_new = 0.9 * first_mom + 0.1 * clipped
    second_new = 0.999 * second_mom + 0.001 * clipped * clipped
    corr_first = 1.0 - 0.9**ADAM_STEP
    corr_second = 1.0 - 0.999**ADAM_STEP
    direction = first_new / corr_first / (jnp.sqrt(second_new / corr_second) + 1e-08)
    return (weight - 0.04 * (direction + 0.01 * weight), first_new, second_new)


def swap(value, axis, mask):
    count = lax.axis_size(axis)
    return lax.ppermute(value, axis, [(i, i ^ mask) for i in range(count)])


def pull(value, k):
    count = lax.axis_size("fsdp")
    return lax.ppermute(value, "fsdp", [((i + k) % count, i) for i in range(count)])


def push(value, k):
    count = lax.axis_size("fsdp")
    return lax.ppermute(value, "fsdp", [(i, (i + k) % count) for i in range(count)])


def is_ring():
    return lax.axis_size("fsdp") == 4


def pick(pair, bit, axis=0):
    low = lax.index_in_dim(pair, 0, axis, keepdims=False)
    high = lax.index_in_dim(pair, 1, axis, keepdims=False)
    return jnp.where(bit == 1, high, low)


def ordered(own, other, bit, axis=0):
    return jnp.stack([jnp.where(bit == 0, own, other), jnp.where(bit == 0, other, own)], axis)


def bits(count):
    return [1 << b for b in range(count.bit_length() - 1)]


def by_xor(stack, rank):
    for mask in (1, 2):
        other = jnp.stack([stack[i ^ mask] for i in range(4)])
        stack = jnp.where(rank & mask == mask, other, stack)
    return stack


def sum_over(value, axes, pace=lambda v: v):
    for axis in axes:
        count = lax.axis_size(axis)
        if count > 4:
            value = lax.psum(value, axis)
            continue
        for mask in bits(count):
            value = value + swap(pace(value), axis, mask)
    return value


def scatter_fc(blocks, pace=lambda v: v):
    if not is_ring():
        return lax.psum_scatter(blocks, ("fsdp", "ctx"), scatter_dimension=0, tiled=False)
    f, c = lax.axis_index("fsdp"), lax.axis_index("ctx")
    shape = blocks.shape[1:]
    held = blocks.reshape((4, 2) + shape)
    held = pick(held, c, 1) + swap(pace(pick(held, 1 - c, 1)), "ctx", 1)
    held = held.reshape((2, 2) + shape)
    high, low = f >> 1, f & 1
    held = pick(held, high) + swap(pace(pick(held, 1 - high)), "fsdp", 2)
    return pick(held, low) + swap(pace(pick(held, 1 - low)), "fsdp", 1)


def gather_fc(value, pace=lambda v: v):
    if not is_ring():
        return lax.all_gather(value, ("fsdp", "ctx"), axis=0, tiled=False)
    f, c = lax.axis_index("fsdp"), lax.axis_index("ctx")
    shape = value.shape
    held = ordered(value, swap(pace(value), "fsdp", 1), f & 1)
    held = ordered(held, swap(pace(held), "fsdp", 2), f >> 1)
    held = held.reshape((4,) + shape)
    held = ordered(held, swap(pace(held), "ctx", 1), c, 1)
    return held.reshape((8,) + shape)


def exchange_tp(blocks):
    t = lax.axis_index("tp")
    mine = by_xor(blocks, t)
    got = jnp.stack([mine[0]] + [swap(mine[k], "tp", k) for k in (1, 2, 3)])
    return by_xor(got, t)


class Lane:
    def __init__(self, depth):
        self.depth = depth
        self.ended = []

    def __call__(self, value, move):
        if len(self.ended) >= self.depth:
            value, _ = lax.optimization_barrier((value, self.ended[-self.depth]))
        moved = move(value)
        self.ended.append(moved)
        return moved


class Pace:
    def __init__(self, lanes):
        self.waiting = list(lanes.ended)

    def __call__(self, value):
        if self.waiting:
            value, _ = lax.optimization_barrier((value, self.waiting.pop(0)))
        return value


class Lanes:
    def __init__(self, x, y, z):
        self.ended = []
        self.lane_x, self.lane_y, self.lane_z = Lane(x), Lane(y), Lane(z)

    def note(self, moved):
        self.ended.append(moved)
        return moved

    def x(self, value):
        return self.note(self.lane_x(value, lambda v: swap(v, "tp", 1)))

    def y(self, value):
        return self.note(self.lane_y(value, lambda v: swap(v, "tp", 2)))

    def pull(self, value, k):
        return self.note(self.lane_z(value, lambda v: pull(v, k)))

    def push(self, value, k):
        return self.note(self.lane_z(value, lambda v: push(v, k)))


def gather_grid(lanes, shard):
    if not is_ring():
        parts = [lax.all_gather(shard, "fsdp", axis=0, tiled=True)]
    else:
        one = lanes.pull(shard, 1)
        x_0, y_0 = lanes.x(shard), lanes.y(shard)
        three = lanes.pull(shard, 3)
        x_1, y_1 = lanes.x(one), lanes.y(one)
        two = lanes.pull(one, 1)
        d_0 = lanes.x(y_0)
        d_1 = lanes.y(x_1)
        x_3, y_3 = lanes.x(three), lanes.y(three)
        x_2, y_2 = lanes.x(two), lanes.y(two)
        d_3 = lanes.x(y_3)
        d_2 = lanes.y(x_2)
        return [
            [shard, x_0, y_0, d_0],
            [one, x_1, y_1, d_1],
            [two, x_2, y_2, d_2],
            [three, x_3, y_3, d_3],
        ]
    near = swap(parts[0], "tp", 1)
    return [[parts[0], near, swap(parts[0], "tp", 2), swap(near, "tp", 2)]]


def add(left, right):
    return left.astype(F32) + right.astype(F32)


def add_low(left, right):
    return add(left, right).astype(BF)


def reduce_grid(lanes, main):
    if not is_ring():
        parts = main[0]
        along_x = swap(parts[1], "tp", 1)
        along_y = swap(add_low(parts[2], swap(parts[3], "tp", 1)), "tp", 2)
        both = add_low(add(parts[0], along_x), along_y)
        return lax.psum_scatter(both, "fsdp", scatter_dimension=0, tiled=True).astype(F32)
    far_2, far_1 = lanes.y(main[2][3]), None
    far_3 = lanes.x(main[3][3])
    y_2 = lanes.y(main[2][2])
    x_2 = lanes.x(add_low(main[2][1], far_2))
    far_1 = lanes.y(main[1][3])
    x_3 = lanes.x(main[3][1])
    y_3 = lanes.y(add_low(main[3][2], far_3))
    sum_2 = lanes.push(add_low(add(main[2][0], x_2), y_2), 1)
    y_1 = lanes.y(main[1][2])
    x_1 = lanes.x(add_low(main[1][1], far_1))
    far_0 = lanes.x(main[0][3])
    sum_3 = lanes.push(add_low(add(main[3][0], x_3), y_3), 3)
    x_0 = lanes.x(main[0][1])
    sum_1 = add(add(add(main[1][0], x_1), y_1), sum_2).astype(BF)
    sum_1 = lanes.push(sum_1, 1)
    y_0 = lanes.y(add_low(main[0][2], far_0))
    return add(add(add(main[0][0], x_0), y_0), sum_3) + sum_1.astype(F32)


def rows_of(table, start, count):
    pad = jnp.zeros((count,) + table.shape[1:], table.dtype)
    padded = jnp.concatenate([pad, table, pad], axis=0)
    return lax.dynamic_slice_in_dim(padded, jnp.clip(start + count, 0, table.shape[0] + count), count, 0)


def call(body, outs, args, flops):
    flat, tree = jax.tree.flatten(args)
    held = sum(a.size * a.dtype.itemsize for a in list(flat) + list(outs))

    def kernel(*refs):
        body(*jax.tree.unflatten(tree, refs[: len(flat)]), *refs[len(flat) :])

    vmem = pl.BlockSpec(memory_space=pltpu.VMEM)
    return pl.pallas_call(
        kernel,
        out_shape=outs,
        in_specs=[vmem] * len(flat),
        out_specs=[vmem] * len(outs),
        compiler_params=pltpu.CompilerParams(vmem_limit_bytes=held + 16 * 1024 * 1024),
        cost_estimate=pl.CostEstimate(flops=flops, bytes_accessed=held, transcendentals=0),
    )(*flat)


def shape(rows, cols, dtype):
    return jax.ShapeDtypeStruct((rows, cols), dtype)


def lanes_of(ref, start, count):
    return ref[:, start : start + count]


def down_rows(parts, k_t, start, stop):
    return jnp.concatenate([row[k_t][:, start:stop] for row in parts], axis=0)


def along_cols(row, start, stop):
    return jnp.concatenate([p[:, start:stop] for p in row], axis=1)


def head_masks(half):
    at = lax.broadcasted_iota(jnp.int32, (1, half), 1) // HEAD_DIM
    return [at == h for h in range(half // HEAD_DIM)]


def softmax_rows(scores):
    top = jnp.max(scores, axis=-1, keepdims=True)
    grown = jnp.exp(scores - top)
    return grown / jnp.sum(grown, axis=-1, keepdims=True)


def merged(masks, values):
    total = values[-1]
    for mask, value in zip(masks[:-1], values[:-1]):
        total = jnp.where(mask, value, total)
    return total


def col_block(ref, starts, k_f, size):
    if starts is None:
        return (slice(None), slice(0, size))
    return (slice(None), pl.ds(pl.multiple_of(starts[k_f], size), size))


def kernel_starts(parts):
    if len(parts) == 1:
        return None
    size = parts[0][0].shape[0]
    f = lax.axis_index("fsdp")
    return [((f + k) & 3) * size for k in range(4)]


def qkv_kernel(tok_count, half, own_ref, other_ref, parts, bias_ref, qkv_ref, attended_ref):
    rows = own_ref.shape[0]
    size = parts[0][0].shape[0]
    masks = head_masks(half)
    starts = kernel_starts(parts)
    for i, ref in enumerate((own_ref, other_ref)):
        turned = jnp.concatenate(
            [ref[col_block(ref, starts, k_f, size)] for k_f in range(len(parts))], axis=1
        )
        for k_t in range(4):
            cols = slice(k_t * 3 * half, (k_t + 1) * 3 * half)
            weight = down_rows(parts, k_t, 0, 3 * half)
            qkv_ref[i * rows : (i + 1) * rows, cols] = (
                mm(turned, weight) + bias_ref[:, cols]
            ).astype(BF)
    for k_t in range(4):
        at = k_t * 3 * half
        for row in range(0, 2 * rows, tok_count):
            here = slice(row, row + tok_count)
            query = qkv_ref[here, at : at + half]
            key = qkv_ref[here, at + half : at + 2 * half]
            value = qkv_ref[here, at + 2 * half : at + 3 * half]
            got = []
            for mask in masks:
                masked = jnp.where(mask, query, jnp.zeros_like(query))
                probs = softmax_rows(mm_nt(masked, key) * 0.125).astype(BF)
                got.append(mm(probs, value))
            attended_ref[here, k_t * half : (k_t + 1) * half] = merged(masks, got).astype(BF)


def attention_back_kernel(tok_count, half, own_ref, other_ref, parts, qkv_ref, out_ref, sum_ref):
    rows = own_ref.shape[0]
    size = parts[0][0].shape[0]
    masks = head_masks(half)
    starts = kernel_starts(parts)
    turned = [
        jnp.concatenate(
            [ref[col_block(ref, starts, k_f, size)] for k_f in range(len(parts))], axis=1
        )
        for ref in (own_ref, other_ref)
    ]
    for k_t in range(4):
        at = k_t * 3 * half
        weight = down_rows(parts, k_t, 3 * half, 4 * half)
        for i in range(2):
            grad_half = mm(turned[i], weight).astype(BF)
            for row in range(0, rows, tok_count):
                here = slice(i * rows + row, i * rows + row + tok_count)
                grad = grad_half[row : row + tok_count]
                query = qkv_ref[here, at : at + half]
                key = qkv_ref[here, at + half : at + 2 * half]
                value = qkv_ref[here, at + 2 * half : at + 3 * half]
                grad_q, grad_k, grad_v = [], [], []
                for mask in masks:
                    zero = jnp.zeros_like(query)
                    probs = softmax_rows(mm_nt(jnp.where(mask, query, zero), key) * 0.125)
                    grad_p = mm_nt(jnp.where(mask, grad, zero), value)
                    grad_s = (
                        probs * (grad_p - jnp.sum(grad_p * probs, axis=-1, keepdims=True))
                    ).astype(BF)
                    grad_q.append(mm(grad_s, key))
                    grad_k.append(mm_tn(grad_s, query))
                    grad_v.append(mm_tn(probs.astype(BF), grad))
                out_ref[here, at : at + half] = (merged(masks, grad_q) * 0.125).astype(BF)
                out_ref[here, at + half : at + 2 * half] = (merged(masks, grad_k) * 0.125).astype(BF)
                out_ref[here, at + 2 * half : at + 3 * half] = merged(masks, grad_v).astype(BF)
        cols = slice(at, at + 3 * half)
        sum_ref[:, cols] = jnp.sum(out_ref[:, cols].astype(F32), axis=0, keepdims=True)


def to_features(left_ref, parts, start, stop, own_ref, other_ref):
    rows = own_ref.shape[0]
    size = parts[0][0].shape[0]
    starts = kernel_starts(parts)
    for k_f, row in enumerate(parts):
        weight = along_cols(row, start, stop)
        own_ref[col_block(own_ref, starts, k_f, size)] = mm_nt(left_ref[:rows], weight)
        other_ref[col_block(other_ref, starts, k_f, size)] = mm_nt(left_ref[rows:], weight)


def proj_kernel(half, attended_ref, parts, own_ref, other_ref):
    to_features(attended_ref, parts, 3 * half, 4 * half, own_ref, other_ref)


def qkv_back_kernel(half, grad_ref, parts, own_ref, other_ref):
    to_features(grad_ref, parts, 0, 3 * half, own_ref, other_ref)


def up_kernel(own_ref, other_ref, weight_ref, bias_ref, pre_ref, act_ref):
    rows, width = own_ref.shape
    size = weight_ref.shape[1] // 2
    for i in range(4):
        cols = slice(i * size, (i + 1) * size)
        weight = weight_ref[i * width : (i + 1) * width, :size]
        for j, ref in enumerate((own_ref, other_ref)):
            pre = mm(ref[...], weight) + bias_ref[:, cols]
            pre_ref[j * rows : (j + 1) * rows, cols] = pre
            act_ref[j * rows : (j + 1) * rows, cols] = gelu_tanh(pre).astype(BF)


def from_hidden(left_ref, weight_ref, at, own_ref, other_ref):
    rows, width = own_ref.shape
    size = weight_ref.shape[1] // 2
    block = width // 4
    for k in range(4):
        cols = slice(k * block, (k + 1) * block)
        weight = jnp.concatenate(
            [
                weight_ref[i * width + k * block : i * width + (k + 1) * block, at * size : (at + 1) * size]
                for i in range(4)
            ],
            axis=1,
        )
        own_ref[:, cols] = mm_nt(left_ref[:rows], weight)
        other_ref[:, cols] = mm_nt(left_ref[rows:], weight)


def down_kernel(act_ref, weight_ref, own_ref, other_ref):
    from_hidden(act_ref, weight_ref, 1, own_ref, other_ref)


def up_back_kernel(grad_ref, weight_ref, own_ref, other_ref):
    from_hidden(grad_ref, weight_ref, 0, own_ref, other_ref)


def gelu_slope(values):
    scale = math.sqrt(2.0 / math.pi)
    bent = jnp.tanh(scale * (values + 0.044715 * (values * values * values)))
    inner = scale * (1.0 + 3.0 * 0.044715 * (values * values))
    return 0.5 * (1.0 + bent) + 0.5 * values * (1.0 - bent * bent) * inner


def down_back_kernel(own_ref, other_ref, weight_ref, pre_ref, grad_ref, sum_ref):
    rows, width = own_ref.shape
    size = weight_ref.shape[1] // 2
    for i in range(4):
        cols = slice(i * size, (i + 1) * size)
        weight = weight_ref[i * width : (i + 1) * width, size:]
        total = 0.0
        for j, ref in enumerate((own_ref, other_ref)):
            here = slice(j * rows, (j + 1) * rows)
            grad = (mm(ref[...], weight) * gelu_slope(pre_ref[here, cols])).astype(BF)
            grad_ref[here, cols] = grad
            total = total + jnp.sum(grad.astype(F32), axis=0, keepdims=True)
        sum_ref[:, cols] = total


def block_starts(width):
    if not is_ring():
        return [0], width
    rows = width // 4
    f = lax.axis_index("fsdp")
    return [((f + k) & 3) * rows for k in range(4)], rows


def on_device(
    latents,
    noise_sample,
    timesteps,
    class_labels,
    w_block,
    w_output,
    w_top,
    w_head,
    w_embed,
    biases,
    m_block,
    m_output,
    m_top,
    m_head,
    m_embed,
    m_biases,
    v_block,
    v_output,
    v_top,
    v_head,
    v_embed,
    v_biases,
):
    f, c, t = lax.axis_index("fsdp"), lax.axis_index("ctx"), lax.axis_index("tp")
    nt = lax.axis_size("tp")
    places = lax.axis_size("fsdp") * lax.axis_size("ctx")
    place = f * lax.axis_size("ctx") + c
    row_count, block_count, local_width = w_block.shape
    half = local_width // 2
    width = local_width * nt
    group_images = latents.shape[0]
    images_all = group_images * places
    img_count = group_images // nt
    grid_side = latents.shape[3] // 2
    tok_count = latents.shape[2] // 2 * grid_side
    embed_rows = w_embed.shape[0]
    top_cols = w_top.shape[1]

    block_low = jnp.transpose(w_block, (1, 0, 2)).astype(BF)
    output_low = jnp.transpose(w_output, (0, 2, 1)).astype(BF)
    top_low = w_top.astype(BF)
    embed_low = w_embed.astype(BF)

    def core_half(blocks):
        low, high = blocks[:, :, :half], blocks[:, :, half:]
        return jnp.where(c == 0, low, high), jnp.where(c == 0, high, low)

    def beside(blocks):
        return jnp.concatenate([blocks[i] for i in range(blocks.shape[0])], axis=1)

    mixed = jnp.concatenate(
        [block_low[0:3], output_low[0:1], block_low[3:7], output_low[1:5]], axis=0
    )
    mine, other = core_half(mixed)
    mine, other = beside(mine), swap(beside(other), "ctx", 1)
    shards = jnp.concatenate(
        [jnp.where(c == 0, mine, other), jnp.where(c == 0, other, mine)], axis=0
    )
    lanes = Lanes(1, 1, 1)
    hidden_full = lax.all_gather(shards[:, 4 * half :], ("tp", "fsdp"), axis=0, tiled=True)
    parts = gather_grid(lanes, shards[:, : 4 * half])
    pace = Pace(lanes)

    patch_rows = rows_of(embed_low, FREQ + CLASSES - embed_rows * t, PATCH_ROWS)
    ids = jnp.concatenate([timesteps, class_labels]).astype(F32)
    ids = jnp.concatenate([ids, jnp.zeros((row_count - 2 * group_images % row_count,), F32)])[None]
    ids = ids.reshape(-1, row_count)
    small = jnp.concatenate([ids, patch_rows.astype(F32), w_head.T.astype(BF).astype(F32)], axis=0)
    small = gather_fc(small, pace)
    ids_all = small[:, : ids.shape[0]].reshape(places, -1)
    steps_all = ids_all[:, :group_images].reshape(images_all)
    labels_all = ids_all[:, group_images : 2 * group_images].reshape(images_all).astype(jnp.int32)
    small = small[:, ids.shape[0] :].transpose(1, 0, 2).reshape(2 * PATCH_ROWS, width)
    patch_part, w_head_t = small[:PATCH_ROWS], small[PATCH_ROWS:].astype(BF)
    embed_at = embed_rows * t + jnp.arange(embed_rows, dtype=jnp.int32)
    half_freq = FREQ // 2
    rates = jnp.exp(-math.log(10000.0) * (embed_at % half_freq).astype(F32) / half_freq)
    angles = steps_all[:, None] * rates[None, :]
    waves = jnp.where(embed_at[None, :] < half_freq, jnp.cos(angles), jnp.sin(angles))
    freq_low = jnp.where(embed_at[None, :] < FREQ, waves, 0.0).astype(BF)
    one_hot = (labels_all[:, None] + FREQ == embed_at[None, :]).astype(BF)
    own_cols = lambda row: lax.dynamic_slice_in_dim(row, place * row_count, row_count, 0)
    over_tp = jnp.concatenate([mm(freq_low, embed_low), patch_part.reshape(-1, row_count)], axis=0)
    over_tp = sum_over(over_tp, ("tp",), pace)
    t_pre = over_tp[:images_all] + own_cols(biases[1])
    w_patch = over_tp[images_all:].reshape(PATCH_ROWS, width).astype(BF)
    t_hidden = jax.nn.silu(t_pre).astype(BF)
    table_part = mm(one_hot, embed_low)
    top_at = top_cols * t + jnp.arange(top_cols, dtype=jnp.int32)
    cond_cols = mm(t_hidden, top_low)
    cond_cols = jnp.where(top_at[None, :] < width, cond_cols, 0.0)
    cond_wide = jnp.concatenate(
        [jnp.zeros((images_all, width), F32), cond_cols, jnp.zeros((images_all, width), F32)], axis=1
    )
    cond_wide = lax.dynamic_slice_in_dim(
        cond_wide, jnp.clip(width - top_cols * t, 0, width + top_cols), width, 1
    )
    cond_blocks = cond_wide.reshape(images_all, places, row_count).transpose(1, 0, 2)
    cond = sum_over(scatter_fc(cond_blocks, pace) + table_part, ("tp",), pace) + own_cols(biases[2])
    cond_low = jax.nn.silu(cond).astype(BF)
    mod_low = block_low[7:13]
    mod_cols = jnp.concatenate([mm(cond_low, mod_low[j]) for j in range(6)], axis=1)
    final_cols = jnp.where(top_at[None, :] < width, 0.0, mm(cond_low, top_low))
    all_cols = jnp.concatenate([mod_cols, final_cols], axis=1)
    group_cols = scatter_fc(all_cols.reshape(places, group_images, all_cols.shape[1]), pace)
    own_parts = exchange_tp(group_cols.reshape(nt, img_count, -1))
    mod_width = 6 * local_width
    modulation = (
        own_parts[:, :, :mod_width]
        .reshape(nt, img_count, 6, local_width)
        .transpose(1, 2, 0, 3)
        .reshape(img_count, 6, width)
    ) + biases[3:9][None]
    final_mod = own_parts[:, :, mod_width:].transpose(1, 0, 2).reshape(img_count, 3 * width)
    final_mod = final_mod[:, width:].reshape(img_count, 2, width) + biases[17:19][None]
    shift_f, scale_f = final_mod[:, 0], final_mod[:, 1]

    def own_images(values):
        return lax.dynamic_slice_in_dim(values, t * img_count, img_count, 0)

    latent_vals = own_images(latents).astype(F32)
    noise_vals = own_images(noise_sample).astype(F32)
    keep_rate, drop_rate = plan(own_images(timesteps))
    noisy = (
        keep_rate[:, None, None, None] * latent_vals + drop_rate[:, None, None, None] * noise_vals
    )
    patches = patchify(noisy).astype(BF)
    target = patchify(noise_vals)

    quarter = width // 4
    pos_rates = jnp.exp(-math.log(10000.0) * jnp.arange(quarter, dtype=F32) / quarter)
    side_angle = jnp.arange(grid_side, dtype=F32)[:, None] * pos_rates[None, :]
    side = jnp.concatenate([jnp.sin(side_angle), jnp.cos(side_angle)], axis=-1)
    rows_side = jnp.broadcast_to(side[:, None, :], (tok_count // grid_side, grid_side, 2 * quarter))
    cols_side = jnp.broadcast_to(side[None, :, :], (tok_count // grid_side, grid_side, 2 * quarter))
    positions = jnp.concatenate([rows_side, cols_side], axis=-1).reshape(tok_count, width)

    bias_width = jnp.stack([biases[0], biases[11], biases[16]])

    def heads_bias(rows):
        shaped = rows.reshape(-1, nt, 2, half)
        mine = jnp.where(c == 0, shaped[:, :, 0], shaped[:, :, 1])
        return by_xor(mine.transpose(1, 0, 2), t)

    bias_qv = heads_bias(biases[9:11])
    bias_qkv = jnp.stack([bias_qv[:, 0], jnp.zeros_like(bias_qv[:, 0]), bias_qv[:, 1]], axis=1).reshape(-1)
    bias_up = biases[12:16].reshape(4, nt, 2, half)
    bias_up = jnp.where(c == 0, bias_up[:, :, 0], bias_up[:, :, 1]).transpose(1, 0, 2).reshape(-1)

    own_count = img_count * tok_count
    core_width = nt * half
    matrix_flops = 4 * own_count * width * half

    def tokens(values):
        flat = values.reshape(own_count, width)
        return flat, swap(flat, "ctx", 1)

    def core_sum(own, other):
        return (own + swap(other, "ctx", 1)).reshape(img_count, tok_count, width)

    two_sums = [shape(own_count, width, F32)] * 2

    def run(body, outs, blocks, *args):
        return call(body, outs, args, blocks * nt * matrix_flops)

    resid_in = (
        jnp.einsum("btc,cd->btd", patches, w_patch, preferred_element_type=F32)
        + bias_width[0]
        + positions[None]
    )
    attn_in = modulate(resid_in, modulation[:, 0], modulation[:, 1]).astype(BF)
    attn_own, attn_other = tokens(attn_in)
    qkv_low, attended = run(
        functools.partial(qkv_kernel, tok_count, half),
        [shape(2 * own_count, 3 * core_width, BF), shape(2 * own_count, core_width, BF)],
        4,
        attn_own,
        attn_other,
        parts,
        bias_qkv[None],
    )
    attn_out = core_sum(
        *run(functools.partial(proj_kernel, half), two_sums, 1, attended, parts)
    ) + bias_width[1]
    resid_mid = resid_in + modulation[:, 2][:, None, :] * attn_out
    mlp_own, mlp_other = tokens(modulate(resid_mid, modulation[:, 3], modulation[:, 4]).astype(BF))
    up_pre, up_act = run(
        up_kernel,
        [shape(2 * own_count, 4 * core_width, F32), shape(2 * own_count, 4 * core_width, BF)],
        4,
        mlp_own,
        mlp_other,
        hidden_full,
        bias_up[None],
    )
    mlp_out = core_sum(
        *run(down_kernel, two_sums, 4, up_act, hidden_full)
    ) + bias_width[2]
    resid_out = resid_mid + modulation[:, 5][:, None, :] * mlp_out
    head_in = modulate(resid_out, shift_f, scale_f).astype(BF)
    predicted = jnp.einsum("btd,cd->btc", head_in, w_head_t, preferred_element_type=F32)
    error = predicted - target
    loss_part = jnp.sum(error * error) / images_all

    grad_pred = (2.0 / images_all * error).astype(BF)
    grad_head_in = jnp.einsum("btc,cd->btd", grad_pred, w_head_t, preferred_element_type=F32)
    grad_head = jnp.einsum("btc,btd->cd", grad_pred, head_in, preferred_element_type=F32)
    grad_resid, grad_shift_f, grad_scale_f = jax.vjp(modulate, resid_out, shift_f, scale_f)[1](
        grad_head_in
    )
    grad_gate_b = jnp.sum(grad_resid * mlp_out, axis=1)
    grad_mlp_own = (grad_resid * modulation[:, 5][:, None, :]).astype(BF)
    grad_b_down = jnp.sum(grad_mlp_own.astype(F32), axis=(0, 1))
    grad_mlp, grad_mlp_other = tokens(grad_mlp_own)
    both_mlp = jnp.concatenate([grad_mlp, grad_mlp_other], axis=0)
    hidden = 4 * half

    def by_hidden(left, right):
        return jnp.concatenate(
            [mm_tn(left, right[:, i * hidden : (i + 1) * hidden]).astype(BF) for i in range(4)], axis=0
        )

    grad_down = by_hidden(both_mlp, up_act)
    down_sum = lax.psum_scatter(grad_down, ("tp", "fsdp"), scatter_dimension=0, tiled=True)
    down_sum = down_sum.astype(F32)
    grad_mlp, grad_mlp_other, _ = lax.optimization_barrier((grad_mlp, grad_mlp_other, grad_down))
    grad_up, grad_b_up = run(
        down_back_kernel,
        [shape(2 * own_count, 4 * core_width, BF), shape(1, 4 * core_width, F32)],
        4,
        grad_mlp,
        grad_mlp_other,
        hidden_full,
        up_pre,
    )
    grad_b_up = grad_b_up[0]
    grad_mlp_in = core_sum(
        *run(up_back_kernel, two_sums, 4, grad_up, hidden_full)
    )
    grad_norm_b = jax.vjp(modulate, resid_mid, modulation[:, 3], modulation[:, 4])[1](grad_mlp_in)
    grad_resid = grad_resid + grad_norm_b[0]
    grad_gate_a = jnp.sum(grad_resid * attn_out, axis=1)
    grad_attn_own = (grad_resid * modulation[:, 2][:, None, :]).astype(BF)
    grad_b_proj = jnp.sum(grad_attn_own.astype(F32), axis=(0, 1))
    grad_attn, grad_attn_other = tokens(grad_attn_own)
    grad_qkv, grad_b_qkv = run(
        functools.partial(attention_back_kernel, tok_count, half),
        [shape(2 * own_count, 3 * core_width, BF), shape(1, 3 * core_width, F32)],
        2,
        grad_attn,
        grad_attn_other,
        parts,
        qkv_low,
    )
    grad_b_qkv = grad_b_qkv[0]
    attn_in = jnp.concatenate([attn_own, attn_other], axis=0)
    mlp_in = jnp.concatenate([mlp_own, mlp_other], axis=0)
    grad_attn = jnp.concatenate([grad_attn, grad_attn_other], axis=0)
    grad_up_w = by_hidden(mlp_in, grad_up)
    starts, block_rows = block_starts(width)
    firsts = [
        (
            mm_tn(attn_in, grad_qkv[:, i * 3 * half : (i + 1) * 3 * half]).astype(BF),
            mm_tn(grad_attn, attended[:, i * half : (i + 1) * half]).astype(BF),
        )
        for i in range(4)
    ]
    pieces = []
    for start in starts:
        line = []
        for k_t in range(4):
            cuts = [lax.dynamic_slice_in_dim(m, start, block_rows, 0) for m in firsts[k_t]]
            hidden_at = (t ^ k_t) * width + start
            cuts.append(lax.dynamic_slice_in_dim(grad_up_w, hidden_at, block_rows, 0))
            line.append(jnp.concatenate(cuts, axis=1))
        pieces.append(line)
    lanes = Lanes(1, 1, 1)
    first_sum = reduce_grid(lanes, pieces)
    grad_attn_in = core_sum(
        *run(functools.partial(qkv_back_kernel, half), two_sums, 3, grad_qkv, parts)
    )
    grad_norm_a = jax.vjp(modulate, resid_in, modulation[:, 0], modulation[:, 1])[1](grad_attn_in)
    grad_resid_low = (grad_resid + grad_norm_a[0]).astype(BF)
    grad_b_patch = jnp.sum(grad_resid_low.astype(F32), axis=(0, 1))
    grad_patch = jnp.einsum("btc,btd->cd", patches, grad_resid_low, preferred_element_type=F32)

    grad_mod = (
        jnp.stack(
            [
                grad_norm_a[1],
                grad_norm_a[2],
                grad_gate_a,
                grad_norm_b[1],
                grad_norm_b[2],
                grad_gate_b,
            ],
            axis=1,
        )
    )
    grad_final = (jnp.stack([grad_shift_f, grad_scale_f], axis=1))
    final_flat = jnp.concatenate(
        [jnp.zeros((img_count, width), F32), grad_final.reshape(img_count, 2 * width)], axis=1
    )
    to_tp = jnp.concatenate(
        [
            grad_mod.reshape(img_count, 6, nt, local_width)
            .transpose(2, 0, 1, 3)
            .reshape(nt, img_count, mod_width),
            final_flat.reshape(img_count, nt, top_cols).transpose(1, 0, 2),
        ],
        axis=-1,
    )
    group_grad = exchange_tp(to_tp).reshape(group_images, -1)
    all_grad = gather_fc(group_grad).reshape(images_all, -1)
    all_mod, all_final = all_grad[:, :mod_width], all_grad[:, mod_width:]
    cond_rows = cond_low.astype(F32)
    grad_w_mod = exact_dot(cond_rows.T, all_mod)
    mod_flat = mod_low.astype(F32).transpose(1, 0, 2).reshape(row_count, mod_width)
    top_rows = top_low.astype(F32)
    grad_cond_act = sum_over(
        exact_dot(all_mod, mod_flat.T) + exact_dot(all_final, top_rows.T), ("tp",)
    )
    grad_cond = jax.vjp(jax.nn.silu, cond)[1](grad_cond_act)[0]
    cond_all = gather_fc(grad_cond).transpose(1, 0, 2).reshape(images_all, width)
    grad_b_cond = jnp.sum(cond_all, axis=0)
    cond_padded = jnp.concatenate([cond_all, jnp.zeros((images_all, 2 * width), F32)], axis=1)
    cond_top = lax.dynamic_slice_in_dim(cond_padded, top_cols * t, top_cols, 1)
    top_grad = exact_dot(cond_rows.T, all_final) + exact_dot(t_hidden.astype(F32).T, cond_top)
    grad_hidden = sum_over(exact_dot(cond_top, top_rows.T), ("tp",))
    grad_t_pre = jax.vjp(jax.nn.silu, t_pre)[1](grad_hidden)[0]

    def heads_place(grad_rows):
        rows = by_xor(grad_rows, t).transpose(1, 0, 2)
        empty = jnp.zeros_like(rows)
        return jnp.stack(
            [jnp.where(c == 0, rows, empty), jnp.where(c == 0, empty, rows)], axis=2
        ).reshape(-1, width)

    qkv_rows = grad_b_qkv.reshape(nt, 3, half)
    up_rows = grad_b_up.reshape(nt, 4, half).transpose(1, 0, 2)
    empty_rows = jnp.zeros_like(up_rows)
    up_rows = jnp.stack(
        [jnp.where(c == 0, up_rows, empty_rows), jnp.where(c == 0, empty_rows, up_rows)], axis=2
    ).reshape(4, width)
    width_rows = (
        jnp.concatenate(
            [grad_b_patch[None], grad_b_proj[None], grad_b_down[None], grad_patch, grad_head], axis=0
        )
    )
    loss_row = jnp.broadcast_to(loss_part, (1, width))
    payload = jnp.concatenate(
        [
            width_rows[0:1],
            loss_row,
            jnp.zeros((1, width), F32),
            jnp.sum(grad_mod, axis=0),
            heads_place(jnp.stack([qkv_rows[:, 0], qkv_rows[:, 2]], axis=1)),
            width_rows[1:2],
            up_rows,
            width_rows[2:3],
            jnp.sum(grad_final, axis=0),
            width_rows[3:],
        ],
        axis=0,
    )
    payload = sum_over(payload, ("ctx", "tp", "fsdp"))
    loss_total = payload[1, 0]
    small_sum = lax.dynamic_slice_in_dim(payload[19:], place * row_count, row_count, 1)
    patch_sum, head_sum = small_sum[:PATCH_ROWS], small_sum[PATCH_ROWS:]
    head_grad_sum = head_sum.T

    def from_cores(total):
        low, high = total[:row_count], total[row_count:]
        own = jnp.where(c == 0, low, high)
        got = swap(jnp.where(c == 0, high, low), "ctx", 1)
        left, right = jnp.where(c == 0, own, got), jnp.where(c == 0, got, own)
        return [
            jnp.concatenate([left[:, i : i + half], right[:, i : i + half]], axis=1)
            for i in range(0, total.shape[1], half)
        ]

    first_own = from_cores(first_sum)
    down_own = from_cores(down_sum)
    block_sum = jnp.stack(first_own[0:3] + first_own[4:8])
    output_sum = jnp.transpose(jnp.stack(first_own[3:4] + down_own), (0, 2, 1))
    block_sum = jnp.concatenate(
        [block_sum, grad_w_mod.reshape(row_count, 6, local_width).transpose(1, 0, 2)], axis=0
    )
    embed_sum = exact_dot(one_hot.astype(F32).T, grad_cond) + exact_dot(
        freq_low.astype(F32).T, grad_t_pre
    )
    patch_padded = jnp.concatenate(
        [jnp.zeros((embed_rows, row_count), F32), patch_sum, jnp.zeros((embed_rows, row_count), F32)],
        axis=0,
    )
    patch_start = embed_rows * t + embed_rows - (FREQ + CLASSES)
    embed_sum = embed_sum + lax.dynamic_slice_in_dim(
        patch_padded, jnp.clip(patch_start, 0, embed_rows + PATCH_ROWS), embed_rows, 0
    )

    head_squares = jnp.where(t == 0, jnp.sum(head_grad_sum * head_grad_sum), 0.0)
    shard_squares = (
        jnp.sum(block_sum * block_sum)
        + jnp.sum(output_sum * output_sum)
        + jnp.sum(embed_sum * embed_sum)
        + jnp.sum(top_grad * top_grad)
        + head_squares
    )
    b1_part = jnp.where(t == 0, jnp.sum(grad_t_pre, axis=0), 0.0)
    b1_row = lax.dynamic_update_slice_in_dim(jnp.zeros((width,), F32), b1_part, place * row_count, 0)
    last = jnp.concatenate([b1_row, jnp.broadcast_to(shard_squares, (128,))])
    last = sum_over(last, ("ctx", "tp", "fsdp"))
    bias_sum = jnp.concatenate(
        [payload[0:1], last[None, :width], grad_b_cond[None], payload[3:19]], axis=0
    )
    grad_norm = jnp.sqrt(last[width] + jnp.sum(bias_sum * bias_sum))
    clip_factor = jnp.minimum(1.0, 1.0 / (grad_norm + 1e-06))
    upd_block = [
        jnp.transpose(u, (1, 0, 2))
        for u in adam_update(
            jnp.transpose(w_block, (1, 0, 2)),
            block_sum,
            jnp.transpose(m_block, (1, 0, 2)),
            jnp.transpose(v_block, (1, 0, 2)),
            clip_factor,
        )
    ]
    upd_output = adam_update(w_output, output_sum, m_output, v_output, clip_factor)
    upd_top = adam_update(w_top, top_grad, m_top, v_top, clip_factor)
    upd_head = adam_update(w_head, head_grad_sum, m_head, v_head, clip_factor)
    upd_embed = adam_update(w_embed, embed_sum, m_embed, v_embed, clip_factor)
    upd_biases = adam_update(biases, bias_sum, m_biases, v_biases, clip_factor)
    updates = (upd_block, upd_output, upd_top, upd_head, upd_embed, upd_biases)
    return (
        (loss_total, grad_norm)
        + tuple(u[0] for u in updates)
        + tuple(u[1] for u in updates)
        + tuple(u[2] for u in updates)
        + (bias_sum * clip_factor,)
    )


def solution(mesh):
    both = ("fsdp", "ctx")
    weights = (
        P(both, None, "tp"),
        P(None, "tp", both),
        P(both, "tp"),
        P(both, None),
        P("tp", both),
        P(),
    )
    images = (P(both, None, None, None), P(both, None, None, None), P(both), P(both))
    return jax.shard_map(
        on_device,
        mesh=mesh,
        in_specs=images + weights * 3,
        out_specs=(P(), P()) + weights * 3 + (P(),),
        check_vma=False,
    )
```

time: 1450 us -> 529 us (0.36)
  waiting for transfers between devices: 961 us -> 199 us
  blocking collectives: 186 us -> 0 us
  starting transfers between devices: 4.99 us -> 67.8 us
  matrix products: 102 us -> 46.1 us
  Pallas kernels: 0 us -> 37.9 us
  other arithmetic: 93.1 us -> 76.1 us
    psum x5 -> x0, waiting for transfers between devices: 501 us -> none  [the longest x4 377 us: head_sum(): return lax.psum(values, 'tp')]
    reduce_scatter x6 -> x1, waiting for transfers between devices: 282 us -> 0.02 us  [on_device(): lax.psum_scatter(grad_down, ('tp', 'fsdp'), scatter_dimension=0, tiled=True)]
    ppermute x0 -> x80, waiting for transfers between devices: none -> 171 us  [the longest x74 143 us: swap(): return lax.ppermute(value, axis, [(i, i ^ mask) for i in range(count)])]
    all_gather x5 -> x1, waiting for transfers between devices: 177 us -> 28 us  [on_device(): lax.all_gather(shards[:, 4 * half:], ('tp', 'fsdp'), axis=0, tiled=True)]
    unnamed x1 -> x0, blocking collectives: 106 us -> none
    ppermute x0 -> x80, starting transfers between devices: none -> 67.5 us  [the longest x74 58.7 us: swap(): return lax.ppermute(value, axis, [(i, i ^ mask) for i in range(count)])]
    psum x1 -> x0, blocking collectives: 41.2 us -> none  [on_device(): lax.psum((grad_bias, loss_part), ('fsdp', 'ctx', 'tp'))]
    all_gather x3 -> x0, blocking collectives: 39.4 us -> none  [the longest x1 17.4 us: on_device(): lax.all_gather(w_embed.astype(jnp.bfloat16), ('fsdp', 'ctx'), axis=1, til...]
  transfers between devices with their start and end apart: 17 -> 82, of which waited for: 15 -> 43; matrix products, arithmetic and copies ran while one was open for 17% -> 23% of each run, Pallas kernels for 0% -> 6%
where the time goes in v1:
time: 529 us; the launch traced here: 522 us
  waiting for transfers between devices  199 us (38%)
  other arithmetic  76.1 us (14%)
  local copies, waits for them, and re-layouts  70.5 us (13%)
  starting transfers between devices  67.8 us (13%)
  matrix products  46.1 us (9%)
  Pallas kernels  37.9 us (7%)
  between operations  25.3 us (5%)
    ppermute x74, waiting for transfers between devices, swap(): return lax.ppermute(value, axis, [(i, i ^ mask) for i in range(count)])  143 us
    ppermute x74, starting transfers between devices, swap(): return lax.ppermute(value, axis, [(i, i ^ mask) for i in range(count)])  58.7 us
    unnamed x433, local copies, waits for them, and re-layouts  41.3 us
    pallas_call x8, Pallas kernels, call(): pl.pallas_call(kernel, out_shape=outs, in_specs=[vmem] * len(flat), out_s...  37.9 us
    all_gather x1, waiting for transfers between devices, on_device(): lax.all_gather(shards[:, 4 * half:], ('tp', 'fsdp'), axis=0, tiled=True)  28 us
    dot_general x16, matrix products, mm_tn(): lax.dot_general(left, right, (((0,), (0,)), ((), ())), preferred_element_...  23.9 us
    ppermute x3, waiting for transfers between devices, pull(): lax.ppermute(value, 'fsdp', [((i + k) % count, i) for i in range(count)])  20.4 us
    dot_general x10, matrix products, mm(): return jnp.dot(left, right, preferred_element_type=F32)  11 us
  transfers between devices with their start and end apart: 82, of which 43 were waited for; matrix products, arithmetic and copies ran while one was open for 23% of the time, Pallas kernels for 6%

profile of v1, /device:TPU:0, one launch (start us, length us, event | category | flops | bytes accessed | tf_op | source)
XLA Modules:
  0.0 522.3 jit_solution(10621710739463776325)
XLA Ops:
  14.3 4.6 collective-permute-start.1
  20.9 4.2 collective-permute-done.1.refs_6_.refs_5_
  28.9 5.2 collective-permute-done.3.refs_3_.refs_2_
  34.1 4.4 collective-permute-start.4
  40.7 4.3 collective-permute-done.5.refs_4_.refs_3_
  48.1 8.8 %collective-permute-done.7.refs_14_.refs_13_ = bf16[256,512]{1,0:T(8,128)(2,1)S(1)} collective-permute-done((bf16[256,512]{1,0:T(8,128)(2,1)S(1)}, bf16[256,512]{1,0:T(8,128)(2,1)S(1)}, u32[]{:S(2)}, u32[]{:S(2)}) %collective-permute-start.7) | collective-permute-done | bytes 262176 | tf_op jit(solution)/shard_map/ppermute | solution.py:83
  57.4 3.8 collective-permute-done.8
  71.2 7.5 %collective-permute-done.13.refs_10_.refs_9_ = bf16[256,512]{1,0:T(8,128)(2,1)S(1)} collective-permute-done((bf16[256,512]{1,0:T(8,128)(2,1)S(1)}, bf16[256,512]{1,0:T(8,128)(2,1)S(1)}, u32[]{:S(2)}, u32[]{:S(2)}) %collective-permute-start.13) | collective-permute-done | bytes 262176 | tf_op jit(solution)/shard_map/ppermute | solution.py:83
  83.6 4.2 collective-permute-done.15.refs_5_.refs_4_
  118.9 8.1 %collective-permute-done.23.refs_11_.refs_10_ = bf16[256,512]{1,0:T(8,128)(2,1)S(1)} collective-permute-done((bf16[256,512]{1,0:T(8,128)(2,1)S(1)}, bf16[256,512]{1,0:T(8,128)(2,1)S(1)}, u32[]{:S(2)}, u32[]{:S(2)}) %collective-permute-start.23) | collective-permute-done | bytes 262176 | tf_op jit(solution)/shard_map/ppermute | solution.py:78
  129.3 7.6 %collective-permute-done.24 = f32[2,4,2304]{2,1,0:T(4,128)S(1)} collective-permute-done((f32[2,4,2304]{2,1,0:T(4,128)S(1)}, f32[2,4,2304]{2,1,0:T(4,128)S(1)}, u32[]{:S(2)}, u32[]{:S(2)}) %collective-permute-start.24) | collective-permute-done | bytes 73760 | tf_op jit(solution)/shard_map/ppermute | solution.py:78
  137.0 5.6 %collective-permute-done.25.refs_12_.refs_11_ = bf16[256,512]{1,0:T(8,128)(2,1)S(1)} collective-permute-done((bf16[256,512]{1,0:T(8,128)(2,1)S(1)}, bf16[256,512]{1,0:T(8,128)(2,1)S(1)}, u32[]{:S(2)}, u32[]{:S(2)}) %collective-permute-start.25) | collective-permute-done | bytes 262176 | tf_op jit(solution)/shard_map/ppermute | solution.py:78
  143.5 5.1 collective-permute-done.26
  164.2 5.7 %shard_map.373 = (bf16[512,1536]{1,0:T(8,128)(2,1)S(1)}, bf16[512,512]{1,0:T(8,128)(2,1)S(1)}) custom-call(bf16[256,1024]{1,0:T(8,128)(2,1)} %add_convert_fusion.10.refs_0_, bf16[256,1024]{1,0:T(8,128)(2,1)} %collective-permute-done.30.refs_1_, bf16[256,512]{1,0:T(8,128)(2,1)S(1)} %pad_maximum_fusion.18.refs_2_.refs_1_, ...), custom_call_target="tpu_custom_call" | custom-call | flops 2147483648 | bytes 7346176 | tf_op jit(solution)/shard_map/pallas_call | solution.py:277
  183.9 28.0 %all-gather.2.cloned.1.call-done.refs_2_.refs_1_ = bf16[4096,1024]{1,0:T(8,128)(2,1)} async-done(((bf16[256,1024]{1,0:T(8,128)(2,1)}), bf16[4096,1024]{1,0:T(8,128)(2,1)}) %all-gather.2.cloned.1.call-update) | async-done | bytes 8388624 | tf_op jit(solution)/shard_map/all_gather | solution.py:550
  211.9 3.4 copy-done
  215.3 3.5 shard_map.375
  258.8 5.5 %shard_map.377 = (bf16[512,2048]{1,0:T(8,128)(2,1)S(1)}, f32[1,2048]{1,0:T(1,128)S(1)}) custom-call(bf16[256,1024]{1,0:T(8,128)(2,1)} %get-tuple-element.107.refs_0_, bf16[256,1024]{1,0:T(8,128)(2,1)} %collective-permute-done.36.refs_1_, bf16[4096,1024]{1,0:T(8,128)(2,1)S(1)} %copy-done.2, f32[512,2048]{1,0:T(8,128)S(1)} %copy-done.5), custom_call_target="tpu_custom_call" | custom-call | flops 2147483648 | bytes 15736832 | tf_op jit(solution)/shard_map/pallas_call | solution.py:277
  264.3 3.4 copy-done.3
  267.7 3.4 shard_map.378
  288.3 11.1 %shard_map.379 = (bf16[512,1536]{1,0:T(8,128)(2,1)S(1)}, f32[1,1536]{1,0:T(1,128)S(1)}) custom-call(bf16[256,1024]{1,0:T(8,128)(2,1)S(1)} %get-tuple-element.224.refs_0_, bf16[256,1024]{1,0:T(8,128)(2,1)S(1)} %collective-permute-done.38.refs_1_, bf16[256,512]{1,0:T(8,128)(2,1)S(1)} %pad_maximum_fusion.18.refs_2_.refs_1_, bf16[256,512]{1,0:T(8,128)(2,1)S(1)} %copy-done.17, ...), custom_call_target="tpu_custom_call" | custom-call | flops 1073741824 | bytes 8394752 | tf_op jit(solution)/shard_map/pallas_call | solution.py:277
  299.4 4.3 shard_map.380
  346.9 4.9 collective-permute-done.49
  362.8 10.2 %collective-permute-done.52 = f32[32,128]{1,0:T(8,128)S(1)} collective-permute-done((f32[32,128]{1,0:T(8,128)S(1)}, f32[32,128]{1,0:T(8,128)S(1)}, u32[]{:S(2)}, u32[]{:S(2)}) %collective-permute-start.52) | collective-permute-done | bytes 16416 | tf_op jit(solution)/shard_map/ppermute | solution.py:78
  382.7 6.0 %collective-permute-done.60 = bf16[256,1024]{1,0:T(8,128)(2,1)S(1)} collective-permute-done((bf16[256,1024]{1,0:T(8,128)(2,1)}, bf16[256,1024]{1,0:T(8,128)(2,1)S(1)}, u32[]{:S(2)}, u32[]{:S(2)}) %collective-permute-start.60) | collective-permute-done | bytes 524320 | tf_op jit(solution)/shard_map/ppermute | solution.py:78
  393.3 11.7 %collective-permute-done.64 = bf16[256,1024]{1,0:T(8,128)(2,1)} collective-permute-done((bf16[256,1024]{1,0:T(8,128)(2,1)}, bf16[256,1024]{1,0:T(8,128)(2,1)}, u32[]{:S(2)}, u32[]{:S(2)}) %collective-permute-start.64) | collective-permute-done | bytes 524320 | tf_op jit(solution)/shard_map/ppermute | solution.py:78
  409.0 10.0 %collective-permute-done.56 = f32[32,128]{1,0:T(8,128)S(1)} collective-permute-done((f32[32,128]{1,0:T(8,128)S(1)}, f32[32,128]{1,0:T(8,128)S(1)}, u32[]{:S(2)}, u32[]{:S(2)}) %collective-permute-start.56) | collective-permute-done | bytes 16416 | tf_op jit(solution)/shard_map/ppermute | solution.py:78
  426.5 7.2 %collective-permute-done.71 = bf16[256,1024]{1,0:T(8,128)(2,1)S(1)} collective-permute-done((bf16[256,1024]{1,0:T(8,128)(2,1)S(1)}, bf16[256,1024]{1,0:T(8,128)(2,1)S(1)}, u32[]{:S(2)}, u32[]{:S(2)}) %collective-permute-start.71) | collective-permute-done | bytes 524320 | tf_op jit(solution)/shard_map/ppermute | solution.py:88
  440.5 3.8 collective-permute-done.42
  445.2 6.9 %collective-permute-done.43 = f32[51,1024]{1,0:T(8,128)S(1)} collective-permute-done((f32[51,1024]{1,0:T(8,128)S(1)}, f32[51,1024]{1,0:T(8,128)S(1)}, u32[]{:S(2)}, u32[]{:S(2)}) %collective-permute-start.43) | collective-permute-done | bytes 208928 | tf_op jit(solution)/shard_map/ppermute | solution.py:78
  454.1 8.3 %collective-permute-done.44 = f32[51,1024]{1,0:T(8,128)S(1)} collective-permute-done((f32[51,1024]{1,0:T(8,128)S(1)}, f32[51,1024]{1,0:T(8,128)S(1)}, u32[]{:S(2)}, u32[]{:S(2)}) %collective-permute-start.44) | collective-permute-done | bytes 208928 | tf_op jit(solution)/shard_map/ppermute | solution.py:78
  506.0 5.7 %fusion.23 = (f32[128,13,256]{2,0,1:T(8,128)}, f32[128,13,256]{2,0,1:T(8,128)}, f32[128,13,256]{2,0,1:T(8,128)}) fusion(f32[13,128,256]{2,1,0:T(8,128)S(1)} %bitcast_dynamic-update-slice_fusion, f32[]{:T(128)S(6)} %min.16, f32[128,13,256]{2,0,1:T(8,128)} %param.38, f32[128,13,256]{2,0,1:T(8,128)} %param.32, f32[128,13,256]{2,0,1:T(8,128)S(1)} %copy-done.58), kind=kLoop, calls=%fused_computation.131 | loop fusion | flops 6815744 | bytes 11927556 | tf_op jit(solution)/shard_map/transpose | solution.py:909
  (886 shorter events, 280.9 us)
Async XLA Ops:
  7.2 204.7 %all-gather.2.cloned.1.call-start = ((), (), s32[]{:S(2)}) async-start(), calls=%async_computation.1 | async-start | bytes 8912896 | tf_op jit(solution)/shard_map/all_gather | solution.py:550
  14.3 10.8 %collective-permute-start.1 = (bf16[256,512]{1,0:T(8,128)(2,1)S(1)}, bf16[256,512]{1,0:T(8,128)(2,1)S(1)}, u32[]{:S(2)}, u32[]{:S(2)}) collective-permute-start(bf16[256,512]{1,0:T(8,128)(2,1)S(1)} %pad_maximum_fusion.18.refs_2_.refs_1_), channel_id=1, source_target_pairs={{8,0},{16,8},{24,16},{0,24},{9,1},{17,9},{25,17},{1,25},{10,2},{18... | collective-permute-start | bytes 786440 | tf_op jit(solution)/shard_map/ppermute | solution.py:83
  45.0 16.2 %collective-permute-start.9 = (bf16[256,512]{1,0:T(8,128)(2,1)S(1)}, bf16[256,512]{1,0:T(8,128)(2,1)S(1)}, u32[]{:S(2)}, u32[]{:S(2)}) collective-permute-start(bf16[256,512]{1,0:T(8,128)(2,1)S(1)} %collective-permute-done.1.refs_6_.refs_5_), channel_id=1, source_target_pairs={{0,1},{1,0},{2,3},{3,2},{4,5},{5,4},{6,7},{7,6},{8,9},{9,8},{10,11... | collective-permute-start | bytes 786440 | tf_op jit(solution)/shard_map/ppermute | solution.py:78
  46.6 10.2 %collective-permute-start.7 = (bf16[256,512]{1,0:T(8,128)(2,1)S(1)}, bf16[256,512]{1,0:T(8,128)(2,1)S(1)}, u32[]{:S(2)}, u32[]{:S(2)}) collective-permute-start(bf16[256,512]{1,0:T(8,128)(2,1)S(1)} %pad_maximum_fusion.18.refs_2_.refs_1_), channel_id=1, source_target_pairs={{24,0},{0,8},{8,16},{16,24},{25,1},{1,9},{9,17},{17,25},{26,2},{2,... | collective-permute-start | bytes 786440 | tf_op jit(solution)/shard_map/ppermute | solution.py:83
  78.9 13.7 %collective-permute-start.17 = (bf16[256,512]{1,0:T(8,128)(2,1)S(1)}, bf16[256,512]{1,0:T(8,128)(2,1)S(1)}, u32[]{:S(2)}, u32[]{:S(2)}) collective-permute-start(bf16[256,512]{1,0:T(8,128)(2,1)S(1)} %collective-permute-done.9.refs_7_.refs_6_), channel_id=1, source_target_pairs={{0,2},{1,3},{2,0},{3,1},{4,6},{5,7},{6,4},{7,5},{8,10},{9,11},{10,... | collective-permute-start | bytes 786440 | tf_op jit(solution)/shard_map/ppermute | solution.py:78
  100.9 366.2 %reduce-scatter.2.cloned.1.call-start = ((), (), s32[]{:S(2)}) async-start(), calls=%async_computation.2 | async-start | bytes 4456448 | tf_op jit(solution)/shard_map/reduce_scatter | solution.py:714
  102.0 14.4 %collective-permute-start.21 = (bf16[256,512]{1,0:T(8,128)(2,1)S(1)}, bf16[256,512]{1,0:T(8,128)(2,1)S(1)}, u32[]{:S(2)}, u32[]{:S(2)}) collective-permute-start(bf16[256,512]{1,0:T(8,128)(2,1)S(1)} %collective-permute-done.7.refs_14_.refs_13_), channel_id=1, source_target_pairs={{0,2},{1,3},{2,0},{3,1},{4,6},{5,7},{6,4},{7,5},{8,10},{9,11},{10,... | collective-permute-start | bytes 786440 | tf_op jit(solution)/shard_map/ppermute | solution.py:78
  127.0 10.0 %collective-permute-start.24 = (f32[2,4,2304]{2,1,0:T(4,128)S(1)}, f32[2,4,2304]{2,1,0:T(4,128)S(1)}, u32[]{:S(2)}, u32[]{:S(2)}) collective-permute-start(f32[2,4,2304]{2,1,0:T(4,128)S(1)} %slice_select_fusion.4), channel_id=1, source_target_pairs={{0,16},{8,24},{16,0},{24,8},{1,17},{9,25},{17,1},{25,9},{2,18},{10... | collective-permute-start | bytes 221192 | tf_op jit(solution)/shard_map/ppermute | solution.py:78
  128.4 14.1 %collective-permute-start.25 = (bf16[256,512]{1,0:T(8,128)(2,1)S(1)}, bf16[256,512]{1,0:T(8,128)(2,1)S(1)}, u32[]{:S(2)}, u32[]{:S(2)}) collective-permute-start(bf16[256,512]{1,0:T(8,128)(2,1)S(1)} %collective-permute-done.13.refs_10_.refs_9_), channel_id=1, source_target_pairs={{0,2},{1,3},{2,0},{3,1},{4,6},{5,7},{6,4},{7,5},{8,10},{9,11},{10,... | collective-permute-start | bytes 786440 | tf_op jit(solution)/shard_map/ppermute | solution.py:78
  303.7 22.9 %collective-permute-start.39 = (f32[256,1024]{1,0:T(8,128)}, f32[256,1024]{1,0:T(8,128)}, u32[]{:S(2)}, u32[]{:S(2)}) collective-permute-start(f32[256,1024]{1,0:T(8,128)} %get-tuple-element.116), channel_id=1, source_target_pairs={{0,4},{4,0},{1,5},{5,1},{2,6},{6,2},{3,7},{7,3},{8,12},{12,8},{9,1... | collective-permute-start | bytes 3145736 | tf_op jit(solution)/shard_map/ppermute | solution.py:78
  313.1 43.7 %collective-permute-start.61 = (bf16[256,1024]{1,0:T(8,128)(2,1)}, bf16[256,1024]{1,0:T(8,128)(2,1)}, u32[]{:S(2)}, u32[]{:S(2)}) collective-permute-start(bf16[256,1024]{1,0:T(8,128)(2,1)} %pad_maximum_fusion.15), channel_id=1, source_target_pairs={{0,1},{1,0},{2,3},{3,2},{4,5},{5,4},{6,7},{7,6},{8,9},{9,8},{10,11... | collective-permute-start | bytes 1572872 | tf_op jit(solution)/shard_map/ppermute | solution.py:78
  315.2 39.4 %collective-permute-start.58 = (bf16[256,1024]{1,0:T(8,128)(2,1)}, bf16[256,1024]{1,0:T(8,128)(2,1)}, u32[]{:S(2)}, u32[]{:S(2)}) collective-permute-start(bf16[256,1024]{1,0:T(8,128)(2,1)} %pad_maximum_fusion.13), channel_id=1, source_target_pairs={{0,2},{1,3},{2,0},{3,1},{4,6},{5,7},{6,4},{7,5},{8,10},{9,11},{10,... | collective-permute-start | bytes 1572872 | tf_op jit(solution)/shard_map/ppermute | solution.py:78
  356.7 17.4 %collective-permute-start.62 = (bf16[256,1024]{1,0:T(8,128)(2,1)}, bf16[256,1024]{1,0:T(8,128)(2,1)}, u32[]{:S(2)}, u32[]{:S(2)}) collective-permute-start(bf16[256,1024]{1,0:T(8,128)(2,1)} %add_convert_fusion.5), channel_id=1, source_target_pairs={{0,1},{1,0},{2,3},{3,2},{4,5},{5,4},{6,7},{7,6},{8,9},{9,8},{10,11... | collective-permute-start | bytes 1572872 | tf_op jit(solution)/shard_map/ppermute | solution.py:78
  358.7 15.8 %collective-permute-start.59 = (bf16[256,1024]{1,0:T(8,128)(2,1)}, bf16[256,1024]{1,0:T(8,128)(2,1)}, u32[]{:S(2)}, u32[]{:S(2)}) collective-permute-start(bf16[256,1024]{1,0:T(8,128)(2,1)} %pad_maximum_fusion.12), channel_id=1, source_target_pairs={{0,2},{1,3},{2,0},{3,1},{4,6},{5,7},{6,4},{7,5},{8,10},{9,11},{10,... | collective-permute-start | bytes 1572872 | tf_op jit(solution)/shard_map/ppermute | solution.py:78
  359.3 13.8 %collective-permute-start.52 = (f32[32,128]{1,0:T(8,128)S(1)}, f32[32,128]{1,0:T(8,128)S(1)}, u32[]{:S(2)}, u32[]{:S(2)}) collective-permute-start(f32[32,128]{1,0:T(8,128)S(1)} %add.746), channel_id=1, source_target_pairs={{0,2},{1,3},{2,0},{3,1},{4,6},{5,7},{6,4},{7,5},{8,10},{9,11},{10,... | collective-permute-start | bytes 49160 | tf_op jit(solution)/shard_map/ppermute | solution.py:78
  374.1 15.6 %collective-permute-start.63 = (bf16[256,1024]{1,0:T(8,128)(2,1)}, bf16[256,1024]{1,0:T(8,128)(2,1)S(1)}, u32[]{:S(2)}, u32[]{:S(2)}) collective-permute-start(bf16[256,1024]{1,0:T(8,128)(2,1)} %pad_maximum_fusion.14), channel_id=1, source_target_pairs={{0,1},{1,0},{2,3},{3,2},{4,5},{5,4},{6,7},{7,6},{8,9},{9,8},{10,11... | collective-permute-start | bytes 1572872 | tf_op jit(solution)/shard_map/ppermute | solution.py:78
  374.5 14.2 %collective-permute-start.60 = (bf16[256,1024]{1,0:T(8,128)(2,1)}, bf16[256,1024]{1,0:T(8,128)(2,1)S(1)}, u32[]{:S(2)}, u32[]{:S(2)}) collective-permute-start(bf16[256,1024]{1,0:T(8,128)(2,1)} %pad_maximum_fusion.11), channel_id=1, source_target_pairs={{0,2},{1,3},{2,0},{3,1},{4,6},{5,7},{6,4},{7,5},{8,10},{9,11},{10,... | collective-permute-start | bytes 1572872 | tf_op jit(solution)/shard_map/ppermute | solution.py:78
  380.6 40.3 %collective-permute-start.70 = (bf16[256,1024]{1,0:T(8,128)(2,1)}, bf16[256,1024]{1,0:T(8,128)(2,1)}, u32[]{:S(2)}, u32[]{:S(2)}) collective-permute-start(bf16[256,1024]{1,0:T(8,128)(2,1)} %add_convert_fusion.1), channel_id=1, source_target_pairs={{0,8},{8,16},{16,24},{24,0},{1,9},{9,17},{17,25},{25,1},{2,10},{10... | collective-permute-start | bytes 1572872 | tf_op jit(solution)/shard_map/ppermute | solution.py:88
  381.4 55.7 %collective-permute-start.41 = (f32[51,1024]{1,0:T(8,128)}, f32[51,1024]{1,0:T(8,128)}, u32[]{:S(2)}, u32[]{:S(2)}) collective-permute-start(f32[51,1024]{1,0:T(8,128)} %add.740), channel_id=1, source_target_pairs={{0,1},{1,0},{2,3},{3,2},{4,5},{5,4},{6,7},{7,6},{8,9},{9,8},{10,11... | collective-permute-start | bytes 626696 | tf_op jit(solution)/shard_map/ppermute | solution.py:78
  382.7 10.6 %collective-permute-start.55 = (f32[4,32,128]{2,1,0:T(8,128)S(1)}, f32[4,32,128]{2,1,0:T(8,128)S(1)}, u32[]{:S(2)}, u32[]{:S(2)}) collective-permute-start(f32[4,32,128]{2,1,0:T(8,128)S(1)} %bitcast.507), channel_id=1, source_target_pairs={{0,4},{4,0},{1,5},{5,1},{2,6},{6,2},{3,7},{7,3},{8,12},{12,8},{9,1... | collective-permute-start | bytes 196616 | tf_op jit(solution)/shard_map/ppermute | solution.py:78
  389.7 15.2 %collective-permute-start.64 = (bf16[256,1024]{1,0:T(8,128)(2,1)}, bf16[256,1024]{1,0:T(8,128)(2,1)}, u32[]{:S(2)}, u32[]{:S(2)}) collective-permute-start(bf16[256,1024]{1,0:T(8,128)(2,1)} %add_convert_fusion.6), channel_id=1, source_target_pairs={{0,1},{1,0},{2,3},{3,2},{4,5},{5,4},{6,7},{7,6},{8,9},{9,8},{10,11... | collective-permute-start | bytes 1572872 | tf_op jit(solution)/shard_map/ppermute | solution.py:78
  392.6 14.8 %collective-permute-start.67 = (bf16[256,1024]{1,0:T(8,128)(2,1)}, bf16[256,1024]{1,0:T(8,128)(2,1)S(1)}, u32[]{:S(2)}, u32[]{:S(2)}) collective-permute-start(bf16[256,1024]{1,0:T(8,128)(2,1)} %add_convert_fusion.3), channel_id=1, source_target_pairs={{0,2},{1,3},{2,0},{3,1},{4,6},{5,7},{6,4},{7,5},{8,10},{9,11},{10,... | collective-permute-start | bytes 1572872 | tf_op jit(solution)/shard_map/ppermute | solution.py:78
  404.9 17.5 %collective-permute-start.65 = (bf16[256,1024]{1,0:T(8,128)(2,1)}, bf16[256,1024]{1,0:T(8,128)(2,1)S(1)}, u32[]{:S(2)}, u32[]{:S(2)}) collective-permute-start(bf16[256,1024]{1,0:T(8,128)(2,1)} %pad_maximum_fusion.10), channel_id=1, source_target_pairs={{0,1},{1,0},{2,3},{3,2},{4,5},{5,4},{6,7},{7,6},{8,9},{9,8},{10,11... | collective-permute-start | bytes 1572872 | tf_op jit(solution)/shard_map/ppermute | solution.py:78
  405.6 13.4 %collective-permute-start.56 = (f32[32,128]{1,0:T(8,128)S(1)}, f32[32,128]{1,0:T(8,128)S(1)}, u32[]{:S(2)}, u32[]{:S(2)}) collective-permute-start(f32[32,128]{1,0:T(8,128)S(1)} %fusion.54), channel_id=1, source_target_pairs={{0,1},{1,0},{2,3},{3,2},{4,5},{5,4},{6,7},{7,6},{8,9},{9,8},{10,11... | collective-permute-start | bytes 49160 | tf_op jit(solution)/shard_map/ppermute | solution.py:78
  407.4 17.0 %collective-permute-start.68 = (bf16[256,1024]{1,0:T(8,128)(2,1)}, bf16[256,1024]{1,0:T(8,128)(2,1)S(1)}, u32[]{:S(2)}, u32[]{:S(2)}) collective-permute-start(bf16[256,1024]{1,0:T(8,128)(2,1)} %pad_maximum_fusion.16), channel_id=1, source_target_pairs={{0,2},{1,3},{2,0},{3,1},{4,6},{5,7},{6,4},{7,5},{8,10},{9,11},{10,... | collective-permute-start | bytes 1572872 | tf_op jit(solution)/shard_map/ppermute | solution.py:78
  419.0 20.8 %collective-permute-start.57 = (f32[32,128]{1,0:T(8,128)S(1)}, f32[32,128]{1,0:T(8,128)S(1)}, u32[]{:S(2)}, u32[]{:S(2)}) collective-permute-start(f32[32,128]{1,0:T(8,128)S(1)} %add.749), channel_id=1, source_target_pairs={{0,2},{1,3},{2,0},{3,1},{4,6},{5,7},{6,4},{7,5},{8,10},{9,11},{10,... | collective-permute-start | bytes 49160 | tf_op jit(solution)/shard_map/ppermute | solution.py:78
  420.9 12.8 %collective-permute-start.71 = (bf16[256,1024]{1,0:T(8,128)(2,1)S(1)}, bf16[256,1024]{1,0:T(8,128)(2,1)S(1)}, u32[]{:S(2)}, u32[]{:S(2)}) collective-permute-start(bf16[256,1024]{1,0:T(8,128)(2,1)S(1)} %add_convert_fusion.2), channel_id=1, source_target_pairs={{0,24},{8,0},{16,8},{24,16},{1,25},{9,1},{17,9},{25,17},{2,26},{10... | collective-permute-start | bytes 1572872 | tf_op jit(solution)/shard_map/ppermute | solution.py:88
  422.5 30.3 %collective-permute-start.66 = (bf16[256,1024]{1,0:T(8,128)(2,1)S(1)}, bf16[256,1024]{1,0:T(8,128)(2,1)S(1)}, u32[]{:S(2)}, u32[]{:S(2)}) collective-permute-start(bf16[256,1024]{1,0:T(8,128)(2,1)S(1)} %copy-done.105), channel_id=1, source_target_pairs={{0,1},{1,0},{2,3},{3,2},{4,5},{5,4},{6,7},{7,6},{8,9},{9,8},{10,11... | collective-permute-start | bytes 1572872 | tf_op jit(solution)/shard_map/ppermute | solution.py:78
  424.4 28.3 %collective-permute-start.69 = (bf16[256,1024]{1,0:T(8,128)(2,1)S(1)}, bf16[256,1024]{1,0:T(8,128)(2,1)S(1)}, u32[]{:S(2)}, u32[]{:S(2)}) collective-permute-start(bf16[256,1024]{1,0:T(8,128)(2,1)S(1)} %add_convert_fusion.4), channel_id=1, source_target_pairs={{0,2},{1,3},{2,0},{3,1},{4,6},{5,7},{6,4},{7,5},{8,10},{9,11},{10,... | collective-permute-start | bytes 1572872 | tf_op jit(solution)/shard_map/ppermute | solution.py:78
  433.7 19.0 %collective-permute-start.72 = (bf16[256,1024]{1,0:T(8,128)(2,1)S(1)}, bf16[256,1024]{1,0:T(8,128)(2,1)S(1)}, u32[]{:S(2)}, u32[]{:S(2)}) collective-permute-start(bf16[256,1024]{1,0:T(8,128)(2,1)S(1)} %add_convert_fusion), channel_id=1, source_target_pairs={{0,8},{8,16},{16,24},{24,0},{1,9},{9,17},{17,25},{25,1},{2,10},{10... | collective-permute-start | bytes 1572872 | tf_op jit(solution)/shard_map/ppermute | solution.py:88
  452.1 10.4 %collective-permute-start.44 = (f32[51,1024]{1,0:T(8,128)S(1)}, f32[51,1024]{1,0:T(8,128)S(1)}, u32[]{:S(2)}, u32[]{:S(2)}) collective-permute-start(f32[51,1024]{1,0:T(8,128)S(1)} %add.743), channel_id=1, source_target_pairs={{0,16},{8,24},{16,0},{24,8},{1,17},{9,25},{17,1},{25,9},{2,18},{10... | collective-permute-start | bytes 626696 | tf_op jit(solution)/shard_map/ppermute | solution.py:78
  454.0 11.5 %collective-permute-start.73 = (f32[128,1024]{1,0:T(8,128)}, f32[128,1024]{1,0:T(8,128)}, u32[]{:S(2)}, u32[]{:S(2)}) collective-permute-start(f32[128,1024]{1,0:T(8,128)} %slice_select_fusion), channel_id=1, source_target_pairs={{0,4},{4,0},{1,5},{5,1},{2,6},{6,2},{3,7},{7,3},{8,12},{12,8},{9,1... | collective-permute-start | bytes 1572872 | tf_op jit(solution)/shard_map/ppermute | solution.py:78
  (250 other events, 3338.8 us)
Sparse Core Ops, SparseCore 0:
  101.0 110.8 all-gather.1
  253.1 95.3 reduce-scatter.1

commit v2 on v1

v2 whole, which is shorter than its diff:
```python
import functools
import math

import jax
import jax.numpy as jnp
from jax import lax
from jax.experimental import pallas as pl
from jax.experimental.pallas import tpu as pltpu
from jax.sharding import PartitionSpec as P

HEAD_DIM = 64
CLASSES = 1000
FREQ = 256
TIMESTEPS = 1000
ADAM_STEP = 10
PATCH_ROWS = 16
PINS = (None, 1, 3, 4, 7)
CHAIN = (16, 1)
BIASES = (14, 1)

PRECISE = lax.Precision.HIGHEST
BF = jnp.bfloat16
F32 = jnp.float32


def exact_dot(left, right):
    return jnp.dot(left, right, precision=PRECISE)


def mm(left, right):
    return jnp.dot(left, right, preferred_element_type=F32)


def mm_nt(left, right):
    return lax.dot_general(left, right, (((1,), (1,)), ((), ())), preferred_element_type=F32)


def mm_tn(left, right):
    return lax.dot_general(left, right, (((0,), (0,)), ((), ())), preferred_element_type=F32)


def gelu_tanh(values):
    return jax.nn.gelu(values, approximate=True)


def plan(step_ids):
    fraction = (step_ids.astype(F32) / TIMESTEPS + 0.008) / 1.008
    kept_share = jnp.cos(fraction * (math.pi / 2.0)) ** 2
    return (jnp.sqrt(kept_share), jnp.sqrt(1.0 - kept_share))


def patchify(field):
    img_count, chan_count, row_count, col_count = field.shape
    shaped = field.reshape(img_count, chan_count, row_count // 2, 2, col_count // 2, 2)
    shaped = shaped.transpose(0, 2, 4, 1, 3, 5)
    return shaped.reshape(img_count, row_count // 2 * (col_count // 2), chan_count * 4)


def adam_update(weight, gradient, first_mom, second_mom, clip_factor):
    clipped = gradient * clip_factor
    first_new = 0.9 * first_mom + 0.1 * clipped
    second_new = 0.999 * second_mom + 0.001 * clipped * clipped
    corr_first = 1.0 - 0.9**ADAM_STEP
    corr_second = 1.0 - 0.999**ADAM_STEP
    direction = first_new / corr_first / (jnp.sqrt(second_new / corr_second) + 1e-08)
    return (weight - 0.04 * (direction + 0.01 * weight), first_new, second_new)


def swap(value, axis, mask):
    count = lax.axis_size(axis)
    return lax.ppermute(value, axis, [(i, i ^ mask) for i in range(count)])


def pull(value, k):
    count = lax.axis_size("fsdp")
    return lax.ppermute(value, "fsdp", [((i + k) % count, i) for i in range(count)])


def push(value, k):
    count = lax.axis_size("fsdp")
    return lax.ppermute(value, "fsdp", [(i, (i + k) % count) for i in range(count)])


def is_ring():
    return lax.axis_size("fsdp") == 4


def pick(pair, bit, axis=0):
    low = lax.index_in_dim(pair, 0, axis, keepdims=False)
    high = lax.index_in_dim(pair, 1, axis, keepdims=False)
    return jnp.where(bit == 1, high, low)


def ordered(own, other, bit, axis=0):
    return jnp.stack([jnp.where(bit == 0, own, other), jnp.where(bit == 0, other, own)], axis)


def bits(count):
    return [1 << b for b in range(count.bit_length() - 1)]


def by_xor(stack, rank):
    for mask in (1, 2):
        other = jnp.stack([stack[i ^ mask] for i in range(4)])
        stack = jnp.where(rank & mask == mask, other, stack)
    return stack


def free(value):
    return value


def sum_over(value, axes, pace=free):
    for axis in axes:
        count = lax.axis_size(axis)
        if count == 2:
            value = value + swap(pace(value), axis, 1)
        elif count == 4:
            sent = pace(value)
            one, two, three = [swap(sent, axis, k) for k in (1, 2, 3)]
            value = (value + one) + (two + three)
        else:
            value = lax.psum(value, axis)
    return value


def sum_slow(value, axes, pace, steps):
    for axis in axes:
        count = lax.axis_size(axis)
        if count > 4:
            value = lax.psum(value, axis)
            continue
        for mask in bits(count):
            moved = swap(pace(value), axis, mask)
            steps.append(moved)
            value = value + moved
    return value


def roll_lead(stack, steps):
    for mask in (1, 2):
        moved = jnp.stack([stack[(i + mask) % 4] for i in range(4)])
        stack = jnp.where(steps & mask == mask, moved, stack)
    return stack


def scatter_fc(blocks, pace=free):
    if not is_ring():
        return lax.psum_scatter(blocks, ("fsdp", "ctx"), scatter_dimension=0, tiled=False)
    f, c = lax.axis_index("fsdp"), lax.axis_index("ctx")
    held = blocks.reshape((4, 2) + blocks.shape[1:])
    held = pick(held, c, 1) + swap(pace(pick(held, 1 - c, 1)), "ctx", 1)
    held = pace(roll_lead(held, f))
    return (held[0] + push(held[2], 2)) + (push(held[1], 1) + push(held[3], 3))


def gather_fc(value, pace=free):
    if not is_ring():
        return lax.all_gather(value, ("fsdp", "ctx"), axis=0, tiled=False)
    f, c = lax.axis_index("fsdp"), lax.axis_index("ctx")
    sent = pace(value)
    held = jnp.stack([value] + [pull(sent, k) for k in (1, 2, 3)])
    held = roll_lead(held, (4 - f) & 3)
    held = ordered(held, swap(pace(held), "ctx", 1), c, 1)
    return held.reshape((8,) + value.shape)


def exchange_tp(blocks, pace=free):
    t = lax.axis_index("tp")
    mine = pace(by_xor(blocks, t))
    got = jnp.stack([mine[0]] + [swap(mine[k], "tp", k) for k in (1, 2, 3)])
    return by_xor(got, t)


class Lane:
    def __init__(self, depth):
        self.depth = depth
        self.ended = []

    def __call__(self, value, move):
        if len(self.ended) >= self.depth:
            value, _ = lax.optimization_barrier((value, self.ended[-self.depth]))
        moved = move(value)
        self.ended.append(moved)
        return moved


class Pace:
    def __init__(self, lanes, first, step, others=()):
        self.ended = list(lanes.ended)
        self.next, self.step = first, step
        self.others = list(others)

    def __call__(self, value):
        at = min(self.next, len(self.ended) - 1)
        if at >= 0:
            value, _ = lax.optimization_barrier((value, self.ended[at]))
        self.next += self.step
        other = self.others.pop(0) if self.others else None
        if other is not None:
            value, _ = lax.optimization_barrier((value, other))
        return value


class Lanes:
    def __init__(self, x, y, z):
        self.ended = []
        self.lane_x, self.lane_y, self.lane_z = Lane(x), Lane(y), Lane(z)

    def note(self, moved):
        self.ended.append(moved)
        return moved

    def x(self, value):
        return self.note(self.lane_x(value, lambda v: swap(v, "tp", 1)))

    def y(self, value):
        return self.note(self.lane_y(value, lambda v: swap(v, "tp", 2)))

    def pull(self, value, k):
        return self.note(self.lane_z(value, lambda v: pull(v, k)))

    def push(self, value, k):
        return self.note(self.lane_z(value, lambda v: push(v, k)))


def add(left, right):
    return left.astype(F32) + right.astype(F32)


def add_low(left, right):
    return add(left, right).astype(BF)


def reduce_grid(lanes, main):
    if not is_ring():
        parts = main[0]
        along_x = swap(parts[1], "tp", 1)
        along_y = swap(add_low(parts[2], swap(parts[3], "tp", 1)), "tp", 2)
        both = add_low(add(parts[0], along_x), along_y)
        return lax.psum_scatter(both, "fsdp", scatter_dimension=0, tiled=True).astype(F32)
    far_2, far_1 = lanes.y(main[2][3]), None
    far_3 = lanes.x(main[3][3])
    y_2 = lanes.y(main[2][2])
    x_2 = lanes.x(add_low(main[2][1], far_2))
    far_1 = lanes.y(main[1][3])
    x_3 = lanes.x(main[3][1])
    y_3 = lanes.y(add_low(main[3][2], far_3))
    sum_2 = lanes.push(add_low(add(main[2][0], x_2), y_2), 1)
    y_1 = lanes.y(main[1][2])
    x_1 = lanes.x(add_low(main[1][1], far_1))
    far_0 = lanes.x(main[0][3])
    sum_3 = lanes.push(add_low(add(main[3][0], x_3), y_3), 3)
    x_0 = lanes.x(main[0][1])
    sum_1 = add(add(add(main[1][0], x_1), y_1), sum_2).astype(BF)
    sum_1 = lanes.push(sum_1, 1)
    y_0 = lanes.y(add_low(main[0][2], far_0))
    return add(add(add(main[0][0], x_0), y_0), sum_3) + sum_1.astype(F32)


def rows_of(table, start, count):
    pad = jnp.zeros((count,) + table.shape[1:], table.dtype)
    padded = jnp.concatenate([pad, table, pad], axis=0)
    return lax.dynamic_slice_in_dim(padded, jnp.clip(start + count, 0, table.shape[0] + count), count, 0)


class View:
    def __init__(self, array, width, index):
        self.array, self.width, self.index = array, width, index


def whole_block(dims):
    return pl.BlockSpec(dims, lambda i: (0,) * len(dims), pipeline_mode=pl.Buffered(1))


def call(body, outs, args, flops, scratch=()):
    flat, tree = jax.tree.flatten(args)
    arrays, specs, held = [], [], 0
    for leaf in flat:
        if isinstance(leaf, View):
            dims = (leaf.array.shape[0], leaf.width)
            at = leaf.index
            specs.append(
                pl.BlockSpec(dims, lambda i, at=at: (0, at), pipeline_mode=pl.Buffered(1))
            )
            arrays.append(leaf.array)
        else:
            dims = leaf.shape
            specs.append(whole_block(dims))
            arrays.append(leaf)
        held += math.prod(dims) * arrays[-1].dtype.itemsize
    held += sum(o.size * o.dtype.itemsize for o in outs)
    room = 2 * held + sum(4 * math.prod(a.shape) for a in scratch) + 8 * 1024 * 1024

    def kernel(*refs):
        body(*jax.tree.unflatten(tree, refs[: len(flat)]), *refs[len(flat) :])

    return pl.pallas_call(
        kernel,
        grid=(1,),
        out_shape=outs,
        in_specs=specs,
        out_specs=[whole_block(o.shape) for o in outs],
        scratch_shapes=list(scratch),
        compiler_params=pltpu.CompilerParams(vmem_limit_bytes=56 * 1024 * 1024),
        cost_estimate=pl.CostEstimate(flops=flops, bytes_accessed=held, transcendentals=0),
    )(*arrays)


def shape(rows, cols, dtype):
    return jax.ShapeDtypeStruct((rows, cols), dtype)


def down_rows(parts, k_t, start, stop):
    return jnp.concatenate([row[k_t][:, start:stop] for row in parts], axis=0)


def head_masks(half):
    at = lax.broadcasted_iota(jnp.int32, (1, half), 1) // HEAD_DIM
    return [at == h for h in range(half // HEAD_DIM)]


def softmax_rows(scores):
    top = jnp.max(scores, axis=-1, keepdims=True)
    grown = jnp.exp(scores - top)
    return grown / jnp.sum(grown, axis=-1, keepdims=True)


def merged(masks, values):
    total = values[-1]
    for mask, value in zip(masks[:-1], values[:-1]):
        total = jnp.where(mask, value, total)
    return total


def split_t(ref):
    width = ref.shape[0] // 4
    return [[ref.at[i * width : (i + 1) * width] for i in range(4)]]


def qkv_kernel(tok_count, half, own_ref, other_ref, weight_ref, bias_ref, qkv_ref, attended_ref):
    parts = split_t(weight_ref)
    rows = own_ref.shape[0]
    masks = head_masks(half)
    for i, ref in enumerate((own_ref, other_ref)):
        left = ref[...]
        for k_t in range(4):
            cols = slice(k_t * 3 * half, (k_t + 1) * 3 * half)
            weight = down_rows(parts, k_t, 0, 3 * half)
            qkv_ref[i * rows : (i + 1) * rows, cols] = (
                mm(left, weight) + bias_ref[:, cols]
            ).astype(BF)
    for k_t in range(4):
        at = k_t * 3 * half
        for row in range(0, 2 * rows, tok_count):
            here = slice(row, row + tok_count)
            query = qkv_ref[here, at : at + half]
            key = qkv_ref[here, at + half : at + 2 * half]
            value = qkv_ref[here, at + 2 * half : at + 3 * half]
            got = []
            for mask in masks:
                masked = jnp.where(mask, query, jnp.zeros_like(query))
                probs = softmax_rows(mm_nt(masked, key) * 0.125).astype(BF)
                got.append(mm(probs, value))
            attended_ref[here, k_t * half : (k_t + 1) * half] = merged(masks, got).astype(BF)


def attention_back_kernel(
    tok_count, half, own_ref, other_ref, weight_ref, qkv_ref, out_ref, sum_ref
):
    parts = split_t(weight_ref)
    rows = own_ref.shape[0]
    masks = head_masks(half)
    left = [ref[...] for ref in (own_ref, other_ref)]
    for k_t in range(4):
        at = k_t * 3 * half
        weight = down_rows(parts, k_t, 0, half)
        for i in range(2):
            grad_half = mm(left[i], weight).astype(BF)
            for row in range(0, rows, tok_count):
                here = slice(i * rows + row, i * rows + row + tok_count)
                grad = grad_half[row : row + tok_count]
                query = qkv_ref[here, at : at + half]
                key = qkv_ref[here, at + half : at + 2 * half]
                value = qkv_ref[here, at + 2 * half : at + 3 * half]
                grad_q, grad_k, grad_v = [], [], []
                for mask in masks:
                    zero = jnp.zeros_like(query)
                    probs = softmax_rows(mm_nt(jnp.where(mask, query, zero), key) * 0.125)
                    grad_p = mm_nt(jnp.where(mask, grad, zero), value)
                    grad_s = (
                        probs * (grad_p - jnp.sum(grad_p * probs, axis=-1, keepdims=True))
                    ).astype(BF)
                    grad_q.append(mm(grad_s, key))
                    grad_k.append(mm_tn(grad_s, query))
                    grad_v.append(mm_tn(probs.astype(BF), grad))
                out_ref[here, at : at + half] = (merged(masks, grad_q) * 0.125).astype(BF)
                out_ref[here, at + half : at + 2 * half] = (merged(masks, grad_k) * 0.125).astype(BF)
                out_ref[here, at + 2 * half : at + 3 * half] = merged(masks, grad_v).astype(BF)
        cols = slice(at, at + 3 * half)
        sum_ref[:, cols] = jnp.sum(out_ref[:, cols].astype(F32), axis=0, keepdims=True)


def features_kernel(left_ref, weight_ref, own_ref, other_ref):
    parts = split_t(weight_ref)
    rows, size = own_ref.shape
    block = size // 4
    for k in range(4):
        cols = slice(k * block, (k + 1) * block)
        weight = jnp.concatenate([p[cols, :] for p in parts[0]], axis=1)
        own_ref[:, cols] = mm_nt(left_ref[:rows], weight)
        other_ref[:, cols] = mm_nt(left_ref[rows:], weight)


def gelu_slope(values):
    scale = math.sqrt(2.0 / math.pi)
    bent = jnp.tanh(scale * (values + 0.044715 * (values * values * values)))
    inner = scale * (1.0 + 3.0 * 0.044715 * (values * values))
    return 0.5 * (1.0 + bent) + 0.5 * values * (1.0 - bent * bent) * inner


def mlp_kernel(own_ref, other_ref, up_ref, down_ref, bias_ref, pre_ref, act_ref, own_out, other_out):
    rows = own_ref.shape[0]

    @pl.when(pl.program_id(0) == 0)
    def _():
        own_out[...] = jnp.zeros_like(own_out)
        other_out[...] = jnp.zeros_like(other_out)

    for i, (ref, out) in enumerate(((own_ref, own_out), (other_ref, other_out))):
        here = slice(i * rows, (i + 1) * rows)
        pre = mm(ref[...], up_ref[...]) + bias_ref[...]
        pre_ref[here, :] = pre
        act = gelu_tanh(pre).astype(BF)
        act_ref[here, :] = act
        out[...] += mm_nt(act, down_ref[...])


def mlp_back_kernel(
    own_ref,
    other_ref,
    own_in,
    other_in,
    up_ref,
    down_ref,
    pre_ref,
    act_ref,
    grad_ref,
    sum_ref,
    own_out,
    other_out,
    flipped,
):
    rows, width = own_ref.shape
    size = up_ref.shape[1]

    @pl.when(pl.program_id(0) == 0)
    def _():
        own_out[...] = jnp.zeros_like(own_out)
        other_out[...] = jnp.zeros_like(other_out)
        for i, ref in enumerate((own_in, other_in, own_ref, other_ref)):
            flipped[
                i // 2 * width : (i // 2 + 1) * width, i % 2 * rows : (i % 2 + 1) * rows
            ] = ref[...].T

    total, grads = 0.0, []
    for i, (ref, out) in enumerate(((own_ref, own_out), (other_ref, other_out))):
        here = slice(i * rows, (i + 1) * rows)
        grad = (mm(ref[...], down_ref[...]) * gelu_slope(pre_ref[here, :])).astype(BF)
        total = total + col_sum(grad.astype(F32))
        out[...] += mm_nt(grad, up_ref[...])
        grads.append(grad)
    sum_ref[...] = total
    grad_ref[:, :size] = mm(flipped[:width, :], jnp.concatenate(grads, axis=0)).astype(BF)
    grad_ref[:, size:] = mm(flipped[width:, :], act_ref[...]).astype(BF)


def over_hidden(kernel, counts, outs, args, flops, scratch=()):
    def spec(block, index):
        return pl.BlockSpec(block, index)

    return pl.pallas_call(
        kernel,
        grid=(counts,),
        out_shape=[o[0] for o in outs],
        in_specs=[spec(a[1], a[2]) for a in args],
        out_specs=[spec(o[1], o[2]) for o in outs],
        scratch_shapes=list(scratch),
        compiler_params=pltpu.CompilerParams(vmem_limit_bytes=56 * 1024 * 1024),
        cost_estimate=pl.CostEstimate(
            flops=flops, bytes_accessed=32 * 1024 * 1024, transcendentals=0
        ),
    )(*[a[0] for a in args])


def piece_kernel(half, places, attn, grad_attn, grad_qkv_ref, attended_ref, *refs):
    outs, flipped = refs[:-1], refs[-1]
    t = lax.axis_index("tp")
    size = outs[0].shape[0]
    width = attn[0].shape[1]
    tokens = attn[0].shape[0]
    for i, pair in enumerate((attn, grad_attn)):
        for j, ref in enumerate(pair):
            flipped[i * width : (i + 1) * width, j * tokens : (j + 1) * tokens] = ref[...].T
    for i, k_f in enumerate(places):
        if size == width:
            start = 0
        else:
            start = pl.multiple_of(((lax.axis_index("fsdp") + k_f) & 3) * size, size)
        left = [flipped[pl.ds(i * width + start, size), :] for i in range(2)]
        for k_t in range(4):
            out = outs[i * 4 + k_t]
            place = t ^ k_t

            def cols(count):
                return pl.ds(pl.multiple_of(place * count, count), count)

            out[:, : 3 * half] = mm(left[0], grad_qkv_ref[:, cols(3 * half)]).astype(BF)
            out[:, 3 * half :] = mm(left[1], attended_ref[:, cols(half)]).astype(BF)


def normed(values):
    center = values - jnp.mean(values, axis=-1, keepdims=True)
    spread = jnp.mean(center * center, axis=-1, keepdims=True)
    inverse = lax.rsqrt(spread + 1e-06)
    return center * inverse, inverse


def norm_back(grad, norm, inverse):
    mean = jnp.mean(grad, axis=-1, keepdims=True)
    slope = jnp.mean(grad * norm, axis=-1, keepdims=True)
    return inverse * (grad - mean - norm * slope)


def col_sum(values):
    return jnp.sum(values, axis=0, keepdims=True)


def enter_kernel(images, patch_ref, w_ref, place_ref, mod_ref, resid_ref, attn_ref):
    count = patch_ref.shape[0] // images
    for i in range(images):
        here = slice(i * count, (i + 1) * count)
        resid = mm(patch_ref[here], w_ref[...]) + place_ref[...]
        resid_ref[here] = resid
        mod = mod_ref[i]
        attn_ref[here] = (normed(resid)[0] * (1.0 + mod[1:2]) + mod[0:1]).astype(BF)


def middle_kernel(images, own_ref, got_ref, bias_ref, resid_ref, mod_ref, out_ref, mid_ref, mlp_ref):
    count = own_ref.shape[0] // images
    for i in range(images):
        here = slice(i * count, (i + 1) * count)
        mod = mod_ref[i]
        out = own_ref[here] + got_ref[here] + bias_ref[...]
        out_ref[here] = out
        mid = resid_ref[here] + mod[2:3] * out
        mid_ref[here] = mid
        mlp_ref[here] = (normed(mid)[0] * (1.0 + mod[4:5]) + mod[3:4]).astype(BF)


def top_kernel(
    images,
    own_ref,
    got_ref,
    bias_ref,
    mid_ref,
    mod_ref,
    final_ref,
    head_ref,
    target_ref,
    resid_ref,
    mlp_ref,
    rows_ref,
    head_grad_ref,
    loss_ref,
    images_all,
):
    count = own_ref.shape[0] // images
    loss, head_grad = 0.0, 0.0
    for i in range(images):
        here = slice(i * count, (i + 1) * count)
        gate = mod_ref[i][5:6]
        shift, scale = final_ref[i][0:1], final_ref[i][1:2]
        out = own_ref[here] + got_ref[here] + bias_ref[...]
        norm, inverse = normed(mid_ref[here] + gate * out)
        head_in = (norm * (1.0 + scale) + shift).astype(BF)
        error = mm_nt(head_in, head_ref[...]) - target_ref[here]
        loss = loss + jnp.sum(col_sum(error * error), axis=1, keepdims=True) / images_all
        grad_pred = (2.0 / images_all * error).astype(BF)
        grad = mm(grad_pred, head_ref[...])
        head_grad = head_grad + mm_tn(grad_pred, head_in)
        resid = norm_back(grad * (1.0 + scale), norm, inverse)
        resid_ref[here] = resid
        mlp = (resid * gate).astype(BF)
        mlp_ref[here] = mlp
        rows_ref[i] = jnp.concatenate(
            [col_sum(grad), col_sum(grad * norm), col_sum(resid * out), col_sum(mlp.astype(F32))], axis=0
        )
    head_grad_ref[...] = head_grad
    loss_ref[...] = jnp.broadcast_to(loss, loss_ref.shape)


def middle_back_kernel(
    images, own_ref, got_ref, mid_ref, mod_ref, resid_ref, out_ref, new_ref, attn_ref, rows_ref
):
    count = own_ref.shape[0] // images
    for i in range(images):
        here = slice(i * count, (i + 1) * count)
        mod = mod_ref[i]
        grad = own_ref[here] + got_ref[here]
        norm, inverse = normed(mid_ref[here])
        resid = resid_ref[here] + norm_back(grad * (1.0 + mod[4:5]), norm, inverse)
        new_ref[here] = resid
        attn = (resid * mod[2:3]).astype(BF)
        attn_ref[here] = attn
        rows_ref[i] = jnp.concatenate(
            [
                col_sum(grad),
                col_sum(grad * norm),
                col_sum(resid * out_ref[here]),
                col_sum(attn.astype(F32)),
            ],
            axis=0,
        )


def enter_back_kernel(
    images, own_ref, got_ref, in_ref, mod_ref, resid_ref, patch_ref, rows_ref, patch_grad_ref
):
    count = own_ref.shape[0] // images
    patch_grad = 0.0
    for i in range(images):
        here = slice(i * count, (i + 1) * count)
        grad = own_ref[here] + got_ref[here]
        norm, inverse = normed(in_ref[here])
        resid = resid_ref[here] + norm_back(grad * (1.0 + mod_ref[i][1:2]), norm, inverse)
        low = resid.astype(BF)
        rows_ref[i] = jnp.concatenate(
            [col_sum(grad), col_sum(grad * norm), col_sum(low.astype(F32))], axis=0
        )
        patch_grad = patch_grad + mm_tn(patch_ref[here], low)
    patch_grad_ref[...] = patch_grad


def adam_kernel(clip_ref, w_ref, g_ref, m_ref, v_ref, new_ref, first_ref, second_ref):
    new_ref[...], first_ref[...], second_ref[...] = adam_update(
        w_ref[...], g_ref[...], m_ref[...], v_ref[...], clip_ref[0, 0]
    )


def adam_blocks(weight, gradient, first_mom, second_mom, clip_factor):
    rows, cols = weight.shape
    count = 4 if rows % 32 == 0 else 1
    block = pl.BlockSpec((rows // count, cols), lambda i: (i, 0))
    return pl.pallas_call(
        adam_kernel,
        grid=(count,),
        out_shape=[jax.ShapeDtypeStruct(weight.shape, F32)] * 3,
        in_specs=[pl.BlockSpec(memory_space=pltpu.SMEM)] + [block] * 4,
        out_specs=[block] * 3,
        compiler_params=pltpu.CompilerParams(vmem_limit_bytes=32 * 1024 * 1024),
        cost_estimate=pl.CostEstimate(flops=0, bytes_accessed=28 * weight.size, transcendentals=0),
    )(clip_factor.reshape(1, 1), weight, gradient, first_mom, second_mom)


def shards_kernel(half, first_ref, first_got, down_ref, down_got, mod_ref, block_ref, output_ref, square_ref):
    c = lax.axis_index("ctx")
    count = first_ref.shape[0]
    total = 0.0

    def joined(own_ref, got_ref, i):
        own, got = own_ref[:, i * half : (i + 1) * half], got_ref[:, i * half : (i + 1) * half]
        both = jnp.concatenate([jnp.where(c == 0, own, got), jnp.where(c == 0, got, own)], axis=1)
        return both, col_sum(both * both)

    for i in range(7):
        both, squares = joined(first_ref, first_got, i) if i < 3 else joined(down_ref, down_got, i - 3)
        block_ref[i * count : (i + 1) * count, :] = both
        total = total + squares
    for i in range(5):
        both, squares = joined(first_ref, first_got, 3) if i == 0 else joined(down_ref, down_got, i + 3)
        output_ref[i * 2 * half : (i + 1) * 2 * half, :] = both.T
        total = total + squares
    for i in range(6):
        part = mod_ref[:, i * 2 * half : (i + 1) * 2 * half]
        block_ref[(7 + i) * count : (8 + i) * count, :] = part
        total = total + col_sum(part * part)
    square_ref[...] = total


def on_device(
    latents,
    noise_sample,
    timesteps,
    class_labels,
    w_block,
    w_output,
    w_top,
    w_head,
    w_embed,
    biases,
    m_block,
    m_output,
    m_top,
    m_head,
    m_embed,
    m_biases,
    v_block,
    v_output,
    v_top,
    v_head,
    v_embed,
    v_biases,
):
    f, c, t = lax.axis_index("fsdp"), lax.axis_index("ctx"), lax.axis_index("tp")
    nt = lax.axis_size("tp")
    places = lax.axis_size("fsdp") * lax.axis_size("ctx")
    place = f * lax.axis_size("ctx") + c
    row_count, block_count, local_width = w_block.shape
    half = local_width // 2
    width = local_width * nt
    group_images = latents.shape[0]
    images_all = group_images * places
    img_count = group_images // nt
    grid_side = latents.shape[3] // 2
    tok_count = latents.shape[2] // 2 * grid_side
    embed_rows = w_embed.shape[0]
    top_cols = w_top.shape[1]

    block_low = jnp.transpose(w_block, (1, 0, 2)).astype(BF)
    output_low = jnp.transpose(w_output, (0, 2, 1)).astype(BF)
    top_low = w_top.astype(BF)
    embed_low = w_embed.astype(BF)

    def core_half(blocks):
        low, high = blocks[:, :, :half], blocks[:, :, half:]
        return jnp.where(c == 0, low, high), jnp.where(c == 0, high, low)

    def beside(blocks):
        return jnp.concatenate([blocks[i] for i in range(blocks.shape[0])], axis=1)

    mixed = jnp.concatenate(
        [block_low[0:3], output_low[0:1], block_low[3:7], output_low[1:5]], axis=0
    )
    mine, other = core_half(mixed)
    mine, other = beside(mine), swap(beside(other), "ctx", 1)
    shards = jnp.concatenate(
        [jnp.where(c == 0, mine, other), jnp.where(c == 0, other, mine)], axis=0
    )
    full = lax.all_gather(shards, ("tp", "fsdp"), axis=0, tiled=True)
    pace = free

    patch_rows = rows_of(embed_low, FREQ + CLASSES - embed_rows * t, PATCH_ROWS)
    ids = jnp.concatenate([timesteps, class_labels]).astype(F32)
    ids = jnp.concatenate([ids, jnp.zeros((row_count - 2 * group_images % row_count,), F32)])[None]
    ids = ids.reshape(-1, row_count)
    small = jnp.concatenate([ids, patch_rows.astype(F32), w_head.T.astype(BF).astype(F32)], axis=0)
    small = gather_fc(small, pace)
    ids_all = small[:, : ids.shape[0]].reshape(places, -1)
    steps_all = ids_all[:, :group_images].reshape(images_all)
    labels_all = ids_all[:, group_images : 2 * group_images].reshape(images_all).astype(jnp.int32)
    small = small[:, ids.shape[0] :].transpose(1, 0, 2).reshape(2 * PATCH_ROWS, width)
    patch_part, w_head_t = small[:PATCH_ROWS], small[PATCH_ROWS:].astype(BF)
    embed_at = embed_rows * t + jnp.arange(embed_rows, dtype=jnp.int32)
    half_freq = FREQ // 2
    rates = jnp.exp(-math.log(10000.0) * (embed_at % half_freq).astype(F32) / half_freq)
    angles = steps_all[:, None] * rates[None, :]
    waves = jnp.where(embed_at[None, :] < half_freq, jnp.cos(angles), jnp.sin(angles))
    freq_low = jnp.where(embed_at[None, :] < FREQ, waves, 0.0).astype(BF)
    one_hot = (labels_all[:, None] + FREQ == embed_at[None, :]).astype(BF)
    own_cols = lambda row: lax.dynamic_slice_in_dim(row, place * row_count, row_count, 0)
    over_tp = jnp.concatenate([mm(freq_low, embed_low), patch_part.reshape(-1, row_count)], axis=0)
    over_tp = sum_over(over_tp, ("tp",), pace)
    t_pre = over_tp[:images_all] + own_cols(biases[1])
    w_patch = over_tp[images_all:].reshape(PATCH_ROWS, width).astype(BF)
    t_hidden = jax.nn.silu(t_pre).astype(BF)
    table_part = mm(one_hot, embed_low)
    top_at = top_cols * t + jnp.arange(top_cols, dtype=jnp.int32)
    cond_cols = mm(t_hidden, top_low)
    cond_cols = jnp.where(top_at[None, :] < width, cond_cols, 0.0)
    cond_wide = jnp.concatenate(
        [jnp.zeros((images_all, width), F32), cond_cols, jnp.zeros((images_all, width), F32)], axis=1
    )
    cond_wide = lax.dynamic_slice_in_dim(
        cond_wide, jnp.clip(width - top_cols * t, 0, width + top_cols), width, 1
    )
    cond_blocks = cond_wide.reshape(images_all, places, row_count).transpose(1, 0, 2)
    cond = sum_over(scatter_fc(cond_blocks, pace) + table_part, ("tp",), pace) + own_cols(biases[2])
    cond_low = jax.nn.silu(cond).astype(BF)
    mod_low = block_low[7:13]
    mod_cols = jnp.concatenate([mm(cond_low, mod_low[j]) for j in range(6)], axis=1)
    final_cols = jnp.where(top_at[None, :] < width, 0.0, mm(cond_low, top_low))
    all_cols = jnp.concatenate([mod_cols, final_cols], axis=1)
    group_cols = scatter_fc(all_cols.reshape(places, group_images, all_cols.shape[1]), pace)
    own_parts = exchange_tp(group_cols.reshape(nt, img_count, -1), pace)
    mod_width = 6 * local_width
    modulation = (
        own_parts[:, :, :mod_width]
        .reshape(nt, img_count, 6, local_width)
        .transpose(1, 2, 0, 3)
        .reshape(img_count, 6, width)
    ) + biases[3:9][None]
    final_mod = own_parts[:, :, mod_width:].transpose(1, 0, 2).reshape(img_count, 3 * width)
    final_mod = final_mod[:, width:].reshape(img_count, 2, width) + biases[17:19][None]
    shift_f, scale_f = final_mod[:, 0], final_mod[:, 1]

    def own_images(values):
        return lax.dynamic_slice_in_dim(values, t * img_count, img_count, 0)

    latent_vals = own_images(latents).astype(F32)
    noise_vals = own_images(noise_sample).astype(F32)
    keep_rate, drop_rate = plan(own_images(timesteps))
    noisy = (
        keep_rate[:, None, None, None] * latent_vals + drop_rate[:, None, None, None] * noise_vals
    )
    patches = patchify(noisy).astype(BF)
    target = patchify(noise_vals)

    quarter = width // 4
    pos_rates = jnp.exp(-math.log(10000.0) * jnp.arange(quarter, dtype=F32) / quarter)
    side_angle = jnp.arange(grid_side, dtype=F32)[:, None] * pos_rates[None, :]
    side = jnp.concatenate([jnp.sin(side_angle), jnp.cos(side_angle)], axis=-1)
    rows_side = jnp.broadcast_to(side[:, None, :], (tok_count // grid_side, grid_side, 2 * quarter))
    cols_side = jnp.broadcast_to(side[None, :, :], (tok_count // grid_side, grid_side, 2 * quarter))
    positions = jnp.concatenate([rows_side, cols_side], axis=-1).reshape(tok_count, width)

    bias_width = jnp.stack([biases[0], biases[11], biases[16]])

    def heads_bias(rows):
        shaped = rows.reshape(-1, nt, 2, half)
        return jnp.where(c == 0, shaped[:, :, 0], shaped[:, :, 1]).transpose(1, 0, 2)

    bias_qv = heads_bias(biases[9:11])
    bias_qkv = jnp.stack([bias_qv[:, 0], jnp.zeros_like(bias_qv[:, 0]), bias_qv[:, 1]], axis=1).reshape(-1)
    bias_up = heads_bias(biases[12:16]).reshape(-1)
    qkv_view, proj_view = View(full, 3 * half, 0), View(full, half, 3)

    own_count = img_count * tok_count
    core_width = nt * half
    matrix_flops = 4 * own_count * width * half

    two_sums = [shape(own_count, width, F32)] * 2

    def run(body, outs, blocks, *args):
        return call(body, outs, args, blocks * nt * matrix_flops)

    def small_run(body, outs, *args):
        return call(functools.partial(body, img_count), outs, args, 0)

    def cube(rows):
        return jax.ShapeDtypeStruct((img_count, rows, width), F32)

    flat_f32, flat_low = shape(own_count, width, F32), shape(own_count, width, BF)

    patches = patches.reshape(own_count, PATCH_ROWS)
    resid_in, attn_own = small_run(
        enter_kernel,
        [flat_f32, flat_low],
        patches,
        w_patch,
        positions + bias_width[0],
        modulation,
    )
    attn_other = swap(attn_own, "ctx", 1)
    qkv_low, attended = run(
        functools.partial(qkv_kernel, tok_count, half),
        [shape(2 * own_count, 3 * core_width, BF), shape(2 * own_count, core_width, BF)],
        4,
        attn_own,
        attn_other,
        qkv_view,
        bias_qkv[None],
    )
    own, other = run(features_kernel, two_sums, 1, attended, proj_view)
    attn_out, resid_mid, mlp_own = small_run(
        middle_kernel,
        [flat_f32, flat_f32, flat_low],
        own,
        swap(other, "ctx", 1),
        bias_width[1:2],
        resid_in,
        modulation,
    )
    mlp_other = swap(mlp_own, "ctx", 1)
    hidden = 4 * half
    fixed = lambda i: (0, 0)
    column = lambda i: (0, i)
    wide_rows = (own_count, width)
    up_pre, up_act, own, other = over_hidden(
        mlp_kernel,
        nt,
        [
            (shape(2 * own_count, nt * hidden, F32), (2 * own_count, hidden), column),
            (shape(2 * own_count, nt * hidden, BF), (2 * own_count, hidden), column),
            (flat_f32, wide_rows, fixed),
            (flat_f32, wide_rows, fixed),
        ],
        [
            (mlp_own, wide_rows, fixed),
            (mlp_other, wide_rows, fixed),
            (full, (width, hidden), lambda i: (i, 1)),
            (full, (width, hidden), lambda i: (i, 2)),
            (bias_up[None], (1, hidden), column),
        ],
        8 * nt * matrix_flops,
    )
    grad_resid, grad_mlp, top_rows_grad, grad_head, loss_part = small_run(
        functools.partial(top_kernel, images_all=images_all),
        [flat_f32, flat_low, cube(4), shape(PATCH_ROWS, width, F32), shape(1, 128, F32)],
        own,
        swap(other, "ctx", 1),
        bias_width[2:3],
        resid_mid,
        modulation,
        final_mod,
        w_head_t,
        target.reshape(own_count, PATCH_ROWS),
    )
    loss_part = loss_part[0, 0]

    grad_mlp_other = swap(grad_mlp, "ctx", 1)
    grad_hidden_w, grad_b_up, own, other = over_hidden(
        mlp_back_kernel,
        nt,
        [
            (shape(nt * width, 2 * hidden, BF), (width, 2 * hidden), lambda i: (i, 0)),
            (shape(1, nt * hidden, F32), (1, hidden), column),
            (flat_f32, wide_rows, fixed),
            (flat_f32, wide_rows, fixed),
        ],
        [
            (grad_mlp, wide_rows, fixed),
            (grad_mlp_other, wide_rows, fixed),
            (mlp_own, wide_rows, fixed),
            (mlp_other, wide_rows, fixed),
            (full, (width, hidden), lambda i: (i, 1)),
            (full, (width, hidden), lambda i: (i, 2)),
            (up_pre, (2 * own_count, hidden), column),
            (up_act, (2 * own_count, hidden), column),
        ],
        16 * nt * matrix_flops,
        [pltpu.VMEM((2 * width, 2 * own_count), BF)],
    )
    grad_b_up = grad_b_up[0]
    lanes = Lanes(2, 2, 1)
    count = 4 if is_ring() else 1
    block_rows = width // count
    hidden_pieces = [
        [
            lax.dynamic_slice_in_dim(
                grad_hidden_w, (t ^ k_t) * width + ((f + k_f) & (count - 1)) * block_rows, block_rows, 0
            )
            for k_t in range(4)
        ]
        for k_f in range(count)
    ]
    hidden_sum = reduce_grid(lanes, hidden_pieces)

    def pin(value, at):
        if lanes.ended and at is not None:
            value, _ = lax.optimization_barrier((value, lanes.ended[at]))
        return value

    own = pin(own, PINS[0])
    grad_resid, grad_attn, middle_rows = small_run(
        middle_back_kernel,
        [flat_f32, flat_low, cube(4)],
        own,
        swap(other, "ctx", 1),
        resid_mid,
        modulation,
        grad_resid,
        attn_out,
    )
    grad_attn_other = swap(grad_attn, "ctx", 1)
    grad_qkv, grad_b_qkv = run(
        functools.partial(attention_back_kernel, tok_count, half),
        [shape(2 * own_count, 3 * core_width, BF), shape(1, 3 * core_width, F32)],
        2,
        pin(grad_attn, PINS[1]),
        grad_attn_other,
        proj_view,
        qkv_low,
    )
    grad_b_qkv = grad_b_qkv[0]
    lists = [(2, 3), (1, 0)] if is_ring() else [(0,)]
    pieces = [None] * (4 if is_ring() else 1)
    piece_size = shape(width // len(pieces), 4 * half, BF)
    for at, distances in enumerate(lists):
        made = call(
            functools.partial(piece_kernel, half, distances),
            [piece_size] * (4 * len(distances)),
            (
                (attn_own, attn_other),
                (grad_attn, grad_attn_other),
                pin(grad_qkv, PINS[2 + at]),
                attended,
            ),
            4 * nt * matrix_flops // len(lists),
            [pltpu.VMEM((2 * width, 2 * own_count), BF)],
        )
        for i, k_f in enumerate(distances):
            pieces[k_f] = made[4 * i : 4 * i + 4]
    first_sum = reduce_grid(lanes, pieces)
    grad_qkv, _ = lax.optimization_barrier((grad_qkv, pieces[0][0]))
    grad_qkv = pin(grad_qkv, PINS[4])
    own, other = run(features_kernel, two_sums, 3, grad_qkv, qkv_view)
    enter_rows, grad_patch = small_run(
        enter_back_kernel,
        [cube(3), shape(PATCH_ROWS, width, F32)],
        own,
        swap(other, "ctx", 1),
        resid_in,
        modulation,
        grad_resid,
        patches,
    )
    grad_b_patch = jnp.sum(enter_rows[:, 2], axis=0)
    grad_b_proj = jnp.sum(middle_rows[:, 3], axis=0)
    grad_b_down = jnp.sum(top_rows_grad[:, 3], axis=0)

    grad_mod = jnp.concatenate(
        [enter_rows[:, 0:2], middle_rows[:, 2:3], middle_rows[:, 0:2], top_rows_grad[:, 2:3]], axis=1
    )
    grad_final = top_rows_grad[:, 0:2]
    def heads_place(grad_rows):
        rows = grad_rows.transpose(1, 0, 2)
        empty = jnp.zeros_like(rows)
        return jnp.stack(
            [jnp.where(c == 0, rows, empty), jnp.where(c == 0, empty, rows)], axis=2
        ).reshape(-1, width)

    qkv_rows = grad_b_qkv.reshape(nt, 3, half)
    up_rows = heads_place(grad_b_up.reshape(nt, 4, half))
    width_rows = (
        jnp.concatenate(
            [grad_b_patch[None], grad_b_proj[None], grad_b_down[None], grad_patch, grad_head], axis=0
        )
    )
    loss_row = jnp.broadcast_to(loss_part, (1, width))
    payload = jnp.concatenate(
        [
            width_rows[0:1],
            loss_row,
            jnp.zeros((1, width), F32),
            jnp.sum(grad_mod, axis=0),
            heads_place(jnp.stack([qkv_rows[:, 0], qkv_rows[:, 2]], axis=1)),
            width_rows[1:2],
            up_rows,
            width_rows[2:3],
            jnp.sum(grad_final, axis=0),
            width_rows[3:],
        ],
        axis=0,
    )
    steps = []
    payload = sum_slow(payload, ("ctx", "tp", "fsdp"), Pace(lanes, *BIASES), steps)
    chain = Pace(lanes, *CHAIN, [None, None] + steps)
    final_flat = jnp.concatenate(
        [jnp.zeros((img_count, width), F32), grad_final.reshape(img_count, 2 * width)], axis=1
    )
    to_tp = jnp.concatenate(
        [
            grad_mod.reshape(img_count, 6, nt, local_width)
            .transpose(2, 0, 1, 3)
            .reshape(nt, img_count, mod_width),
            final_flat.reshape(img_count, nt, top_cols).transpose(1, 0, 2),
        ],
        axis=-1,
    )
    group_grad = exchange_tp(to_tp, chain).reshape(group_images, -1)
    all_grad = gather_fc(group_grad, chain).reshape(images_all, -1)
    all_mod, all_final = all_grad[:, :mod_width], all_grad[:, mod_width:]
    cond_rows = cond_low.astype(F32)
    grad_w_mod = exact_dot(cond_rows.T, all_mod)
    mod_flat = mod_low.astype(F32).transpose(1, 0, 2).reshape(row_count, mod_width)
    top_rows = top_low.astype(F32)
    grad_cond_act = sum_over(
        exact_dot(all_mod, mod_flat.T) + exact_dot(all_final, top_rows.T), ("tp",), chain
    )
    grad_cond = jax.vjp(jax.nn.silu, cond)[1](grad_cond_act)[0]
    cond_all = gather_fc(grad_cond, chain).transpose(1, 0, 2).reshape(images_all, width)
    grad_b_cond = jnp.sum(cond_all, axis=0)
    cond_padded = jnp.concatenate([cond_all, jnp.zeros((images_all, 2 * width), F32)], axis=1)
    cond_top = lax.dynamic_slice_in_dim(cond_padded, top_cols * t, top_cols, 1)
    top_grad = exact_dot(cond_rows.T, all_final) + exact_dot(t_hidden.astype(F32).T, cond_top)
    grad_hidden = sum_over(exact_dot(cond_top, top_rows.T), ("tp",), chain)
    grad_t_pre = jax.vjp(jax.nn.silu, t_pre)[1](grad_hidden)[0]

    loss_total = payload[1, 0]
    small_sum = lax.dynamic_slice_in_dim(payload[19:], place * row_count, row_count, 1)
    patch_sum, head_sum = small_sum[:PATCH_ROWS], small_sum[PATCH_ROWS:]
    head_grad_sum = head_sum.T

    def from_cores(total):
        low, high = total[:row_count], total[row_count:]
        return jnp.where(c == 0, low, high), swap(jnp.where(c == 0, high, low), "ctx", 1)

    block_sum, output_sum, shard_squares = call(
        functools.partial(shards_kernel, half),
        [
            shape(block_count * row_count, local_width, F32),
            shape(5 * local_width, row_count, F32),
            shape(1, local_width, F32),
        ],
        from_cores(first_sum) + from_cores(hidden_sum) + (grad_w_mod,),
        0,
    )
    embed_sum = exact_dot(one_hot.astype(F32).T, grad_cond) + exact_dot(
        freq_low.astype(F32).T, grad_t_pre
    )
    patch_padded = jnp.concatenate(
        [jnp.zeros((embed_rows, row_count), F32), patch_sum, jnp.zeros((embed_rows, row_count), F32)],
        axis=0,
    )
    patch_start = embed_rows * t + embed_rows - (FREQ + CLASSES)
    embed_sum = embed_sum + lax.dynamic_slice_in_dim(
        patch_padded, jnp.clip(patch_start, 0, embed_rows + PATCH_ROWS), embed_rows, 0
    )

    head_squares = jnp.where(t == 0, jnp.sum(head_grad_sum * head_grad_sum), 0.0)
    shard_squares = (
        jnp.sum(shard_squares)
        + jnp.sum(embed_sum * embed_sum)
        + jnp.sum(top_grad * top_grad)
        + head_squares
    )
    b1_part = jnp.where(t == 0, jnp.sum(grad_t_pre, axis=0), 0.0)
    b1_row = lax.dynamic_update_slice_in_dim(jnp.zeros((width,), F32), b1_part, place * row_count, 0)
    last = jnp.concatenate([b1_row, jnp.broadcast_to(shard_squares, (128,))])
    last = sum_over(last, ("ctx", "tp", "fsdp"))
    bias_sum = jnp.concatenate(
        [payload[0:1], last[None, :width], grad_b_cond[None], payload[3:19]], axis=0
    )
    grad_norm = jnp.sqrt(last[width] + jnp.sum(bias_sum * bias_sum))
    clip_factor = jnp.minimum(1.0, 1.0 / (grad_norm + 1e-06))
    def tall(values):
        return jnp.transpose(values, (1, 0, 2)).reshape(block_count * row_count, local_width)

    upd_block = [
        jnp.transpose(u.reshape(block_count, row_count, local_width), (1, 0, 2))
        for u in adam_blocks(tall(w_block), block_sum, tall(m_block), tall(v_block), clip_factor)
    ]
    upd_output = [
        u.reshape(w_output.shape)
        for u in adam_blocks(
            *[m.reshape(output_sum.shape) if m.ndim == 3 else m for m in (w_output, output_sum, m_output, v_output)],
            clip_factor,
        )
    ]
    upd_top = adam_update(w_top, top_grad, m_top, v_top, clip_factor)
    upd_head = adam_update(w_head, head_grad_sum, m_head, v_head, clip_factor)
    upd_embed = adam_update(w_embed, embed_sum, m_embed, v_embed, clip_factor)
    upd_biases = adam_update(biases, bias_sum, m_biases, v_biases, clip_factor)
    updates = (upd_block, upd_output, upd_top, upd_head, upd_embed, upd_biases)
    return (
        (loss_total, grad_norm)
        + tuple(u[0] for u in updates)
        + tuple(u[1] for u in updates)
        + tuple(u[2] for u in updates)
        + (bias_sum * clip_factor,)
    )


def solution(mesh):
    both = ("fsdp", "ctx")
    weights = (
        P(both, None, "tp"),
        P(None, "tp", both),
        P(both, "tp"),
        P(both, None),
        P("tp", both),
        P(),
    )
    images = (P(both, None, None, None), P(both, None, None, None), P(both), P(both))
    return jax.shard_map(
        on_device,
        mesh=mesh,
        in_specs=images + weights * 3,
        out_specs=(P(), P()) + weights * 3 + (P(),),
        check_vma=False,
    )
```

time: 529 us -> 488 us (0.922)
  Pallas kernels: 37.9 us -> 95.7 us
  local copies, waits for them, and re-layouts: 70.5 us -> 28.7 us
  matrix products: 46.1 us -> 8.26 us
  other arithmetic: 76.1 us -> 43.3 us
  starting transfers between devices: 67.8 us -> 97.6 us
  waiting for transfers between devices: 199 us -> 187 us
    ppermute x74 -> x70, waiting for transfers between devices: 143 us -> 73.2 us  [swap(): return lax.ppermute(value, axis, [(i, i ^ mask) for i in range(count)])]
    all_gather x1, waiting for transfers between devices: 28 us -> 89.1 us  [on_device(): full = lax.all_gather(shards, ('tp', 'fsdp'), axis=0, tiled=True)]
    pallas_call x8 -> x16, Pallas kernels: 37.9 us -> 95.7 us  [the longest x12 62.9 us: call(): pl.pallas_call(kernel, grid=(1,), out_shape=outs, in_specs=specs, out_spe...]
    unnamed x433 -> x127, local copies, waits for them, and re-layouts: 41.3 us -> 11.4 us
    dot_general x21 -> x0, matrix products: 28.4 us -> none  [the longest x16 23.9 us: mm_tn(): lax.dot_general(left, right, (((0,), (0,)), ((), ())), preferred_element_...]
    ppermute x3 -> x9, waiting for transfers between devices: 20.4 us -> 2.69 us  [pull(): lax.ppermute(value, 'fsdp', [((i + k) % count, i) for i in range(count)])]
    reduce_sum x15 -> x1, other arithmetic: 16.3 us -> 1.29 us  [on_device(): jnp.sum(shard_squares) + jnp.sum(embed_sum * embed_sum)]
    ppermute x3 -> x12, waiting for transfers between devices: 7.19 us -> 22 us  [push(): lax.ppermute(value, 'fsdp', [(i, (i + k) % count) for i in range(count)])]
  transfers between devices with their start and end apart: 82 -> 92, of which waited for: 43 -> 42; matrix products, arithmetic and copies ran while one was open for 23% -> 11% of each run, Pallas kernels for 6% -> 9%
where the time goes in v2:
time: 488 us; the launch traced here: 483 us
  waiting for transfers between devices  187 us (38%)
  starting transfers between devices  97.6 us (20%)
  Pallas kernels  95.7 us (20%)
  other arithmetic  43.3 us (9%)
  local copies, waits for them, and re-layouts  28.7 us (6%)
  between operations  22.1 us (5%)
  matrix products  8.26 us (2%)
    all_gather x1, waiting for transfers between devices, on_device(): full = lax.all_gather(shards, ('tp', 'fsdp'), axis=0, tiled=True)  89.1 us
    ppermute x70, waiting for transfers between devices, swap(): return lax.ppermute(value, axis, [(i, i ^ mask) for i in range(count)])  73.2 us
    ppermute x70, starting transfers between devices, swap(): return lax.ppermute(value, axis, [(i, i ^ mask) for i in range(count)])  65 us
    pallas_call x12, Pallas kernels, call(): pl.pallas_call(kernel, grid=(1,), out_shape=outs, in_specs=specs, out_spe...  62.9 us
    pallas_call x2, Pallas kernels, over_hidden(): pl.pallas_call(kernel, grid=(counts,), out_shape=[o[0] for o in outs], in...  27.6 us
    ppermute x12, waiting for transfers between devices, push(): lax.ppermute(value, 'fsdp', [(i, (i + k) % count) for i in range(count)])  22 us
    ppermute x12, starting transfers between devices, push(): lax.ppermute(value, 'fsdp', [(i, (i + k) % count) for i in range(count)])  17.7 us
    convert_element_type x9, other arithmetic, add_low(): return add(left, right).astype(BF)  15.9 us
  transfers between devices with their start and end apart: 92, of which 42 were waited for; matrix products, arithmetic and copies ran while one was open for 11% of the time, Pallas kernels for 9%

profile of v2, /device:TPU:0, one launch (start us, length us, event | category | flops | bytes accessed | tf_op | source)
XLA Modules:
  0.0 482.6 jit_solution(5923829867570928846)
XLA Ops:
  13.7 3.0 collective-permute-start.2
  28.7 4.2 collective-permute-done.5
  38.6 3.3 collective-permute-start.10
  43.6 4.1 collective-permute-done.9
  63.0 3.7 collective-permute-done.16
  82.7 89.1 %all-gather.2.cloned.1.call-done.refs_2_.refs_1_.up_ref.down_ref = bf16[4096,1536]{1,0:T(8,128)(2,1)} async-done(((bf16[256,1536]{1,0:T(8,128)(2,1)}), bf16[4096,1536]{1,0:T(8,128)(2,1)}) %all-gather.2.cloned.1.call-update) | async-done | bytes 12582928 | tf_op jit(solution)/shard_map/all_gather | solution.py:750
  171.8 7.3 %shard_map.374 = (bf16[512,1536]{1,0:T(8,128)(2,1)}, bf16[512,512]{1,0:T(8,128)(2,1)}) custom-call(bf16[256,1024]{1,0:T(8,128)(2,1)} %get-tuple-element.124.refs_0_, bf16[256,1024]{1,0:T(8,128)(2,1)} %copy-done.8, bf16[4096,1536]{1,0:T(8,128)(2,1)} %all-gather.2.cloned.1.call-done.refs_2_.refs_1_.up_ref.down_ref, f32[1,1536]{1,0:T(1,128)} %broadcast_in_dim_reshape.7.refs_3_), custom_call_target="tpu_custom_call" | custom-call | flops 2147483648 | bytes 6297600 | tf_op jit(solution)/shard_map/pallas_call | solution.py:298
  179.1 3.5 shard_map.375
  186.5 3.6 shard_map.376
  193.0 10.9 %shard_map.377 = (f32[512,2048]{1,0:T(8,128)}, bf16[512,2048]{1,0:T(8,128)(2,1)}, f32[256,1024]{1,0:T(8,128)}, f32[256,1024]{1,0:T(8,128)}) custom-call(bf16[256,1024]{1,0:T(8,128)(2,1)} %get-tuple-element.129.own_ref.own_in, bf16[256,1024]{1,0:T(8,128)(2,1)} %copy-done.10, bf16[4096,1536]{1,0:T(8,128)(2,1)} %all-gather.2.cloned.1.call-done.refs_2_.refs_1_.up_ref.down_ref, ...), custom_call_target="tpu_custom_call" | custom-call | flops 4294967296 | bytes 33554432 | tf_op jit(solution)/shard_map/pallas_call | solution.py:482
  207.9 4.6 shard_map.378
  215.3 16.7 %shard_map.379 = (bf16[4096,1024]{1,0:T(8,128)(2,1)}, f32[1,2048]{1,0:T(1,128)}, f32[256,1024]{1,0:T(8,128)}, f32[256,1024]{1,0:T(8,128)}) custom-call(bf16[256,1024]{1,0:T(8,128)(2,1)} %get-tuple-element.133.own_ref, bf16[256,1024]{1,0:T(8,128)(2,1)} %copy-done.18, bf16[256,1024]{1,0:T(8,128)(2,1)} %get-tuple-element.129.own_ref.own_in, ...), custom_call_target="tpu_custom_call" | custom-call | flops 8589934592 | bytes 33554432 | tf_op jit(solution)/shard_map/pallas_call | solution.py:482
  232.1 4.0 constant_dynamic-slice_fusion
  238.1 11.9 %collective-permute-done.30 = bf16[256,1024]{1,0:T(8,128)(2,1)S(1)} collective-permute-done((bf16[256,1024]{1,0:T(8,128)(2,1)S(1)}, bf16[256,1024]{1,0:T(8,128)(2,1)S(1)}, u32[]{:S(2)}, u32[]{:S(2)}) %collective-permute-start.30) | collective-permute-done | bytes 524320 | tf_op jit(solution)/shard_map/ppermute | solution.py:71
  254.1 11.1 %collective-permute-done.31 = bf16[256,1024]{1,0:T(8,128)(2,1)} collective-permute-done((bf16[256,1024]{1,0:T(8,128)(2,1)}, bf16[256,1024]{1,0:T(8,128)(2,1)}, u32[]{:S(2)}, u32[]{:S(2)}) %collective-permute-start.31) | collective-permute-done | bytes 524320 | tf_op jit(solution)/shard_map/ppermute | solution.py:71
  265.2 3.3 add_convert_fusion.2
  271.0 4.6 shard_map.380
  283.5 13.3 %shard_map.381 = (bf16[512,1536]{1,0:T(8,128)(2,1)}, f32[1,1536]{1,0:T(1,128)}) custom-call(bf16[256,1024]{1,0:T(8,128)(2,1)} %get-tuple-element.142.refs_0_.refs_2_, bf16[256,1024]{1,0:T(8,128)(2,1)} %copy-done.9, bf16[4096,1536]{1,0:T(8,128)(2,1)} %all-gather.2.cloned.1.call-done.refs_2_.refs_1_.up_ref.down_ref, bf16[512,1536]{1,0:T(8,128)(2,1)} %get-tuple-element.143.refs_3_), custom_call_target="tpu_custom_call" | custom-call | flops 1073741824 | bytes 5249024 | tf_op jit(solution)/shard_map/pallas_call | solution.py:298
  297.5 5.2 %shard_map.385 = (bf16[256,512]{1,0:T(8,128)(2,1)}, bf16[256,512]{1,0:T(8,128)(2,1)}, bf16[256,512]{1,0:T(8,128)(2,1)}, bf16[256,512]{1,0:T(8,128)(2,1)}, bf16[2...) custom-call(bf16[256,1024]{1,0:T(8,128)(2,1)} %get-tuple-element.124.refs_0_, ...), custom_call_target="tpu_custom_call" | custom-call | flops 1073741824 | bytes 6291456 | tf_op jit(solution)/shard_map/pallas_call | solution.py:298
  304.9 4.4 add_convert_fusion
  309.9 5.4 %shard_map.382 = (bf16[256,512]{1,0:T(8,128)(2,1)}, bf16[256,512]{1,0:T(8,128)(2,1)}, bf16[256,512]{1,0:T(8,128)(2,1)}, bf16[256,512]{1,0:T(8,128)(2,1)}, bf16[2...) custom-call(bf16[256,1024]{1,0:T(8,128)(2,1)} %get-tuple-element.124.refs_0_, ...), custom_call_target="tpu_custom_call" | custom-call | flops 1073741824 | bytes 6291456 | tf_op jit(solution)/shard_map/pallas_call | solution.py:298
  319.0 5.6 %shard_map.383 = (f32[256,1024]{1,0:T(8,128)}, f32[256,1024]{1,0:T(8,128)}) custom-call(bf16[512,1536]{1,0:T(8,128)(2,1)} %get-tuple-element.166.refs_4_.refs_0_, bf16[4096,1536]{1,0:T(8,128)(2,1)} %all-gather.2.cloned.1.call-done.refs_2_.refs_1_.up_ref.down_ref), custom_call_target="tpu_custom_call" | custom-call | flops 1610612736 | bytes 6815744 | tf_op jit(solution)/shard_map/pallas_call | solution.py:298
  326.4 3.2 collective-permute-start.69
  331.2 3.0 collective-permute-done.49
  348.9 3.8 shard_map.384
  354.4 3.3 collective-permute-done.70
  376.3 4.5 collective-permute-done.71
  392.9 4.5 collective-permute-done.45
  398.0 3.5 collective-permute-start.64
  419.1 9.0 %collective-permute-done.51 = f32[51,1024]{1,0:T(8,128)S(1)} collective-permute-done((f32[51,1024]{1,0:T(8,128)S(1)}, f32[51,1024]{1,0:T(8,128)S(1)}, u32[]{:S(2)}, u32[]{:S(2)}) %collective-permute-start.51) | collective-permute-done | bytes 208928 | tf_op jit(solution)/shard_map/ppermute | solution.py:71
  434.5 3.4 shard_map.386
  471.1 3.3 shard_map.387
  (518 shorter events, 196.2 us)
Async XLA Ops:
  7.2 164.6 %all-gather.2.cloned.1.call-start = ((), (), s32[]{:S(2)}) async-start(), calls=%async_computation | async-start | bytes 13369344 | tf_op jit(solution)/shard_map/all_gather | solution.py:750
  236.1 14.0 %collective-permute-start.30 = (bf16[256,1024]{1,0:T(8,128)(2,1)S(1)}, bf16[256,1024]{1,0:T(8,128)(2,1)S(1)}, u32[]{:S(2)}, u32[]{:S(2)}) collective-permute-start(bf16[256,1024]{1,0:T(8,128)(2,1)S(1)} %get-tuple-element.255), channel_id=1, source_target_pairs={{0,2},{1,3},{2,0},{3,1},{4,6},{5,7},{6,4},{7,5},{8,10},{9,11},{10,... | collective-permute-start | bytes 1572872 | tf_op jit(solution)/shard_map/ppermute | solution.py:71
  237.5 15.1 %collective-permute-start.28 = (bf16[256,1024]{1,0:T(8,128)(2,1)}, bf16[256,1024]{1,0:T(8,128)(2,1)}, u32[]{:S(2)}, u32[]{:S(2)}) collective-permute-start(bf16[256,1024]{1,0:T(8,128)(2,1)} %get-tuple-element.257), channel_id=1, source_target_pairs={{0,1},{1,0},{2,3},{3,2},{4,5},{5,4},{6,7},{7,6},{8,9},{9,8},{10,11... | collective-permute-start | bytes 1572872 | tf_op jit(solution)/shard_map/ppermute | solution.py:71
  250.0 15.2 %collective-permute-start.31 = (bf16[256,1024]{1,0:T(8,128)(2,1)}, bf16[256,1024]{1,0:T(8,128)(2,1)}, u32[]{:S(2)}, u32[]{:S(2)}) collective-permute-start(bf16[256,1024]{1,0:T(8,128)(2,1)} %get-tuple-element.145), channel_id=1, source_target_pairs={{0,2},{1,3},{2,0},{3,1},{4,6},{5,7},{6,4},{7,5},{8,10},{9,11},{10,... | collective-permute-start | bytes 1572872 | tf_op jit(solution)/shard_map/ppermute | solution.py:71
  251.8 18.1 %collective-permute-start.27 = (f32[256,1024]{1,0:T(8,128)}, f32[256,1024]{1,0:T(8,128)S(1)}, u32[]{:S(2)}, u32[]{:S(2)}) collective-permute-start(f32[256,1024]{1,0:T(8,128)} %get-tuple-element.137), channel_id=1, source_target_pairs={{0,4},{4,0},{1,5},{5,1},{2,6},{6,2},{3,7},{7,3},{8,12},{12,8},{9,1... | collective-permute-start | bytes 3145736 | tf_op jit(solution)/shard_map/ppermute | solution.py:71
  252.0 27.3 %collective-permute-start.33 = (bf16[256,1024]{1,0:T(8,128)(2,1)}, bf16[256,1024]{1,0:T(8,128)(2,1)S(1)}, u32[]{:S(2)}, u32[]{:S(2)}) collective-permute-start(bf16[256,1024]{1,0:T(8,128)(2,1)} %get-tuple-element.254), channel_id=1, source_target_pairs={{0,2},{1,3},{2,0},{3,1},{4,6},{5,7},{6,4},{7,5},{8,10},{9,11},{10,... | collective-permute-start | bytes 1572872 | tf_op jit(solution)/shard_map/ppermute | solution.py:71
  252.6 23.7 %collective-permute-start.36 = (bf16[256,1024]{1,0:T(8,128)(2,1)}, bf16[256,1024]{1,0:T(8,128)(2,1)}, u32[]{:S(2)}, u32[]{:S(2)}) collective-permute-start(bf16[256,1024]{1,0:T(8,128)(2,1)} %get-tuple-element.161), channel_id=1, source_target_pairs={{0,1},{1,0},{2,3},{3,2},{4,5},{5,4},{6,7},{7,6},{8,9},{9,8},{10,11... | collective-permute-start | bytes 1572872 | tf_op jit(solution)/shard_map/ppermute | solution.py:71
  268.5 11.4 %collective-permute-start.32 = (bf16[256,1024]{1,0:T(8,128)(2,1)}, bf16[256,1024]{1,0:T(8,128)(2,1)S(1)}, u32[]{:S(2)}, u32[]{:S(2)}) collective-permute-start(bf16[256,1024]{1,0:T(8,128)(2,1)} %get-tuple-element.249), channel_id=1, source_target_pairs={{0,1},{1,0},{2,3},{3,2},{4,5},{5,4},{6,7},{7,6},{8,9},{9,8},{10,11... | collective-permute-start | bytes 1572872 | tf_op jit(solution)/shard_map/ppermute | solution.py:71
  275.7 27.1 %collective-permute-start.41 = (bf16[256,1024]{1,0:T(8,128)(2,1)}, bf16[256,1024]{1,0:T(8,128)(2,1)}, u32[]{:S(2)}, u32[]{:S(2)}) collective-permute-start(bf16[256,1024]{1,0:T(8,128)(2,1)} %get-tuple-element.168), channel_id=1, source_target_pairs={{0,2},{1,3},{2,0},{3,1},{4,6},{5,7},{6,4},{7,5},{8,10},{9,11},{10,... | collective-permute-start | bytes 1572872 | tf_op jit(solution)/shard_map/ppermute | solution.py:71
  276.3 26.4 %collective-permute-start.37 = (bf16[256,1024]{1,0:T(8,128)(2,1)}, bf16[256,1024]{1,0:T(8,128)(2,1)}, u32[]{:S(2)}, u32[]{:S(2)}) collective-permute-start(bf16[256,1024]{1,0:T(8,128)(2,1)} %get-tuple-element.162), channel_id=1, source_target_pairs={{0,1},{1,0},{2,3},{3,2},{4,5},{5,4},{6,7},{7,6},{8,9},{9,8},{10,11... | collective-permute-start | bytes 1572872 | tf_op jit(solution)/shard_map/ppermute | solution.py:71
  279.3 25.6 %collective-permute-start.38 = (bf16[256,1024]{1,0:T(8,128)(2,1)}, bf16[256,1024]{1,0:T(8,128)(2,1)}, u32[]{:S(2)}, u32[]{:S(2)}) collective-permute-start(bf16[256,1024]{1,0:T(8,128)(2,1)} %get-tuple-element.163), channel_id=1, source_target_pairs={{0,2},{1,3},{2,0},{3,1},{4,6},{5,7},{6,4},{7,5},{8,10},{9,11},{10,... | collective-permute-start | bytes 1572872 | tf_op jit(solution)/shard_map/ppermute | solution.py:71
  279.9 25.0 %collective-permute-start.48 = (bf16[256,1024]{1,0:T(8,128)(2,1)}, bf16[256,1024]{1,0:T(8,128)(2,1)}, u32[]{:S(2)}, u32[]{:S(2)}) collective-permute-start(bf16[256,1024]{1,0:T(8,128)(2,1)} %get-tuple-element.178), channel_id=1, source_target_pairs={{0,1},{1,0},{2,3},{3,2},{4,5},{5,4},{6,7},{7,6},{8,9},{9,8},{10,11... | collective-permute-start | bytes 1572872 | tf_op jit(solution)/shard_map/ppermute | solution.py:71
  282.7 22.3 %collective-permute-start.34 = (bf16[256,1024]{1,0:T(8,128)(2,1)S(1)}, bf16[256,1024]{1,0:T(8,128)(2,1)S(1)}, u32[]{:S(2)}, u32[]{:S(2)}) collective-permute-start(bf16[256,1024]{1,0:T(8,128)(2,1)S(1)} %add_convert_fusion.5), channel_id=1, source_target_pairs={{0,8},{8,16},{16,24},{24,0},{1,9},{9,17},{17,25},{25,1},{2,10},{10... | collective-permute-start | bytes 1572872 | tf_op jit(solution)/shard_map/ppermute | solution.py:81
  302.7 12.6 %collective-permute-start.44 = (bf16[256,512]{1,0:T(8,128)(2,1)}, bf16[256,512]{1,0:T(8,128)(2,1)}, u32[]{:S(2)}, u32[]{:S(2)}) collective-permute-start(bf16[256,512]{1,0:T(8,128)(2,1)} %get-tuple-element.172), channel_id=1, source_target_pairs={{0,1},{1,0},{2,3},{3,2},{4,5},{5,4},{6,7},{7,6},{8,9},{9,8},{10,11... | collective-permute-start | bytes 786440 | tf_op jit(solution)/shard_map/ppermute | solution.py:71
  303.4 13.4 %collective-permute-start.42 = (bf16[256,512]{1,0:T(8,128)(2,1)}, bf16[256,512]{1,0:T(8,128)(2,1)}, u32[]{:S(2)}, u32[]{:S(2)}) collective-permute-start(bf16[256,512]{1,0:T(8,128)(2,1)} %get-tuple-element.169), channel_id=1, source_target_pairs={{0,2},{1,3},{2,0},{3,1},{4,6},{5,7},{6,4},{7,5},{8,10},{9,11},{10,... | collective-permute-start | bytes 786440 | tf_op jit(solution)/shard_map/ppermute | solution.py:71
  309.3 20.3 %collective-permute-start.39 = (bf16[256,1024]{1,0:T(8,128)(2,1)}, bf16[256,1024]{1,0:T(8,128)(2,1)S(1)}, u32[]{:S(2)}, u32[]{:S(2)}) collective-permute-start(bf16[256,1024]{1,0:T(8,128)(2,1)} %get-tuple-element.164), channel_id=1, source_target_pairs={{0,2},{1,3},{2,0},{3,1},{4,6},{5,7},{6,4},{7,5},{8,10},{9,11},{10,... | collective-permute-start | bytes 1572872 | tf_op jit(solution)/shard_map/ppermute | solution.py:71
  315.3 11.1 %collective-permute-start.63 = (bf16[256,512]{1,0:T(8,128)(2,1)S(1)}, bf16[256,512]{1,0:T(8,128)(2,1)}, u32[]{:S(2)}, u32[]{:S(2)}) collective-permute-start(bf16[256,512]{1,0:T(8,128)(2,1)S(1)} %copy-done.45), channel_id=1, source_target_pairs={{0,1},{1,0},{2,3},{3,2},{4,5},{5,4},{6,7},{7,6},{8,9},{9,8},{10,11... | collective-permute-start | bytes 786440 | tf_op jit(solution)/shard_map/ppermute | solution.py:71
  316.8 19.9 %collective-permute-start.59 = (bf16[256,512]{1,0:T(8,128)(2,1)}, bf16[256,512]{1,0:T(8,128)(2,1)S(1)}, u32[]{:S(2)}, u32[]{:S(2)}) collective-permute-start(bf16[256,512]{1,0:T(8,128)(2,1)} %get-tuple-element.187), channel_id=1, source_target_pairs={{0,2},{1,3},{2,0},{3,1},{4,6},{5,7},{6,4},{7,5},{8,10},{9,11},{10,... | collective-permute-start | bytes 786440 | tf_op jit(solution)/shard_map/ppermute | solution.py:71
  317.4 16.8 %collective-permute-start.49 = (bf16[256,1024]{1,0:T(8,128)(2,1)S(1)}, bf16[256,1024]{1,0:T(8,128)(2,1)S(1)}, u32[]{:S(2)}, u32[]{:S(2)}) collective-permute-start(bf16[256,1024]{1,0:T(8,128)(2,1)S(1)} %copy-done.20), channel_id=1, source_target_pairs={{0,1},{1,0},{2,3},{3,2},{4,5},{5,4},{6,7},{7,6},{8,9},{9,8},{10,11... | collective-permute-start | bytes 1572872 | tf_op jit(solution)/shard_map/ppermute | solution.py:71
  324.5 23.4 %collective-permute-start.35 = (f32[256,1024]{1,0:T(8,128)}, f32[256,1024]{1,0:T(8,128)S(1)}, u32[]{:S(2)}, u32[]{:S(2)}) collective-permute-start(f32[256,1024]{1,0:T(8,128)} %get-tuple-element.151), channel_id=1, source_target_pairs={{0,4},{4,0},{1,5},{5,1},{2,6},{6,2},{3,7},{7,3},{8,12},{12,8},{9,1... | collective-permute-start | bytes 3145736 | tf_op jit(solution)/shard_map/ppermute | solution.py:71
  326.4 16.7 %collective-permute-start.69 = (bf16[256,1024]{1,0:T(8,128)(2,1)S(1)}, bf16[256,1024]{1,0:T(8,128)(2,1)S(1)}, u32[]{:S(2)}, u32[]{:S(2)}) collective-permute-start(bf16[256,1024]{1,0:T(8,128)(2,1)S(1)} %get-tuple-element.199), channel_id=1, source_target_pairs={{0,24},{8,0},{16,8},{24,16},{1,25},{9,1},{17,9},{25,17},{2,26},{10... | collective-permute-start | bytes 1572872 | tf_op jit(solution)/shard_map/ppermute | solution.py:81
  334.2 11.0 %collective-permute-start.46 = (bf16[256,512]{1,0:T(8,128)(2,1)S(1)}, bf16[256,512]{1,0:T(8,128)(2,1)S(1)}, u32[]{:S(2)}, u32[]{:S(2)}) collective-permute-start(bf16[256,512]{1,0:T(8,128)(2,1)S(1)} %copy-done.44), channel_id=1, source_target_pairs={{0,2},{1,3},{2,0},{3,1},{4,6},{5,7},{6,4},{7,5},{8,10},{9,11},{10,... | collective-permute-start | bytes 786440 | tf_op jit(solution)/shard_map/ppermute | solution.py:71
  339.9 42.7 %collective-permute-start.80 = (bf16[256,512]{1,0:T(8,128)(2,1)}, bf16[256,512]{1,0:T(8,128)(2,1)}, u32[]{:S(2)}, u32[]{:S(2)}) collective-permute-start(bf16[256,512]{1,0:T(8,128)(2,1)} %get-tuple-element.216), channel_id=1, source_target_pairs={{0,2},{1,3},{2,0},{3,1},{4,6},{5,7},{6,4},{7,5},{8,10},{9,11},{10,... | collective-permute-start | bytes 786440 | tf_op jit(solution)/shard_map/ppermute | solution.py:71
  343.1 14.6 %collective-permute-start.70 = (bf16[256,1024]{1,0:T(8,128)(2,1)}, bf16[256,1024]{1,0:T(8,128)(2,1)S(1)}, u32[]{:S(2)}, u32[]{:S(2)}) collective-permute-start(bf16[256,1024]{1,0:T(8,128)(2,1)} %get-tuple-element.200), channel_id=1, source_target_pairs={{0,8},{8,16},{16,24},{24,0},{1,9},{9,17},{17,25},{25,1},{2,10},{10... | collective-permute-start | bytes 1572872 | tf_op jit(solution)/shard_map/ppermute | solution.py:81
  345.2 16.3 %collective-permute-start.67 = (bf16[256,512]{1,0:T(8,128)(2,1)}, bf16[256,512]{1,0:T(8,128)(2,1)}, u32[]{:S(2)}, u32[]{:S(2)}) collective-permute-start(bf16[256,512]{1,0:T(8,128)(2,1)} %add_convert_fusion.12), channel_id=1, source_target_pairs={{0,2},{1,3},{2,0},{3,1},{4,6},{5,7},{6,4},{7,5},{8,10},{9,11},{10,... | collective-permute-start | bytes 786440 | tf_op jit(solution)/shard_map/ppermute | solution.py:71
  345.7 19.0 %collective-permute-start.75 = (bf16[256,512]{1,0:T(8,128)(2,1)}, bf16[256,512]{1,0:T(8,128)(2,1)}, u32[]{:S(2)}, u32[]{:S(2)}) collective-permute-start(bf16[256,512]{1,0:T(8,128)(2,1)} %add_convert_fusion.10), channel_id=1, source_target_pairs={{0,1},{1,0},{2,3},{3,2},{4,5},{5,4},{6,7},{7,6},{8,9},{9,8},{10,11... | collective-permute-start | bytes 786440 | tf_op jit(solution)/shard_map/ppermute | solution.py:71
  353.7 11.7 %collective-permute-start.54 = (f32[1,2304]{1,0:T(1,128)S(1)}, f32[1,2304]{1,0:T(1,128)S(1)}, u32[]{:S(2)}, u32[]{:S(2)}) collective-permute-start(f32[1,2304]{1,0:T(1,128)S(1)} %get-tuple-element.298), channel_id=1, source_target_pairs={{0,2},{1,3},{2,0},{3,1},{4,6},{5,7},{6,4},{7,5},{8,10},{9,11},{10,... | collective-permute-start | bytes 27656 | tf_op jit(solution)/shard_map/ppermute | solution.py:71
  364.7 68.9 %collective-permute-start.83 = (f32[128,1024]{1,0:T(8,128)S(1)}, f32[128,1024]{1,0:T(8,128)S(1)}, u32[]{:S(2)}, u32[]{:S(2)}) collective-permute-start(f32[128,1024]{1,0:T(8,128)S(1)} %get-tuple-element.258), channel_id=1, source_target_pairs={{0,4},{4,0},{1,5},{5,1},{2,6},{6,2},{3,7},{7,3},{8,12},{12,8},{9,1... | collective-permute-start | bytes 1572872 | tf_op jit(solution)/shard_map/ppermute | solution.py:71
  380.8 21.0 %collective-permute-start.79 = (bf16[256,512]{1,0:T(8,128)(2,1)}, bf16[256,512]{1,0:T(8,128)(2,1)}, u32[]{:S(2)}, u32[]{:S(2)}) collective-permute-start(bf16[256,512]{1,0:T(8,128)(2,1)} %add_convert_fusion.8), channel_id=1, source_target_pairs={{0,24},{8,0},{16,8},{24,16},{1,25},{9,1},{17,9},{25,17},{2,26},{10... | collective-permute-start | bytes 786440 | tf_op jit(solution)/shard_map/ppermute | solution.py:81
  415.2 18.4 %collective-permute-start.82 = (f32[128,512]{1,0:T(8,128)}, f32[128,512]{1,0:T(8,128)S(1)}, u32[]{:S(2)}, u32[]{:S(2)}) collective-permute-start(f32[128,512]{1,0:T(8,128)} %get-tuple-element.264), channel_id=1, source_target_pairs={{0,4},{4,0},{1,5},{5,1},{2,6},{6,2},{3,7},{7,3},{8,12},{12,8},{9,1... | collective-permute-start | bytes 786440 | tf_op jit(solution)/shard_map/ppermute | solution.py:71
  415.7 12.4 %collective-permute-start.51 = (f32[51,1024]{1,0:T(8,128)S(1)}, f32[51,1024]{1,0:T(8,128)S(1)}, u32[]{:S(2)}, u32[]{:S(2)}) collective-permute-start(f32[51,1024]{1,0:T(8,128)S(1)} %add.612), channel_id=1, source_target_pairs={{0,16},{8,24},{16,0},{24,8},{1,17},{9,25},{17,1},{25,9},{2,18},{10... | collective-permute-start | bytes 626696 | tf_op jit(solution)/shard_map/ppermute | solution.py:71
  428.1 11.1 %collective-permute-start.74 = (f32[32,128]{1,0:T(8,128)S(1)}, f32[32,128]{1,0:T(8,128)S(1)}, u32[]{:S(2)}, u32[]{:S(2)}) collective-permute-start(f32[32,128]{1,0:T(8,128)S(1)} %fusion.17), channel_id=1, source_target_pairs={{0,3},{1,2},{2,1},{3,0},{4,7},{5,6},{6,5},{7,4},{8,11},{9,10},{10,... | collective-permute-start | bytes 49160 | tf_op jit(solution)/shard_map/ppermute | solution.py:71
  (109 other events, 918.5 us)
Sparse Core Ops, SparseCore 0:
  13.6 158.1 all-gather.1

commit v3 on v2

--- a/solution.py
+++ b/solution.py
@@ -15,8 +15,7 @@
 ADAM_STEP = 10
 PATCH_ROWS = 16
 PINS = (None, 1, 3, 4, 7)
-CHAIN = (16, 1)
-BIASES = (14, 1)
+CHAIN = (20, 1)
 
 PRECISE = lax.Precision.HIGHEST
 BF = jnp.bfloat16
@@ -124,19 +123,6 @@
     return value
 
 
-def sum_slow(value, axes, pace, steps):
-    for axis in axes:
-        count = lax.axis_size(axis)
-        if count > 4:
-            value = lax.psum(value, axis)
-            continue
-        for mask in bits(count):
-            moved = swap(pace(value), axis, mask)
-            steps.append(moved)
-            value = value + moved
-    return value
-
-
 def roll_lead(stack, steps):
     for mask in (1, 2):
         moved = jnp.stack([stack[(i + mask) % 4] for i in range(4)])
@@ -170,6 +156,56 @@
     mine = pace(by_xor(blocks, t))
     got = jnp.stack([mine[0]] + [swap(mine[k], "tp", k) for k in (1, 2, 3)])
     return by_xor(got, t)
+
+
+def gather_and_sum(to_tp, shared, split, pace):
+    f, c, t = lax.axis_index("fsdp"), lax.axis_index("ctx"), lax.axis_index("tp")
+    images, wide = to_tp.shape[1:]
+    width = shared.shape[1]
+    per_image = -(-wide // width)
+    padded = jnp.pad(to_tp, ((0, 0), (0, 0), (0, per_image * width - wide)))
+    mine = by_xor(padded.reshape(4, images * per_image, width), t)
+    kept, sums = images * per_image, shared.shape[0]
+    rows = jnp.concatenate([shared, split], axis=0)
+    sent = pace(jnp.concatenate([mine.reshape(-1, width), rows], axis=0))
+    whole = [sent[i * kept : (i + 1) * kept] for i in range(4)]
+    rows = sent[4 * kept :]
+    got = [swap(jnp.concatenate([whole[k], rows], axis=0), "tp", k) for k in (1, 2, 3)]
+    group = by_xor(jnp.stack([whole[0]] + [g[:kept] for g in got]), t).reshape(-1, width)
+    rows = (rows + got[0][kept:]) + (got[1][kept:] + got[2][kept:])
+
+    quarter = width // 4
+    shared, split = rows[:sums], rows[sums:]
+    blocks = roll_lead(jnp.stack([split[:, i * quarter : (i + 1) * quarter] for i in range(4)]), f)
+    same = jnp.concatenate([group, shared], axis=0).reshape(-1, quarter)
+    count = same.shape[0]
+    sent = pace(jnp.concatenate([same, blocks.reshape(-1, quarter)], axis=0))
+    same, blocks = sent[:count], [
+        sent[count + i * split.shape[0] : count + (i + 1) * split.shape[0]] for i in range(4)
+    ]
+    got = [None] + [push(jnp.concatenate([same, blocks[k]], axis=0), k) for k in (1, 2, 3)]
+    group_count = 4 * group.shape[0]
+    by_sender = jnp.stack([same[:group_count]] + [got[k][:group_count] for k in (3, 2, 1)])
+    by_sender = roll_lead(by_sender, (4 - f) & 3)
+    shared = same[group_count:]
+    shared = (shared + got[2][group_count:count]) + (got[1][group_count:count] + got[3][group_count:count])
+    split = (blocks[0] + got[2][count:]) + (got[1][count:] + got[3][count:])
+
+    half = quarter // 2
+    low, high = split[:, :half], split[:, half:]
+    other_half = jnp.where(c == 0, high, low)
+    shared_half = shared.reshape(-1, half)
+    sent = pace(
+        jnp.concatenate([by_sender.reshape(-1, half), shared_half, other_half], axis=0)
+    )
+    got = swap(sent, "ctx", 1)
+    count = by_sender.size // half
+    group = ordered(
+        sent[:count].reshape(4, -1), got[:count].reshape(4, -1), c, 1
+    ).reshape(-1, per_image * width)[:, :wide]
+    shared = (shared_half + got[count : count + shared_half.shape[0]]).reshape(-1, width)
+    split = jnp.where(c == 0, low, high) + got[count + shared_half.shape[0] :]
+    return group, shared, split
 
 
 class Lane:
@@ -1032,30 +1068,19 @@
 
     qkv_rows = grad_b_qkv.reshape(nt, 3, half)
     up_rows = heads_place(grad_b_up.reshape(nt, 4, half))
-    width_rows = (
-        jnp.concatenate(
-            [grad_b_patch[None], grad_b_proj[None], grad_b_down[None], grad_patch, grad_head], axis=0
-        )
-    )
     loss_row = jnp.broadcast_to(loss_part, (1, width))
-    payload = jnp.concatenate(
+    shared = jnp.concatenate(
         [
-            width_rows[0:1],
+            heads_place(jnp.stack([qkv_rows[:, 0], qkv_rows[:, 2]], axis=1)),
+            grad_b_proj[None],
+            up_rows,
+            grad_b_down[None],
             loss_row,
-            jnp.zeros((1, width), F32),
-            jnp.sum(grad_mod, axis=0),
-            heads_place(jnp.stack([qkv_rows[:, 0], qkv_rows[:, 2]], axis=1)),
-            width_rows[1:2],
-            up_rows,
-            width_rows[2:3],
-            jnp.sum(grad_final, axis=0),
-            width_rows[3:],
         ],
         axis=0,
     )
-    steps = []
-    payload = sum_slow(payload, ("ctx", "tp", "fsdp"), Pace(lanes, *BIASES), steps)
-    chain = Pace(lanes, *CHAIN, [None, None] + steps)
+    split = jnp.concatenate([grad_patch, grad_head, grad_b_patch[None]], axis=0)
+    chain = Pace(lanes, *CHAIN)
     final_flat = jnp.concatenate(
         [jnp.zeros((img_count, width), F32), grad_final.reshape(img_count, 2 * width)], axis=1
     )
@@ -1068,18 +1093,30 @@
         ],
         axis=-1,
     )
-    group_grad = exchange_tp(to_tp, chain).reshape(group_images, -1)
-    all_grad = gather_fc(group_grad, chain).reshape(images_all, -1)
+    if is_ring():
+        all_grad, shared, split = gather_and_sum(to_tp, shared, split, chain)
+    else:
+        group_grad = exchange_tp(to_tp).reshape(group_images, -1)
+        all_grad = gather_fc(group_grad).reshape(images_all, -1)
+        shared = sum_over(shared, ("tp", "fsdp", "ctx"))
+        split = split.reshape(split.shape[0], places, row_count).transpose(1, 0, 2)
+        split = scatter_fc(sum_over(split, ("tp",)))
     all_mod, all_final = all_grad[:, :mod_width], all_grad[:, mod_width:]
     cond_rows = cond_low.astype(F32)
     grad_w_mod = exact_dot(cond_rows.T, all_mod)
     mod_flat = mod_low.astype(F32).transpose(1, 0, 2).reshape(row_count, mod_width)
     top_rows = top_low.astype(F32)
-    grad_cond_act = sum_over(
-        exact_dot(all_mod, mod_flat.T) + exact_dot(all_final, top_rows.T), ("tp",), chain
-    )
+    part = exact_dot(all_mod, mod_flat.T) + exact_dot(all_final, top_rows.T)
+    sent = chain(jnp.concatenate([part, jnp.sum(all_grad, axis=0).reshape(-1, row_count)], axis=0))
+    got = [sent] + [swap(sent, "tp", k) for k in (1, 2, 3)]
+    grad_cond_act = (got[0] + got[1])[:images_all] + (got[2] + got[3])[:images_all]
+    col_sums = by_xor(jnp.stack([g[images_all:] for g in got]), t).reshape(nt, -1)
+    bias_mod = col_sums[:, :mod_width].reshape(nt, 6, local_width).transpose(1, 0, 2).reshape(6, width)
+    bias_final = col_sums[:, mod_width:].reshape(-1)[width:].reshape(2, width)
     grad_cond = jax.vjp(jax.nn.silu, cond)[1](grad_cond_act)[0]
-    cond_all = gather_fc(grad_cond, chain).transpose(1, 0, 2).reshape(images_all, width)
+    rows_all = gather_fc(jnp.concatenate([grad_cond, split[2 * PATCH_ROWS :]], axis=0), chain)
+    rows_all = rows_all.transpose(1, 0, 2).reshape(-1, width)
+    cond_all, bias_patch = rows_all[:images_all], rows_all[images_all:]
     grad_b_cond = jnp.sum(cond_all, axis=0)
     cond_padded = jnp.concatenate([cond_all, jnp.zeros((images_all, 2 * width), F32)], axis=1)
     cond_top = lax.dynamic_slice_in_dim(cond_padded, top_cols * t, top_cols, 1)
@@ -1087,9 +1124,8 @@
     grad_hidden = sum_over(exact_dot(cond_top, top_rows.T), ("tp",), chain)
     grad_t_pre = jax.vjp(jax.nn.silu, t_pre)[1](grad_hidden)[0]
 
-    loss_total = payload[1, 0]
-    small_sum = lax.dynamic_slice_in_dim(payload[19:], place * row_count, row_count, 1)
-    patch_sum, head_sum = small_sum[:PATCH_ROWS], small_sum[PATCH_ROWS:]
+    loss_total = shared[8, 0]
+    patch_sum, head_sum = split[:PATCH_ROWS], split[PATCH_ROWS : 2 * PATCH_ROWS]
     head_grad_sum = head_sum.T
 
     def from_cores(total):
@@ -1130,7 +1166,7 @@
     last = jnp.concatenate([b1_row, jnp.broadcast_to(shard_squares, (128,))])
     last = sum_over(last, ("ctx", "tp", "fsdp"))
     bias_sum = jnp.concatenate(
-        [payload[0:1], last[None, :width], grad_b_cond[None], payload[3:19]], axis=0
+        [bias_patch, last[None, :width], grad_b_cond[None], bias_mod, shared[:8], bias_final], axis=0
     )
     grad_norm = jnp.sqrt(last[width] + jnp.sum(bias_sum * bias_sum))
     clip_factor = jnp.minimum(1.0, 1.0 / (grad_norm + 1e-06))

time: 488 us -> 475 us (0.973)
  waiting for transfers between devices: 187 us -> 178 us
    ppermute x70 -> x65, starting transfers between devices: 65 us -> 56.1 us  [swap(): return lax.ppermute(value, axis, [(i, i ^ mask) for i in range(count)])]
    ppermute x12 -> x15, waiting for transfers between devices: 22 us -> 14.5 us  [push(): lax.ppermute(value, 'fsdp', [(i, (i + k) % count) for i in range(count)])]
    ppermute x12 -> x15, starting transfers between devices: 17.7 us -> 23.3 us  [push(): lax.ppermute(value, 'fsdp', [(i, (i + k) % count) for i in range(count)])]
    ppermute x70 -> x65, waiting for transfers between devices: 73.2 us -> 70.6 us  [swap(): return lax.ppermute(value, axis, [(i, i ^ mask) for i in range(count)])]
    unnamed x127 -> x163, local copies, waits for them, and re-layouts: 11.4 us -> 13 us
    ppermute x9 -> x6, starting transfers between devices: 14.9 us -> 13.9 us  [pull(): lax.ppermute(value, 'fsdp', [((i + k) % count, i) for i in range(count)])]
  transfers between devices with their start and end apart: 92 -> 87, of which waited for: 42 -> 45; matrix products, arithmetic and copies ran while one was open for 11% -> 11% of each run, Pallas kernels for 9% -> 9%
where the time goes in v3:
time: 475 us; the launch traced here: 470 us
  waiting for transfers between devices  178 us (37%)
  Pallas kernels  95.7 us (20%)
  starting transfers between devices  93.3 us (20%)
  other arithmetic  42.6 us (9%)
  local copies, waits for them, and re-layouts  30.1 us (6%)
  between operations  22.5 us (5%)
  matrix products  8.24 us (2%)
    all_gather x1, waiting for transfers between devices, on_device(): full = lax.all_gather(shards, ('tp', 'fsdp'), axis=0, tiled=True)  89.1 us
    ppermute x65, waiting for transfers between devices, swap(): return lax.ppermute(value, axis, [(i, i ^ mask) for i in range(count)])  70.6 us
    pallas_call x12, Pallas kernels, call(): pl.pallas_call(kernel, grid=(1,), out_shape=outs, in_specs=specs, out_spe...  62.9 us
    ppermute x65, starting transfers between devices, swap(): return lax.ppermute(value, axis, [(i, i ^ mask) for i in range(count)])  56.1 us
    pallas_call x2, Pallas kernels, over_hidden(): pl.pallas_call(kernel, grid=(counts,), out_shape=[o[0] for o in outs], in...  27.6 us
    ppermute x15, starting transfers between devices, push(): lax.ppermute(value, 'fsdp', [(i, (i + k) % count) for i in range(count)])  23.3 us
    convert_element_type x9, other arithmetic, add_low(): return add(left, right).astype(BF)  15.3 us
    ppermute x15, waiting for transfers between devices, push(): lax.ppermute(value, 'fsdp', [(i, (i + k) % count) for i in range(count)])  14.5 us
  transfers between devices with their start and end apart: 87, of which 45 were waited for; matrix products, arithmetic and copies ran while one was open for 11% of the time, Pallas kernels for 9%

profile of v3, /device:TPU:0, one launch (start us, length us, event | category | flops | bytes accessed | tf_op | source)
XLA Modules:
  0.0 470.0 jit_solution(5166528640071197546)
XLA Ops:
  13.7 3.0 collective-permute-start.2
  28.7 4.2 collective-permute-done.5
  38.6 3.3 collective-permute-start.10
  43.6 4.1 collective-permute-done.9
  63.0 3.7 collective-permute-done.16
  82.7 89.1 %all-gather.2.cloned.1.call-done.refs_2_.refs_1_.up_ref.down_ref = bf16[4096,1536]{1,0:T(8,128)(2,1)} async-done(((bf16[256,1536]{1,0:T(8,128)(2,1)}), bf16[4096,1536]{1,0:T(8,128)(2,1)}) %all-gather.2.cloned.1.call-update) | async-done | bytes 12582928 | tf_op jit(solution)/shard_map/all_gather | solution.py:786
  171.8 7.3 %shard_map.374 = (bf16[512,1536]{1,0:T(8,128)(2,1)}, bf16[512,512]{1,0:T(8,128)(2,1)}) custom-call(bf16[256,1024]{1,0:T(8,128)(2,1)} %get-tuple-element.114.refs_0_, bf16[256,1024]{1,0:T(8,128)(2,1)} %copy-done.8, bf16[4096,1536]{1,0:T(8,128)(2,1)} %all-gather.2.cloned.1.call-done.refs_2_.refs_1_.up_ref.down_ref, f32[1,1536]{1,0:T(1,128)} %broadcast_in_dim_reshape.7.refs_3_), custom_call_target="tpu_custom_call" | custom-call | flops 2147483648 | bytes 6297600 | tf_op jit(solution)/shard_map/pallas_call | solution.py:334
  179.1 3.5 shard_map.375
  182.6 2.9 collective-permute-done.23.refs_1_
  186.5 3.6 shard_map.376
  193.0 10.9 %shard_map.377 = (f32[512,2048]{1,0:T(8,128)}, bf16[512,2048]{1,0:T(8,128)(2,1)}, f32[256,1024]{1,0:T(8,128)}, f32[256,1024]{1,0:T(8,128)}) custom-call(bf16[256,1024]{1,0:T(8,128)(2,1)} %get-tuple-element.119.own_ref.own_in, bf16[256,1024]{1,0:T(8,128)(2,1)} %copy-done.10, bf16[4096,1536]{1,0:T(8,128)(2,1)} %all-gather.2.cloned.1.call-done.refs_2_.refs_1_.up_ref.down_ref, ...), custom_call_target="tpu_custom_call" | custom-call | flops 4294967296 | bytes 33554432 | tf_op jit(solution)/shard_map/pallas_call | solution.py:518
  208.2 4.6 shard_map.378
  215.7 16.7 %shard_map.379 = (bf16[4096,1024]{1,0:T(8,128)(2,1)}, f32[1,2048]{1,0:T(1,128)}, f32[256,1024]{1,0:T(8,128)}, f32[256,1024]{1,0:T(8,128)}) custom-call(bf16[256,1024]{1,0:T(8,128)(2,1)} %get-tuple-element.123.own_ref, bf16[256,1024]{1,0:T(8,128)(2,1)} %copy-done.17, bf16[256,1024]{1,0:T(8,128)(2,1)} %get-tuple-element.119.own_ref.own_in, ...), custom_call_target="tpu_custom_call" | custom-call | flops 8589934592 | bytes 33554432 | tf_op jit(solution)/shard_map/pallas_call | solution.py:518
  232.4 4.0 constant_dynamic-slice_fusion
  238.5 12.2 %collective-permute-done.30 = bf16[256,1024]{1,0:T(8,128)(2,1)S(1)} collective-permute-done((bf16[256,1024]{1,0:T(8,128)(2,1)S(1)}, bf16[256,1024]{1,0:T(8,128)(2,1)S(1)}, u32[]{:S(2)}, u32[]{:S(2)}) %collective-permute-start.30) | collective-permute-done | bytes 524320 | tf_op jit(solution)/shard_map/ppermute | solution.py:70
  255.5 11.1 %collective-permute-done.31 = bf16[256,1024]{1,0:T(8,128)(2,1)} collective-permute-done((bf16[256,1024]{1,0:T(8,128)(2,1)}, bf16[256,1024]{1,0:T(8,128)(2,1)}, u32[]{:S(2)}, u32[]{:S(2)}) %collective-permute-start.31) | collective-permute-done | bytes 524320 | tf_op jit(solution)/shard_map/ppermute | solution.py:70
  266.6 3.4 add_convert_fusion.2
  272.6 4.6 shard_map.380
  286.1 13.3 %shard_map.381 = (bf16[512,1536]{1,0:T(8,128)(2,1)}, f32[1,1536]{1,0:T(1,128)}) custom-call(bf16[256,1024]{1,0:T(8,128)(2,1)} %get-tuple-element.132.refs_0_.refs_2_, bf16[256,1024]{1,0:T(8,128)(2,1)} %copy-done.9, bf16[4096,1536]{1,0:T(8,128)(2,1)} %all-gather.2.cloned.1.call-done.refs_2_.refs_1_.up_ref.down_ref, bf16[512,1536]{1,0:T(8,128)(2,1)} %get-tuple-element.133.refs_3_), custom_call_target="tpu_custom_call" | custom-call | flops 1073741824 | bytes 5249024 | tf_op jit(solution)/shard_map/pallas_call | solution.py:334
  300.0 5.3 %shard_map.385 = (bf16[256,512]{1,0:T(8,128)(2,1)}, bf16[256,512]{1,0:T(8,128)(2,1)}, bf16[256,512]{1,0:T(8,128)(2,1)}, bf16[256,512]{1,0:T(8,128)(2,1)}, bf16[2...) custom-call(bf16[256,1024]{1,0:T(8,128)(2,1)} %get-tuple-element.114.refs_0_, ...), custom_call_target="tpu_custom_call" | custom-call | flops 1073741824 | bytes 6291456 | tf_op jit(solution)/shard_map/pallas_call | solution.py:334
  307.4 4.2 add_convert_fusion
  312.3 5.3 %shard_map.382 = (bf16[256,512]{1,0:T(8,128)(2,1)}, bf16[256,512]{1,0:T(8,128)(2,1)}, bf16[256,512]{1,0:T(8,128)(2,1)}, bf16[256,512]{1,0:T(8,128)(2,1)}, bf16[2...) custom-call(bf16[256,1024]{1,0:T(8,128)(2,1)} %get-tuple-element.114.refs_0_, ...), custom_call_target="tpu_custom_call" | custom-call | flops 1073741824 | bytes 6291456 | tf_op jit(solution)/shard_map/pallas_call | solution.py:334
  321.3 5.6 %shard_map.383 = (f32[256,1024]{1,0:T(8,128)}, f32[256,1024]{1,0:T(8,128)}) custom-call(bf16[512,1536]{1,0:T(8,128)(2,1)} %get-tuple-element.151.refs_4_.refs_0_, bf16[4096,1536]{1,0:T(8,128)(2,1)} %all-gather.2.cloned.1.call-done.refs_2_.refs_1_.up_ref.down_ref), custom_call_target="tpu_custom_call" | custom-call | flops 1610612736 | bytes 6815744 | tf_op jit(solution)/shard_map/pallas_call | solution.py:334
  328.5 3.2 collective-permute-start.55
  333.2 5.2 %collective-permute-done.53 = bf16[256,1024]{1,0:T(8,128)(2,1)S(1)} collective-permute-done((bf16[256,1024]{1,0:T(8,128)(2,1)S(1)}, bf16[256,1024]{1,0:T(8,128)(2,1)S(1)}, u32[]{:S(2)}, u32[]{:S(2)}) %collective-permute-start.53) | collective-permute-done | bytes 524320 | tf_op jit(solution)/shard_map/ppermute | solution.py:70
  341.1 2.9 collective-permute-done.68
  351.3 3.8 shard_map.384
  382.1 2.9 collective-permute-start.70
  422.9 3.4 shard_map.386
  436.6 4.2 collective-permute-start.85
  442.5 2.9 collective-permute-done.84
  458.4 3.3 shard_map.387
  (585 shorter events, 189.8 us)
Async XLA Ops:
  7.2 164.6 %all-gather.2.cloned.1.call-start = ((), (), s32[]{:S(2)}) async-start(), calls=%async_computation | async-start | bytes 13369344 | tf_op jit(solution)/shard_map/all_gather | solution.py:786
  236.4 14.2 %collective-permute-start.30 = (bf16[256,1024]{1,0:T(8,128)(2,1)S(1)}, bf16[256,1024]{1,0:T(8,128)(2,1)S(1)}, u32[]{:S(2)}, u32[]{:S(2)}) collective-permute-start(bf16[256,1024]{1,0:T(8,128)(2,1)S(1)} %get-tuple-element.239), channel_id=1, source_target_pairs={{0,2},{1,3},{2,0},{3,1},{4,6},{5,7},{6,4},{7,5},{8,10},{9,11},{10,... | collective-permute-start | bytes 1572872 | tf_op jit(solution)/shard_map/ppermute | solution.py:70
  237.9 16.2 %collective-permute-start.28 = (bf16[256,1024]{1,0:T(8,128)(2,1)}, bf16[256,1024]{1,0:T(8,128)(2,1)}, u32[]{:S(2)}, u32[]{:S(2)}) collective-permute-start(bf16[256,1024]{1,0:T(8,128)(2,1)} %get-tuple-element.241), channel_id=1, source_target_pairs={{0,1},{1,0},{2,3},{3,2},{4,5},{5,4},{6,7},{7,6},{8,9},{9,8},{10,11... | collective-permute-start | bytes 1572872 | tf_op jit(solution)/shard_map/ppermute | solution.py:70
  251.5 15.1 %collective-permute-start.31 = (bf16[256,1024]{1,0:T(8,128)(2,1)}, bf16[256,1024]{1,0:T(8,128)(2,1)}, u32[]{:S(2)}, u32[]{:S(2)}) collective-permute-start(bf16[256,1024]{1,0:T(8,128)(2,1)} %get-tuple-element.135), channel_id=1, source_target_pairs={{0,2},{1,3},{2,0},{3,1},{4,6},{5,7},{6,4},{7,5},{8,10},{9,11},{10,... | collective-permute-start | bytes 1572872 | tf_op jit(solution)/shard_map/ppermute | solution.py:70
  253.3 18.3 %collective-permute-start.27 = (f32[256,1024]{1,0:T(8,128)}, f32[256,1024]{1,0:T(8,128)S(1)}, u32[]{:S(2)}, u32[]{:S(2)}) collective-permute-start(f32[256,1024]{1,0:T(8,128)} %get-tuple-element.127), channel_id=1, source_target_pairs={{0,4},{4,0},{1,5},{5,1},{2,6},{6,2},{3,7},{7,3},{8,12},{12,8},{9,1... | collective-permute-start | bytes 3145736 | tf_op jit(solution)/shard_map/ppermute | solution.py:70
  253.4 27.5 %collective-permute-start.33 = (bf16[256,1024]{1,0:T(8,128)(2,1)}, bf16[256,1024]{1,0:T(8,128)(2,1)}, u32[]{:S(2)}, u32[]{:S(2)}) collective-permute-start(bf16[256,1024]{1,0:T(8,128)(2,1)} %get-tuple-element.238), channel_id=1, source_target_pairs={{0,2},{1,3},{2,0},{3,1},{4,6},{5,7},{6,4},{7,5},{8,10},{9,11},{10,... | collective-permute-start | bytes 1572872 | tf_op jit(solution)/shard_map/ppermute | solution.py:70
  254.1 23.8 %collective-permute-start.36 = (bf16[256,1024]{1,0:T(8,128)(2,1)}, bf16[256,1024]{1,0:T(8,128)(2,1)}, u32[]{:S(2)}, u32[]{:S(2)}) collective-permute-start(bf16[256,1024]{1,0:T(8,128)(2,1)} %get-tuple-element.154), channel_id=1, source_target_pairs={{0,1},{1,0},{2,3},{3,2},{4,5},{5,4},{6,7},{7,6},{8,9},{9,8},{10,11... | collective-permute-start | bytes 1572872 | tf_op jit(solution)/shard_map/ppermute | solution.py:70
  270.0 12.1 %collective-permute-start.32 = (bf16[256,1024]{1,0:T(8,128)(2,1)}, bf16[256,1024]{1,0:T(8,128)(2,1)}, u32[]{:S(2)}, u32[]{:S(2)}) collective-permute-start(bf16[256,1024]{1,0:T(8,128)(2,1)} %get-tuple-element.233), channel_id=1, source_target_pairs={{0,1},{1,0},{2,3},{3,2},{4,5},{5,4},{6,7},{7,6},{8,9},{9,8},{10,11... | collective-permute-start | bytes 1572872 | tf_op jit(solution)/shard_map/ppermute | solution.py:70
  277.2 28.1 %collective-permute-start.50 = (bf16[256,1024]{1,0:T(8,128)(2,1)}, bf16[256,1024]{1,0:T(8,128)(2,1)S(1)}, u32[]{:S(2)}, u32[]{:S(2)}) collective-permute-start(bf16[256,1024]{1,0:T(8,128)(2,1)} %get-tuple-element.169), channel_id=1, source_target_pairs={{0,2},{1,3},{2,0},{3,1},{4,6},{5,7},{6,4},{7,5},{8,10},{9,11},{10,... | collective-permute-start | bytes 1572872 | tf_op jit(solution)/shard_map/ppermute | solution.py:70
  277.9 27.4 %collective-permute-start.37 = (bf16[256,1024]{1,0:T(8,128)(2,1)}, bf16[256,1024]{1,0:T(8,128)(2,1)}, u32[]{:S(2)}, u32[]{:S(2)}) collective-permute-start(bf16[256,1024]{1,0:T(8,128)(2,1)} %get-tuple-element.155), channel_id=1, source_target_pairs={{0,1},{1,0},{2,3},{3,2},{4,5},{5,4},{6,7},{7,6},{8,9},{9,8},{10,11... | collective-permute-start | bytes 1572872 | tf_op jit(solution)/shard_map/ppermute | solution.py:70
  280.9 26.5 %collective-permute-start.43 = (bf16[256,1024]{1,0:T(8,128)(2,1)}, bf16[256,1024]{1,0:T(8,128)(2,1)}, u32[]{:S(2)}, u32[]{:S(2)}) collective-permute-start(bf16[256,1024]{1,0:T(8,128)(2,1)} %get-tuple-element.161), channel_id=1, source_target_pairs={{0,2},{1,3},{2,0},{3,1},{4,6},{5,7},{6,4},{7,5},{8,10},{9,11},{10,... | collective-permute-start | bytes 1572872 | tf_op jit(solution)/shard_map/ppermute | solution.py:70
  282.1 25.3 %collective-permute-start.52 = (bf16[256,1024]{1,0:T(8,128)(2,1)}, bf16[256,1024]{1,0:T(8,128)(2,1)}, u32[]{:S(2)}, u32[]{:S(2)}) collective-permute-start(bf16[256,1024]{1,0:T(8,128)(2,1)} %get-tuple-element.171), channel_id=1, source_target_pairs={{0,1},{1,0},{2,3},{3,2},{4,5},{5,4},{6,7},{7,6},{8,9},{9,8},{10,11... | collective-permute-start | bytes 1572872 | tf_op jit(solution)/shard_map/ppermute | solution.py:70
  285.2 22.2 %collective-permute-start.34 = (bf16[256,1024]{1,0:T(8,128)(2,1)S(1)}, bf16[256,1024]{1,0:T(8,128)(2,1)}, u32[]{:S(2)}, u32[]{:S(2)}) collective-permute-start(bf16[256,1024]{1,0:T(8,128)(2,1)S(1)} %add_convert_fusion.5), channel_id=1, source_target_pairs={{0,8},{8,16},{16,24},{24,0},{1,9},{9,17},{17,25},{25,1},{2,10},{10... | collective-permute-start | bytes 1572872 | tf_op jit(solution)/shard_map/ppermute | solution.py:80
  305.3 12.4 %collective-permute-start.51 = (bf16[256,512]{1,0:T(8,128)(2,1)}, bf16[256,512]{1,0:T(8,128)(2,1)}, u32[]{:S(2)}, u32[]{:S(2)}) collective-permute-start(bf16[256,512]{1,0:T(8,128)(2,1)} %get-tuple-element.170), channel_id=1, source_target_pairs={{0,2},{1,3},{2,0},{3,1},{4,6},{5,7},{6,4},{7,5},{8,10},{9,11},{10,... | collective-permute-start | bytes 786440 | tf_op jit(solution)/shard_map/ppermute | solution.py:70
  306.0 13.1 %collective-permute-start.38 = (bf16[256,512]{1,0:T(8,128)(2,1)}, bf16[256,512]{1,0:T(8,128)(2,1)S(1)}, u32[]{:S(2)}, u32[]{:S(2)}) collective-permute-start(bf16[256,512]{1,0:T(8,128)(2,1)} %get-tuple-element.156), channel_id=1, source_target_pairs={{0,1},{1,0},{2,3},{3,2},{4,5},{5,4},{6,7},{7,6},{8,9},{9,8},{10,11... | collective-permute-start | bytes 786440 | tf_op jit(solution)/shard_map/ppermute | solution.py:70
  311.6 20.1 %collective-permute-start.44 = (bf16[256,1024]{1,0:T(8,128)(2,1)}, bf16[256,1024]{1,0:T(8,128)(2,1)S(1)}, u32[]{:S(2)}, u32[]{:S(2)}) collective-permute-start(bf16[256,1024]{1,0:T(8,128)(2,1)} %get-tuple-element.162), channel_id=1, source_target_pairs={{0,2},{1,3},{2,0},{3,1},{4,6},{5,7},{6,4},{7,5},{8,10},{9,11},{10,... | collective-permute-start | bytes 1572872 | tf_op jit(solution)/shard_map/ppermute | solution.py:70
  317.7 21.2 %collective-permute-start.59 = (bf16[256,512]{1,0:T(8,128)(2,1)}, bf16[256,512]{1,0:T(8,128)(2,1)S(1)}, u32[]{:S(2)}, u32[]{:S(2)}) collective-permute-start(bf16[256,512]{1,0:T(8,128)(2,1)} %get-tuple-element.180), channel_id=1, source_target_pairs={{0,2},{1,3},{2,0},{3,1},{4,6},{5,7},{6,4},{7,5},{8,10},{9,11},{10,... | collective-permute-start | bytes 786440 | tf_op jit(solution)/shard_map/ppermute | solution.py:70
  319.1 9.4 %collective-permute-start.39 = (bf16[256,512]{1,0:T(8,128)(2,1)S(1)}, bf16[256,512]{1,0:T(8,128)(2,1)}, u32[]{:S(2)}, u32[]{:S(2)}) collective-permute-start(bf16[256,512]{1,0:T(8,128)(2,1)S(1)} %copy-done.51), channel_id=1, source_target_pairs={{0,1},{1,0},{2,3},{3,2},{4,5},{5,4},{6,7},{7,6},{8,9},{9,8},{10,11... | collective-permute-start | bytes 786440 | tf_op jit(solution)/shard_map/ppermute | solution.py:70
  319.9 18.5 %collective-permute-start.53 = (bf16[256,1024]{1,0:T(8,128)(2,1)S(1)}, bf16[256,1024]{1,0:T(8,128)(2,1)S(1)}, u32[]{:S(2)}, u32[]{:S(2)}) collective-permute-start(bf16[256,1024]{1,0:T(8,128)(2,1)S(1)} %copy-done.25), channel_id=1, source_target_pairs={{0,1},{1,0},{2,3},{3,2},{4,5},{5,4},{6,7},{7,6},{8,9},{9,8},{10,11... | collective-permute-start | bytes 1572872 | tf_op jit(solution)/shard_map/ppermute | solution.py:70
  326.9 23.4 %collective-permute-start.35 = (f32[256,1024]{1,0:T(8,128)}, f32[256,1024]{1,0:T(8,128)S(1)}, u32[]{:S(2)}, u32[]{:S(2)}) collective-permute-start(f32[256,1024]{1,0:T(8,128)} %get-tuple-element.141), channel_id=1, source_target_pairs={{0,4},{4,0},{1,5},{5,1},{2,6},{6,2},{3,7},{7,3},{8,12},{12,8},{9,1... | collective-permute-start | bytes 3145736 | tf_op jit(solution)/shard_map/ppermute | solution.py:70
  328.5 16.7 %collective-permute-start.55 = (bf16[256,1024]{1,0:T(8,128)(2,1)S(1)}, bf16[256,1024]{1,0:T(8,128)(2,1)S(1)}, u32[]{:S(2)}, u32[]{:S(2)}) collective-permute-start(bf16[256,1024]{1,0:T(8,128)(2,1)S(1)} %copy-done.24), channel_id=1, source_target_pairs={{0,24},{8,0},{16,8},{24,16},{1,25},{9,1},{17,9},{25,17},{2,26},{10... | collective-permute-start | bytes 1572872 | tf_op jit(solution)/shard_map/ppermute | solution.py:80
  331.8 12.3 %collective-permute-start.68 = (bf16[256,512]{1,0:T(8,128)(2,1)S(1)}, bf16[256,512]{1,0:T(8,128)(2,1)S(1)}, u32[]{:S(2)}, u32[]{:S(2)}) collective-permute-start(bf16[256,512]{1,0:T(8,128)(2,1)S(1)} %copy-done.52), channel_id=1, source_target_pairs={{0,1},{1,0},{2,3},{3,2},{4,5},{5,4},{6,7},{7,6},{8,9},{9,8},{10,11... | collective-permute-start | bytes 786440 | tf_op jit(solution)/shard_map/ppermute | solution.py:70
  338.9 9.8 %collective-permute-start.45 = (bf16[256,512]{1,0:T(8,128)(2,1)S(1)}, bf16[256,512]{1,0:T(8,128)(2,1)S(1)}, u32[]{:S(2)}, u32[]{:S(2)}) collective-permute-start(bf16[256,512]{1,0:T(8,128)(2,1)S(1)} %copy-done.50), channel_id=1, source_target_pairs={{0,2},{1,3},{2,0},{3,1},{4,6},{5,7},{6,4},{7,5},{8,10},{9,11},{10,... | collective-permute-start | bytes 786440 | tf_op jit(solution)/shard_map/ppermute | solution.py:70
  344.0 42.6 %collective-permute-start.60 = (bf16[256,512]{1,0:T(8,128)(2,1)}, bf16[256,512]{1,0:T(8,128)(2,1)}, u32[]{:S(2)}, u32[]{:S(2)}) collective-permute-start(bf16[256,512]{1,0:T(8,128)(2,1)} %get-tuple-element.181), channel_id=1, source_target_pairs={{0,2},{1,3},{2,0},{3,1},{4,6},{5,7},{6,4},{7,5},{8,10},{9,11},{10,... | collective-permute-start | bytes 786440 | tf_op jit(solution)/shard_map/ppermute | solution.py:70
  345.2 13.8 %collective-permute-start.56 = (bf16[256,1024]{1,0:T(8,128)(2,1)}, bf16[256,1024]{1,0:T(8,128)(2,1)}, u32[]{:S(2)}, u32[]{:S(2)}) collective-permute-start(bf16[256,1024]{1,0:T(8,128)(2,1)} %get-tuple-element.175), channel_id=1, source_target_pairs={{0,8},{8,16},{16,24},{24,0},{1,9},{9,17},{17,25},{25,1},{2,10},{10... | collective-permute-start | bytes 1572872 | tf_op jit(solution)/shard_map/ppermute | solution.py:80
  347.5 10.3 %collective-permute-start.64 = (bf16[256,512]{1,0:T(8,128)(2,1)}, bf16[256,512]{1,0:T(8,128)(2,1)}, u32[]{:S(2)}, u32[]{:S(2)}) collective-permute-start(bf16[256,512]{1,0:T(8,128)(2,1)} %add_convert_fusion.10), channel_id=1, source_target_pairs={{0,1},{1,0},{2,3},{3,2},{4,5},{5,4},{6,7},{7,6},{8,9},{9,8},{10,11... | collective-permute-start | bytes 786440 | tf_op jit(solution)/shard_map/ppermute | solution.py:70
  348.7 13.7 %collective-permute-start.46 = (bf16[256,512]{1,0:T(8,128)(2,1)}, bf16[256,512]{1,0:T(8,128)(2,1)}, u32[]{:S(2)}, u32[]{:S(2)}) collective-permute-start(bf16[256,512]{1,0:T(8,128)(2,1)} %add_convert_fusion.13), channel_id=1, source_target_pairs={{0,2},{1,3},{2,0},{3,1},{4,6},{5,7},{6,4},{7,5},{8,10},{9,11},{10,... | collective-permute-start | bytes 786440 | tf_op jit(solution)/shard_map/ppermute | solution.py:70
  359.0 19.0 %collective-permute-start.57 = (bf16[256,512]{1,0:T(8,128)(2,1)}, bf16[256,512]{1,0:T(8,128)(2,1)}, u32[]{:S(2)}, u32[]{:S(2)}) collective-permute-start(bf16[256,512]{1,0:T(8,128)(2,1)} %add_convert_fusion.11), channel_id=1, source_target_pairs={{0,8},{8,16},{16,24},{24,0},{1,9},{9,17},{17,25},{25,1},{2,10},{10... | collective-permute-start | bytes 786440 | tf_op jit(solution)/shard_map/ppermute | solution.py:80
  375.2 9.7 %collective-permute-start.49 = (f32[117,256]{1,0:T(8,128)S(1)}, f32[117,256]{1,0:T(8,128)S(1)}, u32[]{:S(2)}, u32[]{:S(2)}) collective-permute-start(f32[117,256]{1,0:T(8,128)S(1)} %get-tuple-element.288), channel_id=1, source_target_pairs={{0,24},{8,0},{16,8},{24,16},{1,25},{9,1},{17,9},{25,17},{2,26},{10... | collective-permute-start | bytes 359432 | tf_op jit(solution)/shard_map/ppermute | solution.py:80
  377.9 40.1 %collective-permute-start.74 = (bf16[256,512]{1,0:T(8,128)(2,1)}, bf16[256,512]{1,0:T(8,128)(2,1)}, u32[]{:S(2)}, u32[]{:S(2)}) collective-permute-start(bf16[256,512]{1,0:T(8,128)(2,1)} %get-tuple-element.193), channel_id=1, source_target_pairs={{0,1},{1,0},{2,3},{3,2},{4,5},{5,4},{6,7},{7,6},{8,9},{9,8},{10,11... | collective-permute-start | bytes 786440 | tf_op jit(solution)/shard_map/ppermute | solution.py:70
  379.1 38.9 %collective-permute-start.75 = (bf16[256,512]{1,0:T(8,128)(2,1)}, bf16[256,512]{1,0:T(8,128)(2,1)}, u32[]{:S(2)}, u32[]{:S(2)}) collective-permute-start(bf16[256,512]{1,0:T(8,128)(2,1)} %add_convert_fusion.8), channel_id=1, source_target_pairs={{0,2},{1,3},{2,0},{3,1},{4,6},{5,7},{6,4},{7,5},{8,10},{9,11},{10,... | collective-permute-start | bytes 786440 | tf_op jit(solution)/shard_map/ppermute | solution.py:70
  405.9 12.2 %collective-permute-start.76 = (bf16[256,512]{1,0:T(8,128)(2,1)}, bf16[256,512]{1,0:T(8,128)(2,1)S(1)}, u32[]{:S(2)}, u32[]{:S(2)}) collective-permute-start(bf16[256,512]{1,0:T(8,128)(2,1)} %add_convert_fusion.7), channel_id=1, source_target_pairs={{0,8},{8,16},{16,24},{24,0},{1,9},{9,17},{17,25},{25,1},{2,10},{10... | collective-permute-start | bytes 786440 | tf_op jit(solution)/shard_map/ppermute | solution.py:80
  (114 other events, 841.8 us)
Sparse Core Ops, SparseCore 0:
  13.6 158.1 all-gather.1

commit v4 on v3

--- a/solution.py
+++ b/solution.py
@@ -14,8 +14,8 @@
 TIMESTEPS = 1000
 ADAM_STEP = 10
 PATCH_ROWS = 16
-PINS = (None, 1, 3, 4, 7)
-CHAIN = (20, 1)
+PINS = (None, 1, 3, 4, 6)
+CHAIN = (18, 1)
 
 PRECISE = lax.Precision.HIGHEST
 BF = jnp.bfloat16
@@ -445,7 +445,7 @@
         cols = slice(k * block, (k + 1) * block)
         weight = jnp.concatenate([p[cols, :] for p in parts[0]], axis=1)
         own_ref[:, cols] = mm_nt(left_ref[:rows], weight)
-        other_ref[:, cols] = mm_nt(left_ref[rows:], weight)
+        other_ref[:, cols] = mm_nt(left_ref[rows:], weight).astype(BF)
 
 
 def gelu_slope(values):
@@ -875,7 +875,7 @@
     core_width = nt * half
     matrix_flops = 4 * own_count * width * half
 
-    two_sums = [shape(own_count, width, F32)] * 2
+    two_sums = [shape(own_count, width, F32), shape(own_count, width, BF)]
 
     def run(body, outs, blocks, *args):
         return call(body, outs, args, blocks * nt * matrix_flops)

time: 475 us -> 471 us (level)
  other arithmetic: 42.6 us -> 48.5 us
  waiting for transfers between devices: 178 us -> 173 us
    ppermute x65, waiting for transfers between devices: 70.6 us -> 55.8 us  [swap(): return lax.ppermute(value, axis, [(i, i ^ mask) for i in range(count)])]
    ppermute x15, waiting for transfers between devices: 14.5 us -> 24.6 us  [push(): lax.ppermute(value, 'fsdp', [(i, (i + k) % count) for i in range(count)])]
    convert_element_type x9 -> x8, other arithmetic: 15.3 us -> 17.6 us  [add_low(): return add(left, right).astype(BF)]
    unnamed x163 -> x149, local copies, waits for them, and re-layouts: 13 us -> 12 us
  transfers between devices with their start and end apart: 87 -> 87, of which waited for: 45 -> 42; matrix products, arithmetic and copies ran while one was open for 11% -> 13% of each run, Pallas kernels for 9% -> 9%
where the time goes in v4:
time: 471 us; the launch traced here: 466 us
  waiting for transfers between devices  173 us (37%)
  Pallas kernels  95.6 us (20%)
  starting transfers between devices  89.3 us (19%)
  other arithmetic  48.5 us (10%)
  local copies, waits for them, and re-layouts  29.3 us (6%)
  between operations  22.5 us (5%)
  matrix products  8.23 us (2%)
    all_gather x1, waiting for transfers between devices, on_device(): full = lax.all_gather(shards, ('tp', 'fsdp'), axis=0, tiled=True)  89.1 us
    pallas_call x12, Pallas kernels, call(): pl.pallas_call(kernel, grid=(1,), out_shape=outs, in_specs=specs, out_spe...  62.6 us
    ppermute x65, waiting for transfers between devices, swap(): return lax.ppermute(value, axis, [(i, i ^ mask) for i in range(count)])  55.8 us
    ppermute x65, starting transfers between devices, swap(): return lax.ppermute(value, axis, [(i, i ^ mask) for i in range(count)])  54.6 us
    pallas_call x2, Pallas kernels, over_hidden(): pl.pallas_call(kernel, grid=(counts,), out_shape=[o[0] for o in outs], in...  27.7 us
    ppermute x15, waiting for transfers between devices, push(): lax.ppermute(value, 'fsdp', [(i, (i + k) % count) for i in range(count)])  24.6 us
    ppermute x15, starting transfers between devices, push(): lax.ppermute(value, 'fsdp', [(i, (i + k) % count) for i in range(count)])  23.5 us
    convert_element_type x8, other arithmetic, add_low(): return add(left, right).astype(BF)  17.6 us
  transfers between devices with their start and end apart: 87, of which 42 were waited for; matrix products, arithmetic and copies ran while one was open for 13% of the time, Pallas kernels for 9%

profile of v4, /device:TPU:0, one launch (start us, length us, event | category | flops | bytes accessed | tf_op | source)
XLA Modules:
  0.0 466.1 jit_solution(14309879288731488353)
XLA Ops:
  13.7 3.0 collective-permute-start.2
  28.7 4.2 collective-permute-done.5
  38.6 3.3 collective-permute-start.10
  43.6 4.1 collective-permute-done.9
  56.8 2.8 collective-permute-start.17
  63.0 3.7 collective-permute-done.16
  82.7 89.1 %all-gather.2.cloned.1.call-done.refs_2_.refs_1_.up_ref.down_ref = bf16[4096,1536]{1,0:T(8,128)(2,1)} async-done(((bf16[256,1536]{1,0:T(8,128)(2,1)}), bf16[4096,1536]{1,0:T(8,128)(2,1)}) %all-gather.2.cloned.1.call-update) | async-done | bytes 12582928 | tf_op jit(solution)/shard_map/all_gather | solution.py:786
  171.8 7.3 %shard_map.374 = (bf16[512,1536]{1,0:T(8,128)(2,1)}, bf16[512,512]{1,0:T(8,128)(2,1)}) custom-call(bf16[256,1024]{1,0:T(8,128)(2,1)} %get-tuple-element.114.refs_0_, bf16[256,1024]{1,0:T(8,128)(2,1)} %copy-done.8, bf16[4096,1536]{1,0:T(8,128)(2,1)} %all-gather.2.cloned.1.call-done.refs_2_.refs_1_.up_ref.down_ref, f32[1,1536]{1,0:T(1,128)} %broadcast_in_dim_reshape.7.refs_3_), custom_call_target="tpu_custom_call" | custom-call | flops 2147483648 | bytes 6297600 | tf_op jit(solution)/shard_map/pallas_call | solution.py:334
  179.1 3.3 shard_map.375
  185.3 3.4 shard_map.376
  191.7 10.9 %shard_map.377 = (f32[512,2048]{1,0:T(8,128)}, bf16[512,2048]{1,0:T(8,128)(2,1)}, f32[256,1024]{1,0:T(8,128)}, f32[256,1024]{1,0:T(8,128)}) custom-call(bf16[256,1024]{1,0:T(8,128)(2,1)} %get-tuple-element.119.own_ref.own_in, bf16[256,1024]{1,0:T(8,128)(2,1)} %copy-done.10, bf16[4096,1536]{1,0:T(8,128)(2,1)} %all-gather.2.cloned.1.call-done.refs_2_.refs_1_.up_ref.down_ref, ...), custom_call_target="tpu_custom_call" | custom-call | flops 4294967296 | bytes 33554432 | tf_op jit(solution)/shard_map/pallas_call | solution.py:518
  206.5 4.5 shard_map.378
  214.0 16.8 %shard_map.379 = (bf16[4096,1024]{1,0:T(8,128)(2,1)}, f32[1,2048]{1,0:T(1,128)}, f32[256,1024]{1,0:T(8,128)}, f32[256,1024]{1,0:T(8,128)}) custom-call(bf16[256,1024]{1,0:T(8,128)(2,1)} %get-tuple-element.123.own_ref, bf16[256,1024]{1,0:T(8,128)(2,1)} %copy-done.15, bf16[256,1024]{1,0:T(8,128)(2,1)} %get-tuple-element.119.own_ref.own_in, ...), custom_call_target="tpu_custom_call" | custom-call | flops 8589934592 | bytes 33554432 | tf_op jit(solution)/shard_map/pallas_call | solution.py:518
  230.9 4.2 constant_dynamic-slice_fusion
  239.0 10.4 %collective-permute-done.28 = bf16[256,1024]{1,0:T(8,128)(2,1)} collective-permute-done((bf16[256,1024]{1,0:T(8,128)(2,1)}, bf16[256,1024]{1,0:T(8,128)(2,1)}, u32[]{:S(2)}, u32[]{:S(2)}) %collective-permute-start.28) | collective-permute-done | bytes 524320 | tf_op jit(solution)/shard_map/ppermute | solution.py:70
  252.2 2.9 add_convert_fusion.5
  255.1 7.6 %collective-permute-done.32 = bf16[256,1024]{1,0:T(8,128)(2,1)S(1)} collective-permute-done((bf16[256,1024]{1,0:T(8,128)(2,1)}, bf16[256,1024]{1,0:T(8,128)(2,1)S(1)}, u32[]{:S(2)}, u32[]{:S(2)}) %collective-permute-start.32) | collective-permute-done | bytes 524320 | tf_op jit(solution)/shard_map/ppermute | solution.py:70
  265.8 4.7 %shard_map.380 = (f32[256,1024]{1,0:T(8,128)}, bf16[256,1024]{1,0:T(8,128)(2,1)}, f32[1,4,1024]{2,1,0:T(4,128)}) custom-call(f32[256,1024]{1,0:T(8,128)} %get-tuple-element.126.refs_0_, f32[256,1024]{1,0:T(8,128)} %copy-done.12, f32[256,1024]{1,0:T(8,128)} %get-tuple-element.122.refs_3_.refs_2_, f32[1,6,1024]{2,1,0:T(8,128)} %add_bitcast_fusion.refs_3_.refs_4_, ...), custom_call_target="tpu_custom_call" | custom-call | bytes 6856704 | tf_op jit(solution)/shard_map/pallas_call | solution.py:334
  276.3 13.5 %shard_map.381 = (bf16[512,1536]{1,0:T(8,128)(2,1)}, f32[1,1536]{1,0:T(1,128)}) custom-call(bf16[256,1024]{1,0:T(8,128)(2,1)} %get-tuple-element.132.refs_0_.refs_2_, bf16[256,1024]{1,0:T(8,128)(2,1)} %copy-done.9, bf16[4096,1536]{1,0:T(8,128)(2,1)} %all-gather.2.cloned.1.call-done.refs_2_.refs_1_.up_ref.down_ref, bf16[512,1536]{1,0:T(8,128)(2,1)} %get-tuple-element.133.refs_3_), custom_call_target="tpu_custom_call" | custom-call | flops 1073741824 | bytes 5249024 | tf_op jit(solution)/shard_map/pallas_call | solution.py:334
  290.5 4.6 add_convert_fusion
  297.2 5.3 %shard_map.385 = (bf16[256,512]{1,0:T(8,128)(2,1)}, bf16[256,512]{1,0:T(8,128)(2,1)}, bf16[256,512]{1,0:T(8,128)(2,1)}, bf16[256,512]{1,0:T(8,128)(2,1)}, bf16[2...) custom-call(bf16[256,1024]{1,0:T(8,128)(2,1)} %get-tuple-element.114.refs_0_, ...), custom_call_target="tpu_custom_call" | custom-call | flops 1073741824 | bytes 6291456 | tf_op jit(solution)/shard_map/pallas_call | solution.py:334
  302.4 5.5 %shard_map.382 = (bf16[256,512]{1,0:T(8,128)(2,1)}, bf16[256,512]{1,0:T(8,128)(2,1)}, bf16[256,512]{1,0:T(8,128)(2,1)}, bf16[256,512]{1,0:T(8,128)(2,1)}, bf16[2...) custom-call(bf16[256,1024]{1,0:T(8,128)(2,1)} %get-tuple-element.114.refs_0_, ...), custom_call_target="tpu_custom_call" | custom-call | flops 1073741824 | bytes 6291456 | tf_op jit(solution)/shard_map/pallas_call | solution.py:334
  310.0 5.3 %shard_map.383 = (f32[256,1024]{1,0:T(8,128)}, bf16[256,1024]{1,0:T(8,128)(2,1)}) custom-call(bf16[512,1536]{1,0:T(8,128)(2,1)} %get-tuple-element.152.refs_4_.refs_0_, bf16[4096,1536]{1,0:T(8,128)(2,1)} %all-gather.2.cloned.1.call-done.refs_2_.refs_1_.up_ref.down_ref), custom_call_target="tpu_custom_call" | custom-call | flops 1610612736 | bytes 6291456 | tf_op jit(solution)/shard_map/pallas_call | solution.py:334
  323.2 3.8 collective-permute-start.60
  330.0 3.6 shard_map.384
  334.8 2.7 add_convert_fusion.1
  357.8 3.7 collective-permute-done.42
  375.9 5.8 %collective-permute-done.62 = bf16[256,512]{1,0:T(8,128)(2,1)} collective-permute-done((bf16[256,512]{1,0:T(8,128)(2,1)}, bf16[256,512]{1,0:T(8,128)(2,1)}, u32[]{:S(2)}, u32[]{:S(2)}) %collective-permute-start.62) | collective-permute-done | bytes 262176 | tf_op jit(solution)/shard_map/ppermute | solution.py:80
  395.8 2.8 collective-permute-start.63
  411.1 5.3 %collective-permute-done.76 = bf16[256,512]{1,0:T(8,128)(2,1)S(1)} collective-permute-done((bf16[256,512]{1,0:T(8,128)(2,1)S(1)}, bf16[256,512]{1,0:T(8,128)(2,1)S(1)}, u32[]{:S(2)}, u32[]{:S(2)}) %collective-permute-start.76) | collective-permute-done | bytes 262176 | tf_op jit(solution)/shard_map/ppermute | solution.py:80
  421.2 3.4 shard_map.386
  454.4 3.3 shard_map.387
  (571 shorter events, 188.3 us)
Async XLA Ops:
  7.2 164.6 %all-gather.2.cloned.1.call-start = ((), (), s32[]{:S(2)}) async-start(), calls=%async_computation | async-start | bytes 13369344 | tf_op jit(solution)/shard_map/all_gather | solution.py:786
  59.9 9.4 %collective-permute-start.15 = (f32[4,2304]{1,0:T(4,128)S(1)}, f32[4,2304]{1,0:T(4,128)S(1)}, u32[]{:S(2)}, u32[]{:S(2)}) collective-permute-start(f32[4,2304]{1,0:T(4,128)S(1)} %get-tuple-element.274), channel_id=1, source_target_pairs={{0,16},{8,24},{16,0},{24,8},{1,17},{9,25},{17,1},{25,9},{2,18},{10... | collective-permute-start | bytes 110600 | tf_op jit(solution)/shard_map/ppermute | solution.py:80
  235.1 14.3 %collective-permute-start.28 = (bf16[256,1024]{1,0:T(8,128)(2,1)}, bf16[256,1024]{1,0:T(8,128)(2,1)}, u32[]{:S(2)}, u32[]{:S(2)}) collective-permute-start(bf16[256,1024]{1,0:T(8,128)(2,1)} %get-tuple-element.239), channel_id=1, source_target_pairs={{0,1},{1,0},{2,3},{3,2},{4,5},{5,4},{6,7},{7,6},{8,9},{9,8},{10,11... | collective-permute-start | bytes 1572872 | tf_op jit(solution)/shard_map/ppermute | solution.py:70
  236.5 28.2 %collective-permute-start.27 = (f32[256,1024]{1,0:T(8,128)}, f32[256,1024]{1,0:T(8,128)S(1)}, u32[]{:S(2)}, u32[]{:S(2)}) collective-permute-start(f32[256,1024]{1,0:T(8,128)} %get-tuple-element.127), channel_id=1, source_target_pairs={{0,4},{4,0},{1,5},{5,1},{2,6},{6,2},{3,7},{7,3},{8,12},{12,8},{9,1... | collective-permute-start | bytes 3145736 | tf_op jit(solution)/shard_map/ppermute | solution.py:70
  236.5 15.0 %collective-permute-start.30 = (bf16[256,1024]{1,0:T(8,128)(2,1)}, bf16[256,1024]{1,0:T(8,128)(2,1)}, u32[]{:S(2)}, u32[]{:S(2)}) collective-permute-start(bf16[256,1024]{1,0:T(8,128)(2,1)} %get-tuple-element.237), channel_id=1, source_target_pairs={{0,2},{1,3},{2,0},{3,1},{4,6},{5,7},{6,4},{7,5},{8,10},{9,11},{10,... | collective-permute-start | bytes 1572872 | tf_op jit(solution)/shard_map/ppermute | solution.py:70
  237.5 25.3 %collective-permute-start.32 = (bf16[256,1024]{1,0:T(8,128)(2,1)}, bf16[256,1024]{1,0:T(8,128)(2,1)S(1)}, u32[]{:S(2)}, u32[]{:S(2)}) collective-permute-start(bf16[256,1024]{1,0:T(8,128)(2,1)} %get-tuple-element.236), channel_id=1, source_target_pairs={{0,2},{1,3},{2,0},{3,1},{4,6},{5,7},{6,4},{7,5},{8,10},{9,11},{10,... | collective-permute-start | bytes 1572872 | tf_op jit(solution)/shard_map/ppermute | solution.py:70
  249.4 21.1 %collective-permute-start.48 = (bf16[256,1024]{1,0:T(8,128)(2,1)}, bf16[256,1024]{1,0:T(8,128)(2,1)}, u32[]{:S(2)}, u32[]{:S(2)}) collective-permute-start(bf16[256,1024]{1,0:T(8,128)(2,1)} %get-tuple-element.166), channel_id=1, source_target_pairs={{0,1},{1,0},{2,3},{3,2},{4,5},{5,4},{6,7},{7,6},{8,9},{9,8},{10,11... | collective-permute-start | bytes 1572872 | tf_op jit(solution)/shard_map/ppermute | solution.py:70
  251.6 22.5 %collective-permute-start.31 = (bf16[256,1024]{1,0:T(8,128)(2,1)}, bf16[256,1024]{1,0:T(8,128)(2,1)}, u32[]{:S(2)}, u32[]{:S(2)}) collective-permute-start(bf16[256,1024]{1,0:T(8,128)(2,1)} %get-tuple-element.135), channel_id=1, source_target_pairs={{0,2},{1,3},{2,0},{3,1},{4,6},{5,7},{6,4},{7,5},{8,10},{9,11},{10,... | collective-permute-start | bytes 1572872 | tf_op jit(solution)/shard_map/ppermute | solution.py:70
  262.7 27.8 %collective-permute-start.33 = (bf16[256,1024]{1,0:T(8,128)(2,1)}, bf16[256,1024]{1,0:T(8,128)(2,1)}, u32[]{:S(2)}, u32[]{:S(2)}) collective-permute-start(bf16[256,1024]{1,0:T(8,128)(2,1)} %get-tuple-element.139), channel_id=1, source_target_pairs={{0,2},{1,3},{2,0},{3,1},{4,6},{5,7},{6,4},{7,5},{8,10},{9,11},{10,... | collective-permute-start | bytes 1572872 | tf_op jit(solution)/shard_map/ppermute | solution.py:70
  263.3 27.2 %collective-permute-start.35 = (bf16[256,1024]{1,0:T(8,128)(2,1)}, bf16[256,1024]{1,0:T(8,128)(2,1)}, u32[]{:S(2)}, u32[]{:S(2)}) collective-permute-start(bf16[256,1024]{1,0:T(8,128)(2,1)} %get-tuple-element.240), channel_id=1, source_target_pairs={{0,1},{1,0},{2,3},{3,2},{4,5},{5,4},{6,7},{7,6},{8,9},{9,8},{10,11... | collective-permute-start | bytes 1572872 | tf_op jit(solution)/shard_map/ppermute | solution.py:70
  270.5 20.0 %collective-permute-start.49 = (bf16[256,1024]{1,0:T(8,128)(2,1)}, bf16[256,1024]{1,0:T(8,128)(2,1)}, u32[]{:S(2)}, u32[]{:S(2)}) collective-permute-start(bf16[256,1024]{1,0:T(8,128)(2,1)} %get-tuple-element.167), channel_id=1, source_target_pairs={{0,1},{1,0},{2,3},{3,2},{4,5},{5,4},{6,7},{7,6},{8,9},{9,8},{10,11... | collective-permute-start | bytes 1572872 | tf_op jit(solution)/shard_map/ppermute | solution.py:70
  274.1 28.4 %collective-permute-start.36 = (bf16[256,1024]{1,0:T(8,128)(2,1)}, bf16[256,1024]{1,0:T(8,128)(2,1)S(1)}, u32[]{:S(2)}, u32[]{:S(2)}) collective-permute-start(bf16[256,1024]{1,0:T(8,128)(2,1)} %get-tuple-element.155), channel_id=1, source_target_pairs={{0,2},{1,3},{2,0},{3,1},{4,6},{5,7},{6,4},{7,5},{8,10},{9,11},{10,... | collective-permute-start | bytes 1572872 | tf_op jit(solution)/shard_map/ppermute | solution.py:70
  295.1 22.5 %collective-permute-start.38 = (bf16[256,1024]{1,0:T(8,128)(2,1)}, bf16[256,1024]{1,0:T(8,128)(2,1)}, u32[]{:S(2)}, u32[]{:S(2)}) collective-permute-start(bf16[256,1024]{1,0:T(8,128)(2,1)} %get-tuple-element.157), channel_id=1, source_target_pairs={{0,1},{1,0},{2,3},{3,2},{4,5},{5,4},{6,7},{7,6},{8,9},{9,8},{10,11... | collective-permute-start | bytes 1572872 | tf_op jit(solution)/shard_map/ppermute | solution.py:70
  296.6 26.6 %collective-permute-start.53 = (bf16[256,1024]{1,0:T(8,128)(2,1)}, bf16[256,1024]{1,0:T(8,128)(2,1)S(1)}, u32[]{:S(2)}, u32[]{:S(2)}) collective-permute-start(bf16[256,1024]{1,0:T(8,128)(2,1)} %get-tuple-element.173), channel_id=1, source_target_pairs={{0,2},{1,3},{2,0},{3,1},{4,6},{5,7},{6,4},{7,5},{8,10},{9,11},{10,... | collective-permute-start | bytes 1572872 | tf_op jit(solution)/shard_map/ppermute | solution.py:70
  297.2 24.7 %collective-permute-start.59 = (bf16[256,1024]{1,0:T(8,128)(2,1)}, bf16[256,1024]{1,0:T(8,128)(2,1)}, u32[]{:S(2)}, u32[]{:S(2)}) collective-permute-start(bf16[256,1024]{1,0:T(8,128)(2,1)} %get-tuple-element.229), channel_id=1, source_target_pairs={{0,8},{8,16},{16,24},{24,0},{1,9},{9,17},{17,25},{25,1},{2,10},{10... | collective-permute-start | bytes 1572872 | tf_op jit(solution)/shard_map/ppermute | solution.py:80
  316.0 13.1 %collective-permute-start.34 = (bf16[256,1024]{1,0:T(8,128)(2,1)}, bf16[256,1024]{1,0:T(8,128)(2,1)S(1)}, u32[]{:S(2)}, u32[]{:S(2)}) collective-permute-start(bf16[256,1024]{1,0:T(8,128)(2,1)} %get-tuple-element.142), channel_id=1, source_target_pairs={{0,4},{4,0},{1,5},{5,1},{2,6},{6,2},{3,7},{7,3},{8,12},{12,8},{9,1... | collective-permute-start | bytes 1572872 | tf_op jit(solution)/shard_map/ppermute | solution.py:70
  316.1 11.0 %collective-permute-start.51 = (bf16[256,512]{1,0:T(8,128)(2,1)}, bf16[256,512]{1,0:T(8,128)(2,1)S(1)}, u32[]{:S(2)}, u32[]{:S(2)}) collective-permute-start(bf16[256,512]{1,0:T(8,128)(2,1)} %get-tuple-element.169), channel_id=1, source_target_pairs={{0,1},{1,0},{2,3},{3,2},{4,5},{5,4},{6,7},{7,6},{8,9},{9,8},{10,11... | collective-permute-start | bytes 786440 | tf_op jit(solution)/shard_map/ppermute | solution.py:70
  317.7 10.1 %collective-permute-start.44 = (bf16[256,512]{1,0:T(8,128)(2,1)}, bf16[256,512]{1,0:T(8,128)(2,1)S(1)}, u32[]{:S(2)}, u32[]{:S(2)}) collective-permute-start(bf16[256,512]{1,0:T(8,128)(2,1)} %get-tuple-element.162), channel_id=1, source_target_pairs={{0,2},{1,3},{2,0},{3,1},{4,6},{5,7},{6,4},{7,5},{8,10},{9,11},{10,... | collective-permute-start | bytes 786440 | tf_op jit(solution)/shard_map/ppermute | solution.py:70
  321.8 19.6 %collective-permute-start.39 = (bf16[256,1024]{1,0:T(8,128)(2,1)}, bf16[256,1024]{1,0:T(8,128)(2,1)S(1)}, u32[]{:S(2)}, u32[]{:S(2)}) collective-permute-start(bf16[256,1024]{1,0:T(8,128)(2,1)} %get-tuple-element.158), channel_id=1, source_target_pairs={{0,1},{1,0},{2,3},{3,2},{4,5},{5,4},{6,7},{7,6},{8,9},{9,8},{10,11... | collective-permute-start | bytes 1572872 | tf_op jit(solution)/shard_map/ppermute | solution.py:70
  323.2 20.6 %collective-permute-start.60 = (bf16[256,1024]{1,0:T(8,128)(2,1)}, bf16[256,1024]{1,0:T(8,128)(2,1)}, u32[]{:S(2)}, u32[]{:S(2)}) collective-permute-start(bf16[256,1024]{1,0:T(8,128)(2,1)} %get-tuple-element.178), channel_id=1, source_target_pairs={{0,24},{8,0},{16,8},{24,16},{1,25},{9,1},{17,9},{25,17},{2,26},{10... | collective-permute-start | bytes 1572872 | tf_op jit(solution)/shard_map/ppermute | solution.py:80
  327.1 11.7 %collective-permute-start.54 = (bf16[256,512]{1,0:T(8,128)(2,1)}, bf16[256,512]{1,0:T(8,128)(2,1)}, u32[]{:S(2)}, u32[]{:S(2)}) collective-permute-start(bf16[256,512]{1,0:T(8,128)(2,1)} %get-tuple-element.174), channel_id=1, source_target_pairs={{0,2},{1,3},{2,0},{3,1},{4,6},{5,7},{6,4},{7,5},{8,10},{9,11},{10,... | collective-permute-start | bytes 786440 | tf_op jit(solution)/shard_map/ppermute | solution.py:70
  327.8 14.4 %collective-permute-start.73 = (bf16[256,512]{1,0:T(8,128)(2,1)}, bf16[256,512]{1,0:T(8,128)(2,1)}, u32[]{:S(2)}, u32[]{:S(2)}) collective-permute-start(bf16[256,512]{1,0:T(8,128)(2,1)} %get-tuple-element.192), channel_id=1, source_target_pairs={{0,1},{1,0},{2,3},{3,2},{4,5},{5,4},{6,7},{7,6},{8,9},{9,8},{10,11... | collective-permute-start | bytes 786440 | tf_op jit(solution)/shard_map/ppermute | solution.py:70
  329.2 52.5 %collective-permute-start.66 = (bf16[256,512]{1,0:T(8,128)(2,1)}, bf16[256,512]{1,0:T(8,128)(2,1)}, u32[]{:S(2)}, u32[]{:S(2)}) collective-permute-start(bf16[256,512]{1,0:T(8,128)(2,1)} %get-tuple-element.183), channel_id=1, source_target_pairs={{0,2},{1,3},{2,0},{3,1},{4,6},{5,7},{6,4},{7,5},{8,10},{9,11},{10,... | collective-permute-start | bytes 786440 | tf_op jit(solution)/shard_map/ppermute | solution.py:70
  343.9 22.0 %collective-permute-start.61 = (bf16[256,1024]{1,0:T(8,128)(2,1)}, bf16[256,1024]{1,0:T(8,128)(2,1)}, u32[]{:S(2)}, u32[]{:S(2)}) collective-permute-start(bf16[256,1024]{1,0:T(8,128)(2,1)} %add_convert_fusion.1), channel_id=1, source_target_pairs={{0,8},{8,16},{16,24},{24,0},{1,9},{9,17},{17,25},{25,1},{2,10},{10... | collective-permute-start | bytes 1572872 | tf_op jit(solution)/shard_map/ppermute | solution.py:80
  350.5 11.0 %collective-permute-start.42 = (f32[45,1024]{1,0:T(8,128)S(1)}, f32[45,1024]{1,0:T(8,128)S(1)}, u32[]{:S(2)}, u32[]{:S(2)}) collective-permute-start(f32[45,1024]{1,0:T(8,128)S(1)} %concatenate.151), channel_id=1, source_target_pairs={{0,3},{1,2},{2,1},{3,0},{4,7},{5,6},{6,5},{7,4},{8,11},{9,10},{10,... | collective-permute-start | bytes 552968 | tf_op jit(solution)/shard_map/ppermute | solution.py:70
  355.9 15.3 %collective-permute-start.68 = (bf16[256,512]{1,0:T(8,128)(2,1)S(1)}, bf16[256,512]{1,0:T(8,128)(2,1)}, u32[]{:S(2)}, u32[]{:S(2)}) collective-permute-start(bf16[256,512]{1,0:T(8,128)(2,1)S(1)} %add_convert_fusion.10), channel_id=1, source_target_pairs={{0,1},{1,0},{2,3},{3,2},{4,5},{5,4},{6,7},{7,6},{8,9},{9,8},{10,11... | collective-permute-start | bytes 786440 | tf_op jit(solution)/shard_map/ppermute | solution.py:70
  362.0 9.3 %collective-permute-start.45 = (f32[117,256]{1,0:T(8,128)S(1)}, f32[117,256]{1,0:T(8,128)S(1)}, u32[]{:S(2)}, u32[]{:S(2)}) collective-permute-start(f32[117,256]{1,0:T(8,128)S(1)} %get-tuple-element.286), channel_id=1, source_target_pairs={{0,16},{8,24},{16,0},{24,8},{1,17},{9,25},{17,1},{25,9},{2,18},{10... | collective-permute-start | bytes 359432 | tf_op jit(solution)/shard_map/ppermute | solution.py:80
  364.4 8.8 %collective-permute-start.46 = (f32[117,256]{1,0:T(8,128)S(1)}, f32[117,256]{1,0:T(8,128)S(1)}, u32[]{:S(2)}, u32[]{:S(2)}) collective-permute-start(f32[117,256]{1,0:T(8,128)S(1)} %get-tuple-element.287), channel_id=1, source_target_pairs={{0,8},{8,16},{16,24},{24,0},{1,9},{9,17},{17,25},{25,1},{2,10},{10... | collective-permute-start | bytes 359432 | tf_op jit(solution)/shard_map/ppermute | solution.py:80
  371.2 39.9 %collective-permute-start.74 = (bf16[256,512]{1,0:T(8,128)(2,1)}, bf16[256,512]{1,0:T(8,128)(2,1)}, u32[]{:S(2)}, u32[]{:S(2)}) collective-permute-start(bf16[256,512]{1,0:T(8,128)(2,1)} %add_convert_fusion.9), channel_id=1, source_target_pairs={{0,2},{1,3},{2,0},{3,1},{4,6},{5,7},{6,4},{7,5},{8,10},{9,11},{10,... | collective-permute-start | bytes 786440 | tf_op jit(solution)/shard_map/ppermute | solution.py:70
  371.4 39.7 %collective-permute-start.72 = (bf16[256,512]{1,0:T(8,128)(2,1)}, bf16[256,512]{1,0:T(8,128)(2,1)}, u32[]{:S(2)}, u32[]{:S(2)}) collective-permute-start(bf16[256,512]{1,0:T(8,128)(2,1)} %get-tuple-element.189), channel_id=1, source_target_pairs={{0,1},{1,0},{2,3},{3,2},{4,5},{5,4},{6,7},{7,6},{8,9},{9,8},{10,11... | collective-permute-start | bytes 786440 | tf_op jit(solution)/shard_map/ppermute | solution.py:70
  407.2 9.1 %collective-permute-start.76 = (bf16[256,512]{1,0:T(8,128)(2,1)S(1)}, bf16[256,512]{1,0:T(8,128)(2,1)S(1)}, u32[]{:S(2)}, u32[]{:S(2)}) collective-permute-start(bf16[256,512]{1,0:T(8,128)(2,1)S(1)} %copy-done.26), channel_id=1, source_target_pairs={{0,8},{8,16},{16,24},{24,0},{1,9},{9,17},{17,25},{25,1},{2,10},{10... | collective-permute-start | bytes 786440 | tf_op jit(solution)/shard_map/ppermute | solution.py:80
  411.0 9.4 %collective-permute-start.78 = (f32[128,1024]{1,0:T(8,128)S(1)}, f32[128,1024]{1,0:T(8,128)S(1)}, u32[]{:S(2)}, u32[]{:S(2)}) collective-permute-start(f32[128,1024]{1,0:T(8,128)S(1)} %get-tuple-element.242), channel_id=1, source_target_pairs={{0,4},{4,0},{1,5},{5,1},{2,6},{6,2},{3,7},{7,3},{8,12},{12,8},{9,1... | collective-permute-start | bytes 1572872 | tf_op jit(solution)/shard_map/ppermute | solution.py:70
  (107 other events, 767.5 us)
Sparse Core Ops, SparseCore 0:
  13.6 158.1 all-gather.1
